TPU v7x, 32 devices: a whole 2x2x4 slice. The times are simulated.
32 devices in a mesh: frame: 4 (over y, core), row: 8 (over z, x).
Axes of the slice: x: 2, y: 2, z: 4, core: 2. Of those that a mesh axis runs over, the one named last changes fastest.
Arguments:
- queries: bfloat16 [4, 8, 128, 1120], P('frame', 'row'), may hold values from -6 to 6
- key_proj: bfloat16 [4, 8, 128, 1120], P('frame', 'row'), may hold values from -6 to 6
- value_proj: bfloat16 [4, 8, 128, 1120], P('frame', 'row'), may hold values from -6 to 6
- attn_grad: bfloat16 [4, 8, 128, 1120], P('frame', 'row'), may hold values from -6 to 6
- conv_grad: bfloat16 [4, 8, 128, 5632], P('frame', 'row'), may hold values from -6 to 6
- conv_weight: float32 [3, 3, 5632], replicated, may hold values from -2 to 2
Outputs:
- query_grad: bfloat16 [4, 8, 128, 1120], P('frame', 'row')
- key_grad: bfloat16 [4, 8, 128, 1120], P('frame', 'row')
- value_grad: bfloat16 [4, 8, 128, 1120], P('frame', 'row')
- input_grad: bfloat16 [4, 8, 128, 5632], P('frame', 'row')
All inputs are finite; a program needn't handle non-finite values.
Results may differ from a plain program's by a relative error of at most 0.001.
Values may be sent and summed in bfloat16 or wider, within the bound.
No kernel may reach another device: no remote copies, remote signals or barrier semaphores. Data moves between devices by JAX's collectives and lax.ppermute only.
A program may use at most 64 MiB of HBM per device.

v0:
```python
import math

import jax
import jax.numpy as jnp
from jax import lax
from jax.sharding import PartitionSpec as P

HEADS = 10
HD = 112


EPSILON = 1e-06
HIGH = lax.Precision.HIGHEST
LANES = 128


def padded(x, sides, width):
    for axis, dim in sides:
        size, length = (lax.axis_size(axis), x.shape[dim])
        up = [(i, (i + 1) % size) for i in range(size - 1)]
        down = [(j, i) for i, j in up]
        last = lax.slice_in_dim(x, length - width, length, axis=dim)
        first = lax.slice_in_dim(x, 0, width, axis=dim)
        before = lax.ppermute(last, axis, up)
        after = lax.ppermute(first, axis, down)
        x = jnp.concatenate([before, x, after], axis=dim)
    return x


def pack_sums(members, groups):
    flat = jnp.concatenate([member.reshape(-1) for member in members])
    unit = LANES * groups
    padded_len = (flat.shape[0] + unit - 1) // unit * unit
    flat = jnp.pad(flat, (0, padded_len - flat.shape[0]))
    return flat.reshape(padded_len // LANES, LANES)


def unpack_sums(packed, members):
    flat = packed.reshape(-1)
    result = []
    offset = 0
    for member in members:
        length = member.size
        result.append(flat[offset : offset + length].reshape(member.shape))
        offset = offset + length
    return tuple(result)


def shards(queries, key_proj, value_proj, attn_grad, conv_grad, conv_weight):
    frames_here, rows_here, cols_here, feat_width = queries.shape
    tok_count = frames_here * rows_here * cols_here
    tokens_all = tok_count * lax.axis_size("frame") * lax.axis_size("row")
    grad_scale = math.sqrt(tokens_all)
    band_count = lax.axis_size("row")
    key_feat = jnp.maximum(key_proj, 0).reshape(tok_count, HEADS, HD)
    value_rows = value_proj.reshape(tok_count, HEADS, HD)
    state_part = jnp.einsum(
        "nhd,nhe->hde", key_feat, value_rows, preferred_element_type=jnp.float32
    )
    norm_part = jnp.sum(key_feat, axis=0, dtype=jnp.float32)
    grad_rows = padded(conv_grad, (("row", 1),), 1)
    grad_pad = jnp.pad(grad_rows, ((0, 0), (0, 0), (1, 1), (0, 0)))
    input_acc = jnp.zeros(conv_grad.shape, jnp.float32)
    for tap_row in range(3):
        for tap_col in range(3):
            shifted = grad_pad[
                :, 2 - tap_row : 2 - tap_row + rows_here, 2 - tap_col : 2 - tap_col + cols_here
            ]
            input_acc = input_acc + conv_weight[tap_row, tap_col] * shifted
    input_grad = input_acc.astype(jnp.bfloat16)
    state_members = (state_part, norm_part)
    state_packed = pack_sums(state_members, band_count)
    state_share = lax.psum_scatter(state_packed, "row", scatter_dimension=0, tiled=True)
    state_share = lax.psum(state_share, "frame")
    state_whole = lax.all_gather(state_share, "row", axis=0, tiled=True)
    full_state, norm_sum = unpack_sums(state_whole, state_members)
    query_feat = jnp.maximum(queries, 0).reshape(tok_count, HEADS, HD).astype(jnp.float32)
    scaled = attn_grad.reshape(tok_count, HEADS, HD).astype(jnp.float32) * grad_scale
    denominator = jnp.einsum("nhd,hd->nh", query_feat, norm_sum, precision=HIGH) + EPSILON
    attn_out = (
        jnp.einsum("nhd,hde->nhe", query_feat, full_state, precision=HIGH) / denominator[..., None]
    )
    weighted = scaled / denominator[..., None]
    projected = jnp.sum(scaled * attn_out, axis=-1) / denominator
    state_term = jnp.einsum("nhd,nhe->hde", query_feat, weighted, precision=HIGH)
    norm_term = -jnp.einsum("nh,nhd->hd", projected, query_feat, precision=HIGH)
    grad_members = (state_term, norm_term)
    grad_packed = pack_sums(grad_members, band_count)
    grad_share = lax.psum_scatter(grad_packed, "row", scatter_dimension=0, tiled=True)
    grad_share = lax.psum(grad_share, "frame")
    grad_whole = lax.all_gather(grad_share, "row", axis=0, tiled=True)
    state_grad, norm_grad = unpack_sums(grad_whole, grad_members)
    query_part = (
        jnp.einsum("hde,nhe->nhd", full_state, weighted, precision=HIGH)
        - projected[..., None] * norm_sum
    )
    query_part = jnp.where(query_feat > 0, query_part, jnp.float32(0.0))
    key_part = (
        jnp.einsum("hde,nhe->nhd", state_grad, value_rows.astype(jnp.float32), precision=HIGH)
        + norm_grad
    )
    key_part = jnp.where(key_proj.reshape(tok_count, HEADS, HD) > 0, key_part, jnp.float32(0.0))
    value_part = jnp.einsum(
        "hde,nhd->nhe", state_grad, key_feat.astype(jnp.float32), precision=HIGH
    )
    query_grad = query_part.reshape(queries.shape).astype(jnp.bfloat16)
    key_grad = key_part.reshape(queries.shape).astype(jnp.bfloat16)
    value_grad = value_part.reshape(queries.shape).astype(jnp.bfloat16)
    return (query_grad, key_grad, value_grad, input_grad)


def solution(mesh):
    placed = (
        P("frame", "row", None, None),
        P("frame", "row", None, None),
        P("frame", "row", None, None),
        P("frame", "row", None, None),
        P("frame", "row", None, None),
        P(),
    )
    return jax.shard_map(
        shards,
        mesh=mesh,
        in_specs=placed,
        out_specs=(
            P("frame", "row", None, None),
            P("frame", "row", None, None),
            P("frame", "row", None, None),
            P("frame", "row", None, None),
        ),
        check_vma=False,
    )
```

profile of v0, /device:TPU:0, one launch (start us, length us, event | category | flops | bytes accessed | tf_op | source)
XLA Modules:
  0.0 241.5 jit_solution(16456573723586706052)
XLA Ops:
  0.6 0.0 copy-start
  0.6 0.0 copy-start.3
  0.7 1.4 collective-permute-start.1
  2.1 6.6 %collective-permute-start = (bf16[1,1,128,5632]{3,2,1,0:T(8,128)(2,1)}, bf16[1,1,128,5632]{3,2,1,0:T(8,128)(2,1)}, u32[]{:S(2)}, u32[]{:S(2)}) collective-permute-start(bf16[1,1,128,5632]{3,2,1,0:T(8,128)(2,1)} %param.10), channel_id=1, source_target_pairs={{0,1},{1,2},{2,3},{3,4},{4,5},{5,6},{6,7},{8,9},{9,10},{10,11},{11... | collective-permute-start | bytes 4325384 | tf_op jit(solution)/shard_map/ppermute | solution.py:24
  8.7 1.1 convert_reduce_fusion
  9.8 1.0 broadcast_maximum_fusion
  10.8 0.0 copy-start.10
  10.8 0.3 fusion.24
  11.1 0.5 reshape.137
  11.7 74.7 %fusion = f32[128,128]{1,0:T(8,128)S(1)} fusion(f32[992,128]{1,0:T(8,128)S(1)} %fusion.18), kind=kCustom, calls=%all-reduce-scatter | all-reduce-scatter fusion | flops 131073 | bytes 573952
  86.4 1.4 collective-permute-start.2
  87.8 0.7 broadcast_compare_fusion
  88.6 1.0 broadcast_maximum_fusion.1
  89.5 1.8 convert_multiply_fusion
  91.4 2.4 %slice_reduce_fusion.8 = (f32[5632]{0:T(1024)S(1)}, f32[5632]{0:T(1024)S(1)}, f32[5632]{0:T(1024)S(1)}, f32[5632]{0:T(1024)S(1)}, f32[5632]{0:T(1024)}, /*index=...) fusion(f32[3,3,5632]{2,1,0:T(4,128)} %param.11), kind=kLoop, calls=%fused_computation.43 | loop fusion | bytes 405504 | tf_op jit(solution)/shard_map/slice | solution.py:69
  93.8 0.6 dynamic-slice.6
  95.0 0.0 collective-permute-done.2
  95.1 0.3 concatenate.12
  95.4 10.7 %psum.14 = f32[124,128]{1,0:T(8,128)S(1)} all-reduce(f32[124,128]{1,0:T(8,128)S(1)} %constant_dynamic-slice_fusion.1), channel_id=1, replica_groups=mesh['frame'=4,'row'=8] {'frame'}, use_global_device_ids=true, to_apply=%region_2.3 | all-reduce | flops 15872 | bytes 126976 | tf_op jit(solution)/shard_map/psum | solution.py:74
  106.0 31.3 %all-gather = f32[8,124,128]{2,1,0:T(8,128)S(1)} all-gather(f32[1,124,128]{2,1,0:T(8,128)S(1)} %bitcast.84), channel_id=1, replica_groups=mesh['frame'=4,'row'=8] {'row'}, dimensions={0}, use_global_device_ids=true | all-gather | bytes 571392 | tf_op jit(solution)/shard_map/all_gather | solution.py:75
  137.3 0.8 reshape.139
  138.2 0.7 slice.84
  138.9 0.1 reshape.158
  139.0 0.3 fusion.25
  139.4 1.1 reshape.141
  140.5 2.6 %fusion.19 = f32[10,112,112]{2,1,0:T(8,128)} fusion(bf16[128,10,112]{0,2,1:T(8,128)(2,1)S(1)} %bitcast.74, f32[128,10,112]{0,2,1:T(8,128)} %bitcast.79, f32[128,10]{0,1:T(8,128)S(1)} %fusion.20), kind=kOutput, calls=%fused_computation.31 | convolution fusion | flops 192819200 | bytes 1367040 | tf_op jit(solution)/shard_map/nhd,nhe->hde/dot_general | solution.py:85
  143.1 1.7 fusion.16
  144.8 1.5 reshape.142
  146.4 0.5 fusion.21
  146.9 0.1 reshape.143
  147.1 0.1 reshape.140
  147.2 25.5 %fusion.1 = f32[128,128]{1,0:T(8,128)S(1)} fusion(f32[992,128]{1,0:T(8,128)S(1)} %fusion.17), kind=kCustom, calls=%all-reduce-scatter.1 | all-reduce-scatter fusion | flops 131073 | bytes 573952
  172.6 1.3 collective-permute-start.3
  173.9 2.7 %fusion.15 = bf16[128,10,112]{0,2,1:T(8,128)(2,1)} fusion(f32[10,112,112]{2,1,0:T(8,128)} %reshape.141, bf16[128,10,112]{0,2,1:T(8,128)(2,1)S(1)} %bitcast.77, f32[10,112]{1,0:T(8,128)S(1)} %reshape.140, f32[128,10]{0,1:T(8,128)S(1)} %fusion.23, f32[128,10,112]{0,2,1:T(8,128)} %bitcast.80, f32[128,10]{0,1:T(8,128)S(1)} %fusion.20), kind=kOutput, calls=%fused_computation.19 | convolution fusion | flops 193679360 | bytes 1663360 | tf_op jit(solution)/shard_map/hde,nhe->nhd/dot_general | solution.py:94
  176.7 0.3 concatenate.13
  177.0 10.7 %psum.15 = f32[124,128]{1,0:T(8,128)S(1)} all-reduce(f32[124,128]{1,0:T(8,128)S(1)} %constant_dynamic-slice_fusion), channel_id=1, replica_groups=mesh['frame'=4,'row'=8] {'frame'}, use_global_device_ids=true, to_apply=%region_5.6 | all-reduce | flops 15872 | bytes 126976 | tf_op jit(solution)/shard_map/psum | solution.py:90
  187.6 31.3 %all-gather.1 = f32[8,124,128]{2,1,0:T(8,128)S(1)} all-gather(f32[1,124,128]{2,1,0:T(8,128)S(1)} %bitcast.85), channel_id=1, replica_groups=mesh['frame'=4,'row'=8] {'row'}, dimensions={0}, use_global_device_ids=true | all-gather | bytes 571392 | tf_op jit(solution)/shard_map/all_gather | solution.py:91
  218.9 0.8 copy-done.2
  219.7 0.8 reshape.146
  220.6 2.0 reshape.150
  222.5 1.3 slice.87
  223.8 1.9 slice.86
  225.7 1.4 add.63
  227.1 2.2 reshape.145
  229.2 2.4 convolution_convert_fusion
  231.6 2.3 fusion.14
  234.0 2.6 %fusion.7 = bf16[1,3,130,5632]{3,2,1,0:T(8,128)(2,1)S(1)} fusion(bf16[1,1,128,5632]{3,2,1,0:T(8,128)(2,1)S(1)} %collective-permute-done.1, bf16[1,1,128,5632]{3,2,1,0:T(8,128)(2,1)S(1)} %copy-done.1, bf16[1,1,128,5632]{3,2,1,0:T(8,128)(2,1)} %collective-permute-done), kind=kLoop, calls=%fused_computation.7 | loop fusion | flops 26357760 | bytes 8718336 | tf_op jit(solution)/shard_map/concatenate | solution.py:26
  236.7 4.8 %add_convert_fusion = bf16[1,1,128,5632]{3,2,1,0:T(8,128)(2,1)} fusion(bf16[1,1,128,5632]{3,2,1,0:T(8,128)(2,1)} %collective-permute-done, bf16[1,1,128,5632]{3,2,1,0:T(8,128)(2,1)S(1)} %copy-done.1, bf16[1,1,128,5632]{3,2,1,0:T(8,128)(2,1)S(1)} %collective-permute-done.1, bf16[1,3,130,5632]{3,2,1,0:T(8,128)(2,1)S(1)} %fusion.7, f32[5632]{0:T(1024)S(1)} %copy-done.8, ...), kind=kLoop, calls=%fused_computation.8 | loop fusion | flops 19464192 | bytes 14620672 | tf_op jit(solution)/shard_map/convert_element_type | solution.py:70
  (32 shorter events, 0.3 us)
Async XLA Ops:
  0.6 10.2 %copy-start = (bf16[1,1,128,1120]{2,3,1,0:T(8,128)(2,1)S(1)}, bf16[1,1,128,1120]{2,3,1,0:T(8,128)(2,1)}, u32[]{:S(2)}) copy-start(bf16[1,1,128,1120]{2,3,1,0:T(8,128)(2,1)} %param.8) | copy-start | bytes 860164
  0.6 87.2 %copy-start.3 = (bf16[1,1,128,1120]{2,3,1,0:T(8,128)(2,1)S(1)}, bf16[1,1,128,1120]{2,3,1,0:T(8,128)(2,1)}, u32[]{:S(2)}) copy-start(bf16[1,1,128,1120]{2,3,1,0:T(8,128)(2,1)} %param.7) | copy-start | bytes 860164
  0.7 233.3 %collective-permute-start.1 = (bf16[1,1,128,5632]{3,2,1,0:T(8,128)(2,1)}, bf16[1,1,128,5632]{3,2,1,0:T(8,128)(2,1)S(1)}, u32[]{:S(2)}, u32[]{:S(2)}) collective-permute-start(bf16[1,1,128,5632]{3,2,1,0:T(8,128)(2,1)} %param.10), channel_id=1, source_target_pairs={{1,0},{2,1},{3,2},{4,3},{5,4},{6,5},{7,6},{9,8},{10,9},{11,10},{12... | collective-permute-start | bytes 4325384 | tf_op jit(solution)/shard_map/ppermute | solution.py:25
  2.1 231.9 %collective-permute-start = (bf16[1,1,128,5632]{3,2,1,0:T(8,128)(2,1)}, bf16[1,1,128,5632]{3,2,1,0:T(8,128)(2,1)}, u32[]{:S(2)}, u32[]{:S(2)}) collective-permute-start(bf16[1,1,128,5632]{3,2,1,0:T(8,128)(2,1)} %param.10), channel_id=1, source_target_pairs={{0,1},{1,2},{2,3},{3,4},{4,5},{5,6},{6,7},{8,9},{9,10},{10,11},{11... | collective-permute-start | bytes 4325384 | tf_op jit(solution)/shard_map/ppermute | solution.py:24
  10.8 83.0 %copy-start.10 = (u32[32]{0:T(128)S(1)}, u32[32]{0:T(128)}, u32[]{:S(2)}) copy-start(u32[32]{0:T(128)} %constant.26) | copy-start | bytes 388
  86.4 8.7 %collective-permute-start.2 = (f32[28,128]{1,0:T(8,128)S(1)}, f32[28,128]{1,0:T(8,128)S(1)}, u32[]{:S(2)}, u32[]{:S(2)}) collective-permute-start(f32[28,128]{1,0:T(8,128)S(1)} %slice.94), channel_id=1, source_target_pairs={{0,1},{1,2},{2,3},{3,4},{4,5},{5,6},{6,7},{8,9},{9,10},{10,11},{11... | collective-permute-start | bytes 43016
  138.9 4.2 %copy-start.4 = (f32[1,1,128,1120]{2,3,1,0:T(8,128)S(1)}, f32[1,1,128,1120]{2,3,1,0:T(8,128)}, u32[]{:S(2)}) copy-start(f32[1,1,128,1120]{2,3,1,0:T(8,128)} %convert_multiply_fusion) | copy-start | bytes 1720324
  172.6 4.0 %collective-permute-start.3 = (f32[28,128]{1,0:T(8,128)S(1)}, f32[28,128]{1,0:T(8,128)S(1)}, u32[]{:S(2)}, u32[]{:S(2)}) collective-permute-start(f32[28,128]{1,0:T(8,128)S(1)} %slice.95), channel_id=1, source_target_pairs={{0,1},{1,2},{2,3},{3,4},{4,5},{5,6},{6,7},{8,9},{9,10},{10,11},{11... | collective-permute-start | bytes 43016
  218.9 0.8 copy-start.2
  220.5 13.4 %copy-start.1 = (bf16[1,1,128,5632]{3,2,1,0:T(8,128)(2,1)S(1)}, bf16[1,1,128,5632]{3,2,1,0:T(8,128)(2,1)}, u32[]{:S(2)}) copy-start(bf16[1,1,128,5632]{3,2,1,0:T(8,128)(2,1)} %param.10) | copy-start | bytes 4325380
  233.9 2.7 %copy-start.5 = (f32[5632]{0:T(1024)S(1)}, f32[5632]{0:T(1024)}, u32[]{:S(2)}) copy-start(f32[5632]{0:T(1024)} %get-tuple-element.8) | copy-start | bytes 67588
  233.9 2.7 %copy-start.6 = (f32[5632]{0:T(1024)S(1)}, f32[5632]{0:T(1024)}, u32[]{:S(2)}) copy-start(f32[5632]{0:T(1024)} %get-tuple-element.9) | copy-start | bytes 67588
  233.9 2.7 %copy-start.7 = (f32[5632]{0:T(1024)S(1)}, f32[5632]{0:T(1024)}, u32[]{:S(2)}) copy-start(f32[5632]{0:T(1024)} %get-tuple-element.10) | copy-start | bytes 67588
  233.9 2.7 %copy-start.8 = (f32[5632]{0:T(1024)S(1)}, f32[5632]{0:T(1024)}, u32[]{:S(2)}) copy-start(f32[5632]{0:T(1024)} %get-tuple-element.11) | copy-start | bytes 67588
  234.0 2.7 %copy-start.9 = (f32[5632]{0:T(1024)S(1)}, f32[5632]{0:T(1024)}, u32[]{:S(2)}) copy-start(f32[5632]{0:T(1024)} %get-tuple-element.12) | copy-start | bytes 67588
where the time goes:
time: 242 us; the launch traced here: 241 us
  blocking collectives  184 us (76%)
  local copies, waits for them, and re-layouts  18.9 us (8%)
  other arithmetic  13.2 us (5%)
  matrix products  12.9 us (5%)
  starting transfers between devices  10.7 us (4%)
    unnamed x2, blocking collectives  100 us
    all_gather x1, blocking collectives, shards(): state_whole = lax.all_gather(state_share, 'row', axis=0, tiled=True)  31.3 us
    all_gather x1, blocking collectives, shards(): grad_whole = lax.all_gather(grad_share, 'row', axis=0, tiled=True)  31.3 us
    psum x1, blocking collectives, shards(): state_share = lax.psum(state_share, 'frame')  10.7 us
    psum x1, blocking collectives, shards(): grad_share = lax.psum(grad_share, 'frame')  10.7 us
    ppermute x1, starting transfers between devices, padded(): before = lax.ppermute(last, axis, up)  6.6 us
  transfers between devices with their start and end apart: 4, of which 0 were waited for; matrix products, arithmetic and copies ran while one was open for 57% of the time, Pallas kernels for 0%

commit v1 on v0

v1 whole, which is shorter than its diff:
```python
import functools
import math

import jax
import jax.numpy as jnp
from jax import lax
from jax.experimental import pallas as pl
from jax.experimental.pallas import tpu as pltpu
from jax.sharding import Mesh, PartitionSpec as P

HEADS = 10
HD = 112
EPSILON = 1e-06
HALF = HEADS // 2
CHUNKS = 2
CHIPS = ("y", "z", "x")
F32 = jnp.float32
BF16 = jnp.bfloat16

NT = (((1,), (1,)), ((), ()))
TN = (((0,), (0,)), ((), ()))
NN = (((1,), (0,)), ((), ()))


def vmem(n):
    return [pl.BlockSpec(memory_space=pltpu.VMEM)] * n


def call(body, out_shape, args, scratch=(), flops=0):
    size = sum(math.prod(a.shape) * a.dtype.itemsize for a in list(args) + list(out_shape))
    return pl.pallas_call(
        body,
        out_shape=out_shape,
        in_specs=vmem(len(args)),
        out_specs=vmem(len(out_shape)),
        scratch_shapes=list(scratch),
        compiler_params=pltpu.CompilerParams(vmem_limit_bytes=48 * 1024 * 1024),
        cost_estimate=pl.CostEstimate(flops=flops, bytes_accessed=size, transcendentals=0),
    )(*args)


def dot(a, b, dims):
    return lax.dot_general(a, b, dims, preferred_element_type=F32)


def pieces(x):
    hi = x.astype(BF16)
    lo = (x - hi.astype(F32)).astype(BF16)
    return hi, lo


def split_heads(a_ref, b_ref, mine_ref, theirs_ref):
    core = lax.axis_index("c")
    for here in range(2):

        @pl.when(core == here)
        def _():
            for i, ref in enumerate((a_ref, b_ref)):
                for h in range(HEADS):
                    part = ref[:, h * HD : (h + 1) * HD]
                    dest = mine_ref if h // HALF == here else theirs_ref
                    dest[i, h % HALF] = part


def merge_heads(parts, n_out):
    def body(qm, qt, km, kt, q_ref, k_ref, v_ref):
        core = lax.axis_index("c")
        for here in range(2):

            @pl.when(core == here)
            def _():
                for h in range(HEADS):
                    own = h // HALF == here
                    cols = slice(h * HD, (h + 1) * HD)
                    q_ref[:, cols] = (qm if own else qt)[h % HALF]
                    k_ref[:, cols] = (km if own else kt)[0, h % HALF]
                    v_ref[:, cols] = (km if own else kt)[1, h % HALF]

    return body


def both(mine, theirs, i, h):
    return jnp.concatenate([mine[i, h], theirs[i, h]], axis=0)


def state_body(n, rows, mine, theirs, pay, whole):
    for h in range(HALF):
        key = jnp.maximum(both(mine, theirs, 0, h), 0)
        val = both(mine, theirs, 1, h)
        whole[h * HD : (h + 1) * HD] = dot(key, val, TN)
        norm = jnp.sum(key.astype(F32), axis=0, keepdims=True)
        pay[:, rows + h : rows + h + 1] = jnp.broadcast_to(norm[None], (n, 1, HD))
    for j in range(n):
        pay[j, :rows] = whole[j * rows : (j + 1) * rows]


def inverse(query, norm):
    den = jnp.sum(query * norm, axis=1, keepdims=True) + EPSILON
    return 1.0 / den


def grad_body(n, rows, scale, got, mine, theirs, pay, norm_ref, whole):
    total = got[0]
    for j in range(1, n):
        total = total + got[j]
    norm_ref[...] = total[rows : rows + HALF]
    for h in range(HALF):
        query = jnp.maximum(both(mine, theirs, 0, h), 0)
        grad = both(mine, theirs, 1, h)
        inv = inverse(query.astype(F32), total[rows + h : rows + h + 1])
        hi, lo = pieces(grad.astype(F32) * (inv * scale))
        whole[h * HD : (h + 1) * HD] = dot(query, hi, TN) + dot(query, lo, TN)
    shard = total[:rows]
    for j in range(n):
        pay[j, :rows] = shard
        pay[j, rows : 2 * rows] = whole[j * rows : (j + 1) * rows]


def query_body(n, rows, scale, tok, got, mine, theirs, norm_ref, pay, out_mine, out_theirs, whole):
    total = got[0, rows : 2 * rows]
    for j in range(1, n):
        total = total + got[j, rows : 2 * rows]
    for j in range(n):
        whole[j * rows : (j + 1) * rows] = got[j, :rows]
        pay[j, :rows] = total
    for h in range(HALF):
        query = jnp.maximum(both(mine, theirs, 0, h), 0).astype(F32)
        grad = both(mine, theirs, 1, h)
        norm = norm_ref[h : h + 1]
        inv = inverse(query, norm)
        hi, lo = pieces(whole[h * HD : (h + 1) * HD])
        prod = dot(grad, hi, NT) + dot(grad, lo, NT)
        weight = inv * scale
        proj = jnp.sum(query * prod, axis=1, keepdims=True) * weight * inv
        term = -jnp.sum(query * proj, axis=0, keepdims=True)
        pay[:, rows + h : rows + h + 1] = jnp.broadcast_to(term[None], (n, 1, HD))
        out = jnp.where(query > 0, prod * weight - proj * norm, 0.0).astype(BF16)
        out_mine[h] = out[:tok]
        out_theirs[h] = out[tok:]


def key_body(n, rows, tok, got, mine, theirs, out_mine, out_theirs, whole):
    total = got[0, rows : rows + HALF]
    for j in range(1, n):
        total = total + got[j, rows : rows + HALF]
    for j in range(n):
        whole[j * rows : (j + 1) * rows] = got[j, :rows]
    for h in range(HALF):
        key = both(mine, theirs, 0, h)
        val = both(mine, theirs, 1, h)
        hi, lo = pieces(whole[h * HD : (h + 1) * HD])
        k_out = dot(val, hi, NT) + dot(val, lo, NT) + total[h : h + 1]
        k_out = jnp.where(key > 0, k_out, 0.0).astype(BF16)
        feat = jnp.maximum(key, 0)
        v_out = (dot(feat, hi, NN) + dot(feat, lo, NN)).astype(BF16)
        out_mine[0, h] = k_out[:tok]
        out_theirs[0, h] = k_out[tok:]
        out_mine[1, h] = v_out[:tok]
        out_theirs[1, h] = v_out[tok:]


def conv_body(pair, far, weight, out):
    side = lax.axis_index("x")
    cols, width = out.shape
    even = pair[0].astype(F32)
    odd = pair[1].astype(F32)
    other = far[...].astype(F32)
    sums = []
    for j in range(3):
        w_even = weight[1 + side, pl.ds(j, 1)]
        w_odd = weight[side, pl.ds(j, 1)]
        w_other = weight[2 - 2 * side, pl.ds(j, 1)]
        sums.append(even * w_even + odd * w_odd + other * w_other)
    zero = jnp.zeros((1, width), F32)
    right = jnp.concatenate([sums[0][1:], zero], axis=0)
    left = jnp.concatenate([zero, sums[2][:-1]], axis=0)
    out[...] = (sums[1] + right + left).astype(BF16)


def conv(pair, far, weight, first, tile):
    _, cols, width = pair.shape
    return pl.pallas_call(
        conv_body,
        grid=(width // tile,),
        out_shape=jax.ShapeDtypeStruct((cols, width), BF16),
        in_specs=[
            pl.BlockSpec((2, cols, tile), lambda i: (0, 0, i)),
            pl.BlockSpec((cols, tile), lambda i: (0, i)),
            pl.BlockSpec((3, 3, tile), lambda i: (0, 0, i + first // tile)),
        ],
        out_specs=pl.BlockSpec((cols, tile), lambda i: (0, i)),
        cost_estimate=pl.CostEstimate(
            flops=20 * cols * width, bytes_accessed=8 * cols * width, transcendentals=0
        ),
    )(pair, far, weight)


def shards(queries, key_proj, value_proj, attn_grad, conv_grad, conv_weight):
    tok = queries.shape[0] * queries.shape[1] * queries.shape[2]
    tokens_all = tok * lax.axis_size(("y", "c", "z", "x"))
    scale = math.sqrt(tokens_all)
    n = lax.axis_size(CHIPS)
    rows = -(-HALF * HD // n)
    pay_one = -(-(rows + HALF) // 8) * 8
    pay_two = -(-2 * rows // 8) * 8
    swap = [(0, 1), (1, 0)]
    q, k, v, g = (a.reshape(tok, HEADS * HD) for a in (queries, key_proj, value_proj, attn_grad))
    sd = jax.ShapeDtypeStruct
    scratch = [pltpu.VMEM((n * rows, HD), F32)]
    pair_shape = [sd((2, HALF, tok, HD), BF16)] * 2

    z_size = lax.axis_size("z")
    ahead = [(2 * z, 2 * z + 2) for z in range(z_size - 1)]
    back = [(2 * z + 3, 2 * z + 1) for z in range(z_size - 1)]
    cols, ch = conv_grad.shape[2:]
    width = ch // CHUNKS
    pairs = [
        lax.all_gather(
            conv_grad.reshape(cols, ch)[:, i * width : (i + 1) * width], "x", axis=0, tiled=False
        )
        for i in range(CHUNKS)
    ]

    kv_mine, kv_send = call(split_heads, pair_shape, (k, v))
    kv_got = lax.ppermute(kv_send, "c", swap)
    qg_mine, qg_send = call(split_heads, pair_shape, (q, g))
    qg_got = lax.ppermute(qg_send, "c", swap)

    def exchange(pay):
        return lax.all_to_all(pay, CHIPS, split_axis=0, concat_axis=0, tiled=True)

    macs = HALF * 2 * tok * HD * HD
    (pay,) = call(
        functools.partial(state_body, n, rows),
        [sd((n, pay_one, HD), F32)],
        (kv_mine, kv_got),
        scratch,
        flops=2 * macs,
    )
    got = exchange(pay)
    pay, norm = call(
        functools.partial(grad_body, n, rows, scale),
        [sd((n, pay_two, HD), F32), sd((HALF, HD), F32)],
        (got, qg_mine, qg_got),
        scratch,
        flops=4 * macs,
    )
    got = exchange(pay)
    pay, query_mine, query_send = call(
        functools.partial(query_body, n, rows, scale, tok),
        [sd((n, pay_one, HD), F32)] + [sd((HALF, tok, HD), BF16)] * 2,
        (got, qg_mine, qg_got, norm),
        scratch,
        flops=4 * macs,
    )
    query_got = lax.ppermute(query_send, "c", swap)
    got = exchange(pay)
    key_mine, key_send = call(
        functools.partial(key_body, n, rows, tok),
        pair_shape,
        (got, kv_mine, kv_got),
        scratch,
        flops=8 * macs,
    )
    key_got = lax.ppermute(key_send, "c", swap)
    outs = call(
        merge_heads(None, 3),
        [sd((tok, HEADS * HD), BF16)] * 3,
        (query_mine, query_got, key_mine, key_got),
    )

    side = lax.axis_index("x")
    made = []
    for i, pair in enumerate(pairs):
        near = lax.dynamic_index_in_dim(pair, 1 - side, axis=0, keepdims=False)
        far = lax.ppermute(near, ("z", "x"), ahead + back)
        made.append(conv(pair, far, conv_weight, i * width, 256))
    input_grad = jnp.concatenate(made, axis=1)
    return tuple(o.reshape(queries.shape) for o in outs) + (input_grad.reshape(conv_grad.shape),)


def solution(mesh):
    frames, bands = mesh.shape["frame"], mesh.shape["row"]
    fine = Mesh(mesh.devices.reshape(frames // 2, 2, bands // 2, 2), ("y", "c", "z", "x"))
    split = P(("y", "c"), ("z", "x"), None, None)
    return jax.shard_map(
        shards,
        mesh=fine,
        in_specs=(split,) * 5 + (P(),),
        out_specs=(split,) * 4,
        check_vma=False,
    )
```

time: 242 us -> 116 us (0.48)
  the two profiles are of different devices: /device:TPU:0 before, /device:TPU:17 now
where the time goes in v1:
time: 116 us; the launch traced here: 115 us
  waiting for transfers between devices  36.9 us (32%)
  starting transfers between devices  31.7 us (27%)
  Pallas kernels  20.2 us (17%)
  between operations  14.1 us (12%)
  local copies, waits for them, and re-layouts  11.1 us (10%)
  other arithmetic  1.19 us (1%)
    all_gather x2, waiting for transfers between devices, shards(): lax.all_gather(conv_grad.reshape(cols, ch)[:, i * width:(i + 1) * width],...  27.4 us
    all_to_all x3, starting transfers between devices, exchange(): return lax.all_to_all(pay, CHIPS, split_axis=0, concat_axis=0, tiled=True)  16.8 us
    pallas_call x2, Pallas kernels, conv(): pl.pallas_call(conv_body, grid=(width // tile,), out_shape=jax.ShapeDtype...  14.7 us
    ppermute x2, starting transfers between devices, shards(): far = lax.ppermute(near, ('z', 'x'), ahead + back)  6.61 us
    all_to_all x3, waiting for transfers between devices, exchange(): return lax.all_to_all(pay, CHIPS, split_axis=0, concat_axis=0, tiled=True)  6.2 us
    pallas_call x7, Pallas kernels, call(): pl.pallas_call(body, out_shape=out_shape, in_specs=vmem(len(args)), out_s...  5.47 us
    ppermute x1, starting transfers between devices, shards(): key_got = lax.ppermute(key_send, 'c', swap)  4.92 us
    unnamed x21, local copies, waits for them, and re-layouts  4.54 us
  transfers between devices with their start and end apart: 11, of which 6 were waited for; matrix products, arithmetic and copies ran while one was open for 5% of the time, Pallas kernels for 17%

profile of v1, /device:TPU:17, one launch (start us, length us, event | category | flops | bytes accessed | tf_op | source)
XLA Modules:
  0.0 115.2 jit_solution(16295069967468352436)
XLA Ops:
  7.2 0.0 all-gather.5.cloned.1.call-start
  7.2 2.5 %fusion = (bf16[128,2816]{1,0:T(8,128)(2,1)}, bf16[128,2816]{1,0:T(8,128)(2,1)}) fusion(bf16[128,5632]{1,0:T(8,128)(2,1)} %bitcast.27), kind=kLoop, calls=%fused_computation.3 | loop fusion | bytes 2883584 | tf_op jit(solution)/shard_map/slice | solution.py:219
  9.7 0.0 all-gather.5.cloned.1.call-update
  9.8 0.0 all-gather.7.cloned.1.call-start
  9.8 0.7 all-gather.7.cloned.1.call-update
  10.5 0.2 copy-done.3
  10.7 0.2 copy.10
  10.9 0.0 copy-start.5
  10.9 0.2 copy.11
  11.1 0.0 copy-start.6
  11.1 0.3 shard_map.93
  11.5 0.7 collective-permute-start
  12.2 1.3 %collective-permute-done.theirs = bf16[2,5,128,112]{3,2,1,0:T(8,128)(2,1)S(1)} collective-permute-done((bf16[2,5,128,112]{3,2,1,0:T(8,128)(2,1)S(1)}, bf16[2,5,128,112]{3,2,1,0:T(8,128)(2,1)S(1)}, u32[]{:S(2)}, u32[]{:S(2)}) %collective-permute-start) | collective-permute-done | bytes 286752 | tf_op jit(solution)/shard_map/ppermute | solution.py:225
  13.5 1.0 shard_map.94
  14.5 6.5 %all-to-all-start = ((f32[16,40,112]{2,1,0:T(8,128)}), f32[16,40,112]{2,1,0:T(8,128)S(1)}, u32[]{:S(2)}, u32[]{:S(2)}) async-start(f32[16,40,112]{2,1,0:T(8,128)} %shard_map.94), calls=%async_computation | async-start | bytes 655360 | tf_op jit(solution)/shard_map/all_to_all | solution.py:230
  21.1 0.2 copy.12
  21.3 0.2 copy.13
  21.5 0.3 shard_map.95
  21.8 1.0 collective-permute-start.1
  22.8 1.3 %collective-permute-done.1.theirs = bf16[2,5,128,112]{3,2,1,0:T(8,128)(2,1)S(1)} collective-permute-done((bf16[2,5,128,112]{3,2,1,0:T(8,128)(2,1)S(1)}, bf16[2,5,128,112]{3,2,1,0:T(8,128)(2,1)S(1)}, u32[]{:S(2)}, u32[]{:S(2)}) %collective-permute-start.1) | collective-permute-done | bytes 286752 | tf_op jit(solution)/shard_map/ppermute | solution.py:227
  24.1 6.2 %all-to-all-done.got = f32[16,40,112]{2,1,0:T(8,128)S(1)} async-done(((f32[16,40,112]{2,1,0:T(8,128)}), f32[16,40,112]{2,1,0:T(8,128)S(1)}, u32[]{:S(2)}, u32[]{:S(2)}) %all-to-all-start) | async-done | bytes 286752 | tf_op jit(solution)/shard_map/all_to_all | solution.py:230
  30.3 1.4 %shard_map.96 = (f32[16,72,112]{2,1,0:T(8,128)}, f32[5,112]{1,0:T(8,128)S(1)}) custom-call(f32[16,40,112]{2,1,0:T(8,128)S(1)} %all-to-all-done.got, bf16[2,5,128,112]{3,2,1,0:T(8,128)(2,1)S(1)} %get-tuple-element.20.mine, bf16[2,5,128,112]{3,2,1,0:T(8,128)(2,1)S(1)} %collective-permute-done.1.theirs), custom_call_target="tpu_custom_call" | custom-call | flops 64225280 | bytes 1378496 | tf_op jit(solution)/shard_map/pallas_call | solution.py:31
  31.7 4.9 %all-to-all-start.1 = ((f32[16,72,112]{2,1,0:T(8,128)}), f32[16,72,112]{2,1,0:T(8,128)S(1)}, u32[]{:S(2)}, u32[]{:S(2)}) async-start(f32[16,72,112]{2,1,0:T(8,128)} %get-tuple-element.22), calls=%async_computation.1 | async-start | bytes 1179648 | tf_op jit(solution)/shard_map/all_to_all | solution.py:230
  36.6 4.4 %all-gather.5.cloned.1.call-done = bf16[256,2816]{1,0:T(8,128)(2,1)} async-done(((bf16[128,2816]{1,0:T(8,128)(2,1)}), bf16[256,2816]{1,0:T(8,128)(2,1)}) %all-gather.5.cloned.1.call-update) | async-done | bytes 1441808 | tf_op jit(solution)/shard_map/all_gather | solution.py:218
  41.0 2.0 %dynamic-slice_bitcast_fusion.1 = bf16[128,2816]{1,0:T(8,128)(2,1)} fusion(bf16[2,128,2816]{2,1,0:T(8,128)(2,1)} %bitcast.23, s32[]{:T(128)S(6)} %select_n.5), kind=kLoop, calls=%fused_computation.2 | loop fusion | bytes 1441796 | tf_op jit(solution)/shard_map/jit(dynamic_index_in_dim)/squeeze | solution.py:275
  43.0 3.5 %collective-permute-start.4 = (bf16[128,2816]{1,0:T(8,128)(2,1)}, bf16[128,2816]{1,0:T(8,128)(2,1)S(1)}, u32[]{:S(2)}, u32[]{:S(2)}) collective-permute-start(bf16[128,2816]{1,0:T(8,128)(2,1)} %dynamic-slice_bitcast_fusion.1), channel_id=1, source_target_pairs={{0,2},{2,4},{4,6},{3,1},{5,3},{7,5},{8,10},{10,12},{12,14},{11,9},... | collective-permute-start | bytes 2162696 | tf_op jit(solution)/shard_map/ppermute | solution.py:276
  46.5 23.0 %all-gather.7.cloned.1.call-done = bf16[256,2816]{1,0:T(8,128)(2,1)} async-done(((bf16[128,2816]{1,0:T(8,128)(2,1)}), bf16[256,2816]{1,0:T(8,128)(2,1)}) %all-gather.7.cloned.1.call-update) | async-done | bytes 1441808 | tf_op jit(solution)/shard_map/all_gather | solution.py:218
  69.5 2.0 %dynamic-slice_bitcast_fusion = bf16[128,2816]{1,0:T(8,128)(2,1)} fusion(bf16[2,128,2816]{2,1,0:T(8,128)(2,1)} %bitcast.25, s32[]{:T(128)S(6)} %select_n.5), kind=kLoop, calls=%fused_computation.1 | loop fusion | bytes 1441796 | tf_op jit(solution)/shard_map/jit(dynamic_index_in_dim)/squeeze | solution.py:275
  71.6 3.1 %collective-permute-start.5 = (bf16[128,2816]{1,0:T(8,128)(2,1)}, bf16[128,2816]{1,0:T(8,128)(2,1)}, u32[]{:S(2)}, u32[]{:S(2)}) collective-permute-start(bf16[128,2816]{1,0:T(8,128)(2,1)} %dynamic-slice_bitcast_fusion), channel_id=1, source_target_pairs={{0,2},{2,4},{4,6},{3,1},{5,3},{7,5},{8,10},{10,12},{12,14},{11,9},... | collective-permute-start | bytes 2162696 | tf_op jit(solution)/shard_map/ppermute | solution.py:276
  74.7 0.0 all-to-all-done.1.got
  74.7 1.4 %shard_map.97 = (f32[16,40,112]{2,1,0:T(8,128)}, bf16[5,128,112]{2,1,0:T(8,128)(2,1)S(1)}, bf16[5,128,112]{2,1,0:T(8,128)(2,1)S(1)}) custom-call(f32[16,72,112]{2,1,0:T(8,128)S(1)} %all-to-all-done.1.got, bf16[2,5,128,112]{3,2,1,0:T(8,128)(2,1)S(1)} %get-tuple-element.20.mine, bf16[2,5,128,112]{3,2,1,0:T(8,128)(2,1)S(1)} %collective-permute-done.1.theirs, ...), custom_call_target="tpu_custom_call" | custom-call | flops 64225280 | bytes 1665216 | tf_op jit(solution)/shard_map/pallas_call | solution.py:31
  76.0 5.4 %all-to-all-start.2 = ((f32[16,40,112]{2,1,0:T(8,128)}), f32[16,40,112]{2,1,0:T(8,128)S(1)}, u32[]{:S(2)}, u32[]{:S(2)}) async-start(f32[16,40,112]{2,1,0:T(8,128)} %get-tuple-element.26), calls=%async_computation.2 | async-start | bytes 655360 | tf_op jit(solution)/shard_map/all_to_all | solution.py:230
  81.4 1.5 %collective-permute-start.2 = (bf16[5,128,112]{2,1,0:T(8,128)(2,1)S(1)}, bf16[5,128,112]{2,1,0:T(8,128)(2,1)S(1)}, u32[]{:S(2)}, u32[]{:S(2)}) collective-permute-start(bf16[5,128,112]{2,1,0:T(8,128)(2,1)S(1)} %get-tuple-element.25), channel_id=1, source_target_pairs={{0,8},{8,0},{1,9},{9,1},{2,10},{10,2},{3,11},{11,3},{4,12},{12,4},... | collective-permute-start | bytes 430088 | tf_op jit(solution)/shard_map/ppermute | solution.py:256
  82.9 0.0 collective-permute-done.4.far
  82.9 0.9 copy-done.2
  83.8 7.3 %shard_map.100 = bf16[128,2816]{1,0:T(8,128)(2,1)} custom-call(bf16[2,128,2816]{2,1,0:T(8,128)(2,1)} %bitcast.24, bf16[128,2816]{1,0:T(8,128)(2,1)} %copy-done.2, f32[3,3,5632]{2,1,0:T(4,128)} %weight.3), custom_call_target="tpu_custom_call" | custom-call | flops 7208960 | bytes 2883584 | tf_op jit(solution)/shard_map/pallas_call | solution.py:182
  91.1 0.0 collective-permute-done.5.far
  91.1 7.4 %shard_map.101 = bf16[128,2816]{1,0:T(8,128)(2,1)} custom-call(bf16[2,128,2816]{2,1,0:T(8,128)(2,1)} %bitcast.26, bf16[128,2816]{1,0:T(8,128)(2,1)} %collective-permute-done.5.far, f32[3,3,5632]{2,1,0:T(4,128)} %weight.3), custom_call_target="tpu_custom_call" | custom-call | flops 7208960 | bytes 2883584 | tf_op jit(solution)/shard_map/pallas_call | solution.py:182
  98.5 0.0 all-to-all-done.2.got
  98.5 0.5 shard_map.98
  99.0 4.9 %collective-permute-start.3 = (bf16[2,5,128,112]{3,2,1,0:T(8,128)(2,1)S(1)}, bf16[2,5,128,112]{3,2,1,0:T(8,128)(2,1)S(1)}, u32[]{:S(2)}, u32[]{:S(2)}) collective-permute-start(bf16[2,5,128,112]{3,2,1,0:T(8,128)(2,1)S(1)} %get-tuple-element.28), channel_id=1, source_target_pairs={{0,8},{8,0},{1,9},{9,1},{2,10},{10,2},{3,11},{11,3},{4,12},{12,4},... | collective-permute-start | bytes 860168 | tf_op jit(solution)/shard_map/ppermute | solution.py:265
  104.0 1.2 %maximum_bitcast_fusion = bf16[1,1,128,5632]{3,2,1,0:T(8,128)(2,1)} fusion(bf16[128,2816]{1,0:T(8,128)(2,1)S(1)} %copy-done.1, bf16[128,2816]{1,0:T(8,128)(2,1)S(1)} %copy-done), kind=kLoop, calls=%fused_computation | loop fusion | flops 2883584 | bytes 2883584 | tf_op jit(solution)/shard_map/reshape | solution.py:279
  105.2 0.0 collective-permute-done.2.qt
  105.2 0.1 collective-permute-done.3.kt
  105.2 0.5 shard_map.99
  105.7 0.9 copy.14
  106.6 0.9 copy.15
  107.5 0.9 copy.16
  (10 shorter events, 0.0 us)
Async XLA Ops:
  7.2 33.8 %all-gather.5.cloned.1.call-start = ((), (), s32[]{:S(2)}) async-start(), calls=%async_computation.3 | async-start | bytes 2162688 | tf_op jit(solution)/shard_map/all_gather | solution.py:218
  9.7 1.0 copy-start.3
  9.7 1.2 %copy-start.4 = (bf16[1,1,128,1120]{2,3,1,0:T(8,128)(2,1)S(1)}, bf16[1,1,128,1120]{2,3,1,0:T(8,128)(2,1)}, u32[]{:S(2)}) copy-start(bf16[1,1,128,1120]{2,3,1,0:T(8,128)(2,1)} %param.8) | copy-start | bytes 860164
  9.8 59.8 %all-gather.7.cloned.1.call-start = ((), (), s32[]{:S(2)}) async-start(), calls=%async_computation.4 | async-start | bytes 2162688 | tf_op jit(solution)/shard_map/all_gather | solution.py:218
  10.9 10.1 %copy-start.5 = (bf16[1,1,128,1120]{2,3,1,0:T(8,128)(2,1)S(1)}, bf16[1,1,128,1120]{2,3,1,0:T(8,128)(2,1)}, u32[]{:S(2)}) copy-start(bf16[1,1,128,1120]{2,3,1,0:T(8,128)(2,1)} %param.6) | copy-start | bytes 860164
  11.1 10.1 %copy-start.6 = (bf16[1,1,128,1120]{2,3,1,0:T(8,128)(2,1)S(1)}, bf16[1,1,128,1120]{2,3,1,0:T(8,128)(2,1)}, u32[]{:S(2)}) copy-start(bf16[1,1,128,1120]{2,3,1,0:T(8,128)(2,1)} %param.9) | copy-start | bytes 860164
  11.5 2.0 %collective-permute-start = (bf16[2,5,128,112]{3,2,1,0:T(8,128)(2,1)S(1)}, bf16[2,5,128,112]{3,2,1,0:T(8,128)(2,1)S(1)}, u32[]{:S(2)}, u32[]{:S(2)}) collective-permute-start(bf16[2,5,128,112]{3,2,1,0:T(8,128)(2,1)S(1)} %get-tuple-element.19), channel_id=1, source_target_pairs={{0,8},{8,0},{1,9},{9,1},{2,10},{10,2},{3,11},{11,3},{4,12},{12,4},... | collective-permute-start | bytes 860168 | tf_op jit(solution)/shard_map/ppermute | solution.py:225
  14.5 15.8 %all-to-all-start = ((f32[16,40,112]{2,1,0:T(8,128)}), f32[16,40,112]{2,1,0:T(8,128)S(1)}, u32[]{:S(2)}, u32[]{:S(2)}) async-start(f32[16,40,112]{2,1,0:T(8,128)} %shard_map.94), calls=%async_computation | async-start | bytes 655360 | tf_op jit(solution)/shard_map/all_to_all | solution.py:230
  21.8 2.3 %collective-permute-start.1 = (bf16[2,5,128,112]{3,2,1,0:T(8,128)(2,1)S(1)}, bf16[2,5,128,112]{3,2,1,0:T(8,128)(2,1)S(1)}, u32[]{:S(2)}, u32[]{:S(2)}) collective-permute-start(bf16[2,5,128,112]{3,2,1,0:T(8,128)(2,1)S(1)} %get-tuple-element.21), channel_id=1, source_target_pairs={{0,8},{8,0},{1,9},{9,1},{2,10},{10,2},{3,11},{11,3},{4,12},{12,4},... | collective-permute-start | bytes 860168 | tf_op jit(solution)/shard_map/ppermute | solution.py:227
  31.7 42.9 %all-to-all-start.1 = ((f32[16,72,112]{2,1,0:T(8,128)}), f32[16,72,112]{2,1,0:T(8,128)S(1)}, u32[]{:S(2)}, u32[]{:S(2)}) async-start(f32[16,72,112]{2,1,0:T(8,128)} %get-tuple-element.22), calls=%async_computation.1 | async-start | bytes 1179648 | tf_op jit(solution)/shard_map/all_to_all | solution.py:230
  43.0 39.9 %collective-permute-start.4 = (bf16[128,2816]{1,0:T(8,128)(2,1)}, bf16[128,2816]{1,0:T(8,128)(2,1)S(1)}, u32[]{:S(2)}, u32[]{:S(2)}) collective-permute-start(bf16[128,2816]{1,0:T(8,128)(2,1)} %dynamic-slice_bitcast_fusion.1), channel_id=1, source_target_pairs={{0,2},{2,4},{4,6},{3,1},{5,3},{7,5},{8,10},{10,12},{12,14},{11,9},... | collective-permute-start | bytes 2162696 | tf_op jit(solution)/shard_map/ppermute | solution.py:276
  71.6 19.6 %collective-permute-start.5 = (bf16[128,2816]{1,0:T(8,128)(2,1)}, bf16[128,2816]{1,0:T(8,128)(2,1)}, u32[]{:S(2)}, u32[]{:S(2)}) collective-permute-start(bf16[128,2816]{1,0:T(8,128)(2,1)} %dynamic-slice_bitcast_fusion), channel_id=1, source_target_pairs={{0,2},{2,4},{4,6},{3,1},{5,3},{7,5},{8,10},{10,12},{12,14},{11,9},... | collective-permute-start | bytes 2162696 | tf_op jit(solution)/shard_map/ppermute | solution.py:276
  76.0 22.5 %all-to-all-start.2 = ((f32[16,40,112]{2,1,0:T(8,128)}), f32[16,40,112]{2,1,0:T(8,128)S(1)}, u32[]{:S(2)}, u32[]{:S(2)}) async-start(f32[16,40,112]{2,1,0:T(8,128)} %get-tuple-element.26), calls=%async_computation.2 | async-start | bytes 655360 | tf_op jit(solution)/shard_map/all_to_all | solution.py:230
  81.4 23.7 %collective-permute-start.2 = (bf16[5,128,112]{2,1,0:T(8,128)(2,1)S(1)}, bf16[5,128,112]{2,1,0:T(8,128)(2,1)S(1)}, u32[]{:S(2)}, u32[]{:S(2)}) collective-permute-start(bf16[5,128,112]{2,1,0:T(8,128)(2,1)S(1)} %get-tuple-element.25), channel_id=1, source_target_pairs={{0,8},{8,0},{1,9},{9,1},{2,10},{10,2},{3,11},{11,3},{4,12},{12,4},... | collective-permute-start | bytes 430088 | tf_op jit(solution)/shard_map/ppermute | solution.py:256
  82.9 0.9 copy-start.2
  91.1 12.8 %copy-start = (bf16[128,2816]{1,0:T(8,128)(2,1)S(1)}, bf16[128,2816]{1,0:T(8,128)(2,1)}, u32[]{:S(2)}) copy-start(bf16[128,2816]{1,0:T(8,128)(2,1)} %shard_map.100) | copy-start | bytes 2162692
  98.5 5.4 %copy-start.1 = (bf16[128,2816]{1,0:T(8,128)(2,1)S(1)}, bf16[128,2816]{1,0:T(8,128)(2,1)}, u32[]{:S(2)}) copy-start(bf16[128,2816]{1,0:T(8,128)(2,1)} %shard_map.101) | copy-start | bytes 2162692
  99.0 6.2 %collective-permute-start.3 = (bf16[2,5,128,112]{3,2,1,0:T(8,128)(2,1)S(1)}, bf16[2,5,128,112]{3,2,1,0:T(8,128)(2,1)S(1)}, u32[]{:S(2)}, u32[]{:S(2)}) collective-permute-start(bf16[2,5,128,112]{3,2,1,0:T(8,128)(2,1)S(1)} %get-tuple-element.28), channel_id=1, source_target_pairs={{0,8},{8,0},{1,9},{9,1},{2,10},{10,2},{3,11},{11,3},{4,12},{12,4},... | collective-permute-start | bytes 860168 | tf_op jit(solution)/shard_map/ppermute | solution.py:265
Sparse Core Ops, SparseCore 0:
  10.1 30.8 all-gather.4
  42.5 26.9 all-gather.6

commit v2 on v1

v2 whole, which is shorter than its diff:
```python
import functools
import math

import jax
import jax.numpy as jnp
from jax import lax
from jax.experimental import pallas as pl
from jax.experimental.pallas import tpu as pltpu
from jax.sharding import Mesh, PartitionSpec as P

HEADS = 10
HD = 112
EPSILON = 1e-06
HALF = HEADS // 2
LANES = 128
CHIPS = ("y", "z", "x")
F32 = jnp.float32
BF16 = jnp.bfloat16

NT = (((1,), (1,)), ((), ()))
TN = (((0,), (0,)), ((), ()))
NN = (((1,), (0,)), ((), ()))


def vmem(n):
    return [pl.BlockSpec(memory_space=pltpu.VMEM)] * n


def call(body, out_shape, args, scratch=(), flops=0):
    size = sum(math.prod(a.shape) * a.dtype.itemsize for a in list(args) + list(out_shape))
    return pl.pallas_call(
        body,
        out_shape=out_shape,
        in_specs=vmem(len(args)),
        out_specs=vmem(len(out_shape)),
        scratch_shapes=list(scratch),
        compiler_params=pltpu.CompilerParams(vmem_limit_bytes=48 * 1024 * 1024),
        cost_estimate=pl.CostEstimate(flops=flops, bytes_accessed=size, transcendentals=0),
    )(*args)


def dot(a, b, dims):
    return lax.dot_general(a, b, dims, preferred_element_type=F32)


def pieces(x):
    hi = x.astype(BF16)
    lo = (x - hi.astype(F32)).astype(BF16)
    return hi, lo


def pieces3(x):
    hi = x.astype(BF16)
    mid, lo = pieces(x - hi.astype(F32))
    return [hi, mid, lo]


def exact_rows(row, mat, dims):
    stack = jnp.concatenate(pieces3(row), axis=0)
    return jnp.sum(dot(stack, mat, dims), axis=0, keepdims=True)


def send_half(a_ref, b_ref, send_ref):
    there = 1 - lax.axis_index("c")
    size = send_ref.shape[1]
    part = pl.ds(pl.multiple_of(there * size, 16), size)
    send_ref[0] = a_ref[part]
    send_ref[1] = b_ref[part]


def merge_half(qm, qt, km, kt, q_ref, k_ref, v_ref):
    core = lax.axis_index("c")
    size = qm.shape[0]
    mine = pl.ds(pl.multiple_of(core * size, 16), size)
    theirs = pl.ds(pl.multiple_of((1 - core) * size, 16), size)
    q_ref[mine] = qm[...]
    q_ref[theirs] = qt[...]
    k_ref[mine] = km[0]
    k_ref[theirs] = kt[0]
    v_ref[mine] = km[1]
    v_ref[theirs] = kt[1]


def head_of(ref, got, i, h):
    start = lax.axis_index("c") * (HALF * HD) + h * HD
    own = ref[pl.ds(pl.multiple_of(start, 16), HD)]
    return jnp.concatenate([own, got[i, h * HD : (h + 1) * HD]], axis=1)


def columns(rows):
    wide = jnp.concatenate([rows, jnp.zeros((HALF, LANES - HD), F32)], axis=1)
    tall = jnp.concatenate([wide, jnp.zeros((8 - HALF, LANES), F32)], axis=0)
    return jnp.transpose(tall)


def spread(row, n):
    return jnp.broadcast_to(row[None], (n, 1, HD))


def sum_of(got, n, first, last):
    total = got[0, first:last]
    for j in range(1, n):
        total = total + got[j, first:last]
    return total


def state_body(n, rows, k_ref, v_ref, kv_got, pay, whole):
    for h in range(HALF):
        key = jnp.maximum(head_of(k_ref, kv_got, 0, h), 0)
        val = head_of(v_ref, kv_got, 1, h)
        whole[h * HD : (h + 1) * HD] = dot(key, val, NT)
        norm = dot(jnp.ones((8, key.shape[1]), BF16), key, NT)[:1]
        pay[:, rows + h : rows + h + 1] = spread(norm, n)
    for j in range(n):
        pay[j, :rows] = whole[j * rows : (j + 1) * rows]


def grad_body(n, rows, scale, got, q_ref, g_ref, qg_got, pay, norm_ref, inv_ref, whole):
    total = sum_of(got, n, 0, rows + HALF)
    norm_ref[...] = total[rows:]
    for h in range(HALF):
        query = jnp.maximum(head_of(q_ref, qg_got, 0, h), 0)
        grad = head_of(g_ref, qg_got, 1, h)
        inv = 1.0 / (exact_rows(total[rows + h : rows + h + 1], query, NN) + EPSILON)
        inv_ref[h : h + 1] = inv
        hi, lo = pieces(grad.astype(F32) * (inv * scale))
        whole[h * HD : (h + 1) * HD] = dot(query, hi, NT) + dot(query, lo, NT)
    shard = total[:rows]
    for j in range(n):
        pay[j, :rows] = shard
        pay[j, rows : 2 * rows] = whole[j * rows : (j + 1) * rows]


def query_body(
    n, rows, scale, got, q_ref, g_ref, qg_got, norm_ref, inv_ref, pay, out_mine, out_theirs, whole
):
    total = sum_of(got, n, rows, 2 * rows)
    for j in range(n):
        whole[j * rows : (j + 1) * rows] = got[j, :rows]
        pay[j, :rows] = total
    norms = columns(norm_ref[...])
    tok = out_mine.shape[1]
    for h in range(HALF):
        part = slice(h * HD, (h + 1) * HD)
        feat = jnp.maximum(head_of(q_ref, qg_got, 0, h), 0)
        query = feat.astype(F32)
        grad = head_of(g_ref, qg_got, 1, h)
        hi, lo = pieces(whole[part])
        prod = dot(hi, grad, NN) + dot(lo, grad, NN)
        inv = inv_ref[h : h + 1]
        weight = inv * scale
        proj = jnp.sum(query * prod, axis=0, keepdims=True) * weight * inv
        pay[:, rows + h : rows + h + 1] = spread(-exact_rows(proj, feat, NT), n)
        out = prod * weight - norms[:HD, h : h + 1] * proj
        out = jnp.where(query > 0, out, 0.0).astype(BF16)
        out_mine[part] = out[:, :tok]
        out_theirs[part] = out[:, tok:]


def key_body(n, rows, got, k_ref, v_ref, kv_got, out_mine, out_theirs, whole):
    for j in range(n):
        whole[j * rows : (j + 1) * rows] = got[j, :rows]
    norms = columns(sum_of(got, n, rows, rows + HALF))
    tok = out_mine.shape[2]
    for h in range(HALF):
        part = slice(h * HD, (h + 1) * HD)
        key = head_of(k_ref, kv_got, 0, h)
        val = head_of(v_ref, kv_got, 1, h)
        hi, lo = pieces(whole[part])
        k_out = dot(hi, val, NN) + dot(lo, val, NN) + norms[:HD, h : h + 1]
        k_out = jnp.where(key.astype(F32) > 0, k_out, 0.0).astype(BF16)
        feat = jnp.maximum(key, 0)
        v_out = (dot(hi, feat, TN) + dot(lo, feat, TN)).astype(BF16)
        out_mine[0, part] = k_out[:, :tok]
        out_theirs[0, part] = k_out[:, tok:]
        out_mine[1, part] = v_out[:, :tok]
        out_theirs[1, part] = v_out[:, tok:]


def shift(x, step):
    rows = lax.broadcasted_iota(jnp.int32, x.shape, 0)
    moved = pltpu.roll(x, step % x.shape[0], 0)
    edge = 0 if step > 0 else x.shape[0] - 1
    return jnp.where(rows == edge, 0.0, moved)


def taps(sources, weight, picks, lanes):
    planes = [ref[:, lanes].astype(F32) for ref in sources]

    def column(j):
        return sum(p * weight[i, pl.ds(j, 1), lanes] for p, i in zip(planes, picks))

    return (column(1) + shift(column(0), -1) + shift(column(2), 1)).astype(BF16)


def halve_body(row, mine, send):
    side = lax.axis_index("x")
    width = mine.shape[1]
    for here in range(2):

        @pl.when(side == here)
        def _():
            mine[...] = row[0, 0, :, here * width : (here + 1) * width]
            send[...] = row[0, 0, :, (1 - here) * width : (2 - here) * width]


def send_body(mine, got, far, weight, out):
    side = lax.axis_index("x")
    width = mine.shape[1]

    @pl.loop(0, width // LANES)
    def _(t):
        lanes = pl.ds(pl.multiple_of(t * LANES, LANES), LANES)
        out[:, lanes] = taps((got, mine, far), weight, (1, 2 - 2 * side, 2 * side), lanes)


def keep_body(mine, got, far, back, weight, out):
    side = lax.axis_index("x")
    width = mine.shape[1]

    @pl.loop(0, width // LANES)
    def _(t):
        at = t * LANES
        lanes = pl.ds(pl.multiple_of(at, LANES), LANES)
        here = pl.ds(pl.multiple_of(side * width + at, LANES), LANES)
        there = pl.ds(pl.multiple_of((1 - side) * width + at, LANES), LANES)
        out[0, 0, :, here] = taps((mine, got, far), weight, (1, 2 * side, 2 - 2 * side), lanes)
        out[0, 0, :, there] = back[:, lanes]


def shards(queries, key_proj, value_proj, attn_grad, conv_grad, conv_weight):
    tok = queries.shape[0] * queries.shape[1] * queries.shape[2]
    tokens_all = tok * lax.axis_size(("y", "c", "z", "x"))
    scale = math.sqrt(tokens_all)
    n = lax.axis_size(CHIPS)
    rows = -(-HALF * HD // n)
    pay_one = -(-(rows + HALF) // 8) * 8
    pay_two = -(-2 * rows // 8) * 8
    swap = [(0, 1), (1, 0)]
    sd = jax.ShapeDtypeStruct
    scratch = [pltpu.VMEM((n * rows, HD), F32)]
    half = HALF * HD
    pair_shape = sd((2, half, tok), BF16)
    q, k, v, g = (
        jnp.swapaxes(a, 2, 3).reshape(2 * half, tok)
        for a in (queries, key_proj, value_proj, attn_grad)
    )

    z_size = lax.axis_size("z")
    ahead = [(z, z + 1) for z in range(z_size - 1)]
    even_up = [(2 * i, 2 * j) for i, j in ahead]
    even_down = [(2 * j, 2 * i) for i, j in ahead]
    odd_up = [(2 * i + 1, 2 * j + 1) for i, j in ahead]
    odd_down = [(2 * j + 1, 2 * i + 1) for i, j in ahead]
    cols, ch = conv_grad.shape[2:]
    width = ch // 2
    half_shape = sd((cols, width), BF16)
    row_mine, row_send = call(halve_body, [half_shape] * 2, (conv_grad,))
    row_got = lax.ppermute(row_send, "x", swap)
    far_own = lax.ppermute(row_mine, ("z", "x"), even_down + odd_up)
    far_fwd = lax.ppermute(row_got, ("z", "x"), even_up + odd_down)
    side = lax.axis_index("x")
    weight = lax.dynamic_slice_in_dim(conv_weight, side * width, width, axis=2)
    (out_send,) = call(
        send_body, [half_shape], (row_mine, row_got, far_own, weight), flops=20 * cols * width
    )
    out_got = lax.ppermute(out_send, "x", swap)
    (input_grad,) = call(
        keep_body,
        [sd(conv_grad.shape, BF16)],
        (row_mine, row_got, far_fwd, out_got, weight),
        flops=20 * cols * width,
    )

    kv_send = call(send_half, [pair_shape], (k, v))[0]
    kv_got = lax.ppermute(kv_send, "c", swap)
    qg_send = call(send_half, [pair_shape], (q, g))[0]
    qg_got = lax.ppermute(qg_send, "c", swap)

    def exchange(pay):
        return lax.all_to_all(pay, CHIPS, split_axis=0, concat_axis=0, tiled=True)

    macs = HALF * 2 * tok * HD * HD
    (pay,) = call(
        functools.partial(state_body, n, rows),
        [sd((n, pay_one, HD), F32)],
        (k, v, kv_got),
        scratch,
        flops=2 * macs,
    )
    got = exchange(pay)
    pay, norm, inv = call(
        functools.partial(grad_body, n, rows, scale),
        [sd((n, pay_two, HD), F32), sd((HALF, HD), F32), sd((HALF, 2 * tok), F32)],
        (got, q, g, qg_got),
        scratch,
        flops=4 * macs,
    )
    got = exchange(pay)
    pay, query_mine, query_send = call(
        functools.partial(query_body, n, rows, scale),
        [sd((n, pay_one, HD), F32)] + [sd((half, tok), BF16)] * 2,
        (got, q, g, qg_got, norm, inv),
        scratch,
        flops=4 * macs,
    )
    query_got = lax.ppermute(query_send, "c", swap)
    got = exchange(pay)
    key_mine, key_send = call(
        functools.partial(key_body, n, rows),
        [pair_shape] * 2,
        (got, k, v, kv_got),
        scratch,
        flops=8 * macs,
    )
    key_got = lax.ppermute(key_send, "c", swap)
    outs = call(
        merge_half,
        [sd((2 * half, tok), BF16)] * 3,
        (query_mine, query_got, key_mine, key_got),
    )
    outs = [jnp.swapaxes(o.reshape(*queries.shape[:2], 2 * half, -1), 2, 3) for o in outs]
    return (*outs, input_grad)


def solution(mesh):
    frames, bands = mesh.shape["frame"], mesh.shape["row"]
    fine = Mesh(mesh.devices.reshape(frames // 2, 2, bands // 2, 2), ("y", "c", "z", "x"))
    split = P(("y", "c"), ("z", "x"), None, None)
    return jax.shard_map(
        shards,
        mesh=fine,
        in_specs=(split,) * 5 + (P(),),
        out_specs=(split,) * 4,
        check_vma=False,
    )
```

time: 116 us -> 87.8 us (0.76)
  the two profiles are of different devices: /device:TPU:17 before, /device:TPU:18 now
where the time goes in v2:
time: 87.8 us; the launch traced here: 87.2 us
  waiting for transfers between devices  39.3 us (45%)
  starting transfers between devices  27.9 us (32%)
  Pallas kernels  13.7 us (16%)
  local copies, waits for them, and re-layouts  5.43 us (6%)
    all_to_all x3, starting transfers between devices, exchange(): return lax.all_to_all(pay, CHIPS, split_axis=0, concat_axis=0, tiled=True)  20.6 us
    all_to_all x3, waiting for transfers between devices, exchange(): return lax.all_to_all(pay, CHIPS, split_axis=0, concat_axis=0, tiled=True)  13.9 us
    pallas_call x10, Pallas kernels, call(): pl.pallas_call(body, out_shape=out_shape, in_specs=vmem(len(args)), out_s...  13.7 us
    ppermute x1, waiting for transfers between devices, shards(): out_got = lax.ppermute(out_send, 'x', swap)  8.36 us
    ppermute x1, waiting for transfers between devices, shards(): far_fwd = lax.ppermute(row_got, ('z', 'x'), even_up + odd_down)  7.6 us
    ppermute x1, waiting for transfers between devices, shards(): far_own = lax.ppermute(row_mine, ('z', 'x'), even_down + odd_up)  5.85 us
    unnamed x26, local copies, waits for them, and re-layouts  5.4 us
    ppermute x1, starting transfers between devices, shards(): far_own = lax.ppermute(row_mine, ('z', 'x'), even_down + odd_up)  3.37 us
  transfers between devices with their start and end apart: 11, of which 8 were waited for; matrix products, arithmetic and copies ran while one was open for 0% of the time, Pallas kernels for 11%

profile of v2, /device:TPU:18, one launch (start us, length us, event | category | flops | bytes accessed | tf_op | source)
XLA Modules:
  0.0 87.2 jit_solution(7020138841141257319)
XLA Ops:
  0.6 0.0 copy-start
  0.6 0.0 copy-start.1
  0.7 1.0 %copy-done.1 = bf16[1,1,128,1120]{2,3,1,0:T(8,128)(2,1)S(1)} copy-done((bf16[1,1,128,1120]{2,3,1,0:T(8,128)(2,1)S(1)}, bf16[1,1,128,1120]{2,3,1,0:T(8,128)(2,1)}, u32[]{:S(2)}) %copy-start.1) | copy-done | bytes 286744
  1.7 1.0 %copy-done.3 = bf16[1,1,128,1120]{2,3,1,0:T(8,128)(2,1)S(1)} copy-done((bf16[1,1,128,1120]{2,3,1,0:T(8,128)(2,1)S(1)}, bf16[1,1,128,1120]{2,3,1,0:T(8,128)(2,1)}, u32[]{:S(2)}) %copy-start.3) | copy-done | bytes 286744
  2.6 0.1 collective-permute-start
  2.7 1.6 %collective-permute-done.kv_got = bf16[2,560,128]{2,1,0:T(8,128)(2,1)S(1)} collective-permute-done((bf16[2,560,128]{2,1,0:T(8,128)(2,1)S(1)}, bf16[2,560,128]{2,1,0:T(8,128)(2,1)S(1)}, u32[]{:S(2)}, u32[]{:S(2)}) %collective-permute-start) | collective-permute-done | bytes 286752 | tf_op jit(solution)/shard_map/ppermute | solution.py:276
  4.3 1.1 %shard_map.94 = f32[16,40,112]{2,1,0:T(8,128)} custom-call(bf16[1120,128]{1,0:T(8,128)(2,1)S(1)} %bitcast.22, bf16[1120,128]{1,0:T(8,128)(2,1)S(1)} %bitcast.25, bf16[2,560,128]{2,1,0:T(8,128)(2,1)S(1)} %collective-permute-done.kv_got), custom_call_target="tpu_custom_call" | custom-call | flops 32112640 | bytes 1146880 | tf_op jit(solution)/shard_map/pallas_call | solution.py:31
  5.4 7.1 %all-to-all-start = ((f32[16,40,112]{2,1,0:T(8,128)}), f32[16,40,112]{2,1,0:T(8,128)S(1)}, u32[]{:S(2)}, u32[]{:S(2)}) async-start(f32[16,40,112]{2,1,0:T(8,128)} %shard_map.94), calls=%async_computation | async-start | bytes 655360 | tf_op jit(solution)/shard_map/all_to_all | solution.py:281
  12.4 0.0 copy-done.5
  12.5 0.0 copy-done.6
  12.5 0.1 collective-permute-start.1
  12.6 1.6 %collective-permute-done.1.qg_got = bf16[2,560,128]{2,1,0:T(8,128)(2,1)S(1)} collective-permute-done((bf16[2,560,128]{2,1,0:T(8,128)(2,1)S(1)}, bf16[2,560,128]{2,1,0:T(8,128)(2,1)S(1)}, u32[]{:S(2)}, u32[]{:S(2)}) %collective-permute-start.1) | collective-permute-done | bytes 286752 | tf_op jit(solution)/shard_map/ppermute | solution.py:278
  14.1 6.8 %all-to-all-done.got = f32[16,40,112]{2,1,0:T(8,128)S(1)} async-done(((f32[16,40,112]{2,1,0:T(8,128)}), f32[16,40,112]{2,1,0:T(8,128)S(1)}, u32[]{:S(2)}, u32[]{:S(2)}) %all-to-all-start) | async-done | bytes 286752 | tf_op jit(solution)/shard_map/all_to_all | solution.py:281
  20.9 1.7 %shard_map.96 = (f32[16,72,112]{2,1,0:T(8,128)}, f32[5,112]{1,0:T(8,128)S(1)}, f32[5,256]{1,0:T(8,128)S(1)}) custom-call(f32[16,40,112]{2,1,0:T(8,128)S(1)} %all-to-all-done.got, bf16[1120,128]{1,0:T(8,128)(2,1)S(1)} %bitcast.28, bf16[1120,128]{1,0:T(8,128)(2,1)S(1)} %bitcast.31, bf16[2,560,128]{2,1,0:T(8,128)(2,1)S(1)} %collective-permute-done.1.qg_got), custom_call_target="tpu_custom_call" | custom-call | flops 64225280 | bytes 1670336 | tf_op jit(solution)/shard_map/pallas_call | solution.py:31
  22.7 6.6 %all-to-all-start.1 = ((f32[16,72,112]{2,1,0:T(8,128)}), f32[16,72,112]{2,1,0:T(8,128)S(1)}, u32[]{:S(2)}, u32[]{:S(2)}) async-start(f32[16,72,112]{2,1,0:T(8,128)} %get-tuple-element.17), calls=%async_computation.1 | async-start | bytes 1179648 | tf_op jit(solution)/shard_map/all_to_all | solution.py:281
  29.3 1.4 %copy-done.7 = bf16[1,1,128,5632]{3,2,1,0:T(8,128)(2,1)S(1)} copy-done((bf16[1,1,128,5632]{3,2,1,0:T(8,128)(2,1)S(1)}, bf16[1,1,128,5632]{3,2,1,0:T(8,128)(2,1)}, u32[]{:S(2)}) %copy-start.7) | copy-done | bytes 1441816
  30.7 1.0 %shard_map.100 = (bf16[128,2816]{1,0:T(8,128)(2,1)S(1)}, bf16[128,2816]{1,0:T(8,128)(2,1)}) custom-call(bf16[1,1,128,5632]{3,2,1,0:T(8,128)(2,1)S(1)} %copy-done.7), custom_call_target="tpu_custom_call" | custom-call | bytes 2883584 | tf_op jit(solution)/shard_map/pallas_call | solution.py:31
  31.6 0.6 collective-permute-start.4
  32.2 3.4 %collective-permute-start.6 = (bf16[128,2816]{1,0:T(8,128)(2,1)S(1)}, bf16[128,2816]{1,0:T(8,128)(2,1)}, u32[]{:S(2)}, u32[]{:S(2)}) collective-permute-start(bf16[128,2816]{1,0:T(8,128)(2,1)S(1)} %get-tuple-element.28.mine), channel_id=1, source_target_pairs={{2,0},{4,2},{6,4},{1,3},{3,5},{5,7},{10,8},{12,10},{14,12},{9,11},... | collective-permute-start | bytes 2162696 | tf_op jit(solution)/shard_map/ppermute | solution.py:260
  35.6 7.2 %all-to-all-done.1.got = f32[16,72,112]{2,1,0:T(8,128)S(1)} async-done(((f32[16,72,112]{2,1,0:T(8,128)}), f32[16,72,112]{2,1,0:T(8,128)S(1)}, u32[]{:S(2)}, u32[]{:S(2)}) %all-to-all-start.1) | async-done | bytes 516128 | tf_op jit(solution)/shard_map/all_to_all | solution.py:281
  42.7 1.3 %shard_map.97 = (f32[16,40,112]{2,1,0:T(8,128)S(1)}, bf16[560,128]{1,0:T(8,128)(2,1)S(1)}, bf16[560,128]{1,0:T(8,128)(2,1)S(1)}) custom-call(f32[16,72,112]{2,1,0:T(8,128)S(1)} %all-to-all-done.1.got, bf16[1120,128]{1,0:T(8,128)(2,1)S(1)} %bitcast.29, bf16[1120,128]{1,0:T(8,128)(2,1)S(1)} %bitcast.32, ...), custom_call_target="tpu_custom_call" | custom-call | flops 64225280 | bytes 1957056 | tf_op jit(solution)/shard_map/pallas_call | solution.py:31
  44.0 0.0 copy-start.8
  44.0 0.7 copy-done.8
  44.7 0.7 copy-done.9
  45.4 0.7 copy-done.11
  46.0 6.9 %all-to-all-start.2 = ((f32[16,40,112]{2,1,0:T(8,128)}), f32[16,40,112]{2,1,0:T(8,128)S(1)}, u32[]{:S(2)}, u32[]{:S(2)}) async-start(f32[16,40,112]{2,1,0:T(8,128)} %copy-done.8), calls=%async_computation.2 | async-start | bytes 655360 | tf_op jit(solution)/shard_map/all_to_all | solution.py:281
  52.9 0.0 copy-done
  52.9 0.0 copy-start.2
  52.9 0.0 copy-start.4
  53.0 0.0 copy-start.12
  53.0 0.5 collective-permute-done.4.got
  53.5 2.5 %collective-permute-start.5 = (bf16[128,2816]{1,0:T(8,128)(2,1)S(1)}, bf16[128,2816]{1,0:T(8,128)(2,1)}, u32[]{:S(2)}, u32[]{:S(2)}) collective-permute-start(bf16[128,2816]{1,0:T(8,128)(2,1)S(1)} %collective-permute-done.4.got), channel_id=1, source_target_pairs={{0,2},{2,4},{4,6},{3,1},{5,3},{7,5},{8,10},{10,12},{12,14},{11,9},... | collective-permute-start | bytes 2162696 | tf_op jit(solution)/shard_map/ppermute | solution.py:261
  55.9 5.8 %collective-permute-done.6.far = bf16[128,2816]{1,0:T(8,128)(2,1)} collective-permute-done((bf16[128,2816]{1,0:T(8,128)(2,1)S(1)}, bf16[128,2816]{1,0:T(8,128)(2,1)}, u32[]{:S(2)}, u32[]{:S(2)}) %collective-permute-start.6) | collective-permute-done | bytes 720928 | tf_op jit(solution)/shard_map/ppermute | solution.py:260
  61.8 3.3 %shard_map.101 = bf16[128,2816]{1,0:T(8,128)(2,1)} custom-call(bf16[128,2816]{1,0:T(8,128)(2,1)S(1)} %get-tuple-element.28.mine, bf16[128,2816]{1,0:T(8,128)(2,1)S(1)} %collective-permute-done.4.got, bf16[128,2816]{1,0:T(8,128)(2,1)} %collective-permute-done.6.far, f32[3,3,2816]{2,1,0:T(4,128)S(1)} %constant_dynamic-slice_fusion.weight), custom_call_target="tpu_custom_call" | custom-call | flops 7208960 | bytes 2984960 | tf_op jit(solution)/shard_map/pallas_call | solution.py:31
  65.1 0.3 collective-permute-start.7
  65.3 0.0 all-to-all-done.2.got
  65.3 0.0 copy-done.2
  65.3 0.0 copy-done.4
  65.3 0.5 shard_map.98
  65.9 0.1 collective-permute-start.3
  65.9 0.0 copy-start.10
  66.0 0.5 collective-permute-start.2
  66.4 7.6 %collective-permute-done.5.far = bf16[128,2816]{1,0:T(8,128)(2,1)} collective-permute-done((bf16[128,2816]{1,0:T(8,128)(2,1)S(1)}, bf16[128,2816]{1,0:T(8,128)(2,1)}, u32[]{:S(2)}, u32[]{:S(2)}) %collective-permute-start.5) | collective-permute-done | bytes 720928 | tf_op jit(solution)/shard_map/ppermute | solution.py:261
  74.0 8.4 %collective-permute-done.7.back = bf16[128,2816]{1,0:T(8,128)(2,1)} collective-permute-done((bf16[128,2816]{1,0:T(8,128)(2,1)}, bf16[128,2816]{1,0:T(8,128)(2,1)}, u32[]{:S(2)}, u32[]{:S(2)}) %collective-permute-start.7) | collective-permute-done | bytes 720928 | tf_op jit(solution)/shard_map/ppermute | solution.py:267
  82.4 3.8 %shard_map.102 = bf16[1,1,128,5632]{3,2,1,0:T(8,128)(2,1)} custom-call(bf16[128,2816]{1,0:T(8,128)(2,1)S(1)} %get-tuple-element.28.mine, bf16[128,2816]{1,0:T(8,128)(2,1)S(1)} %collective-permute-done.4.got, bf16[128,2816]{1,0:T(8,128)(2,1)} %collective-permute-done.5.far, bf16[128,2816]{1,0:T(8,128)(2,1)} %collective-permute-done.7.back, ...), custom_call_target="tpu_custom_call" | custom-call | flops 7208960 | bytes 4426752 | tf_op jit(solution)/shard_map/pallas_call | solution.py:31
  86.2 0.0 collective-permute-done.2.qt
  86.2 0.0 collective-permute-done.3.kt
  86.2 1.0 %shard_map.99 = (bf16[1120,128]{1,0:T(8,128)(2,1)}, bf16[1120,128]{1,0:T(8,128)(2,1)}, bf16[1120,128]{1,0:T(8,128)(2,1)}) custom-call(bf16[560,128]{1,0:T(8,128)(2,1)S(1)} %copy-done.10, bf16[560,128]{1,0:T(8,128)(2,1)S(1)} %collective-permute-done.2.qt, bf16[2,560,128]{2,1,0:T(8,128)(2,1)S(1)} %get-tuple-element.23.km, ...), custom_call_target="tpu_custom_call" | custom-call | bytes 1720320 | tf_op jit(solution)/shard_map/pallas_call | solution.py:31
  (11 shorter events, 0.1 us)
Async XLA Ops:
  0.6 52.3 %copy-start = (f32[3,3,5632]{2,1,0:T(4,128)S(1)}, f32[3,3,5632]{2,1,0:T(4,128)}, u32[]{:S(2)}) copy-start(f32[3,3,5632]{2,1,0:T(4,128)} %param.11) | copy-start | bytes 608260
  0.6 1.0 %copy-start.1 = (bf16[1,1,128,1120]{2,3,1,0:T(8,128)(2,1)S(1)}, bf16[1,1,128,1120]{2,3,1,0:T(8,128)(2,1)}, u32[]{:S(2)}) copy-start(bf16[1,1,128,1120]{2,3,1,0:T(8,128)(2,1)} %param.7) | copy-start | bytes 860164
  1.6 1.0 %copy-start.3 = (bf16[1,1,128,1120]{2,3,1,0:T(8,128)(2,1)S(1)}, bf16[1,1,128,1120]{2,3,1,0:T(8,128)(2,1)}, u32[]{:S(2)}) copy-start(bf16[1,1,128,1120]{2,3,1,0:T(8,128)(2,1)} %param.8) | copy-start | bytes 860164
  2.6 9.8 %copy-start.5 = (bf16[1,1,128,1120]{2,3,1,0:T(8,128)(2,1)S(1)}, bf16[1,1,128,1120]{2,3,1,0:T(8,128)(2,1)}, u32[]{:S(2)}) copy-start(bf16[1,1,128,1120]{2,3,1,0:T(8,128)(2,1)} %param.6) | copy-start | bytes 860164
  2.6 9.8 %copy-start.6 = (bf16[1,1,128,1120]{2,3,1,0:T(8,128)(2,1)S(1)}, bf16[1,1,128,1120]{2,3,1,0:T(8,128)(2,1)}, u32[]{:S(2)}) copy-start(bf16[1,1,128,1120]{2,3,1,0:T(8,128)(2,1)} %param.9) | copy-start | bytes 860164
  2.6 1.6 %collective-permute-start = (bf16[2,560,128]{2,1,0:T(8,128)(2,1)S(1)}, bf16[2,560,128]{2,1,0:T(8,128)(2,1)S(1)}, u32[]{:S(2)}, u32[]{:S(2)}) collective-permute-start(bf16[2,560,128]{2,1,0:T(8,128)(2,1)S(1)} %shard_map.93), channel_id=1, source_target_pairs={{0,8},{8,0},{1,9},{9,1},{2,10},{10,2},{3,11},{11,3},{4,12},{12,4},... | collective-permute-start | bytes 860168 | tf_op jit(solution)/shard_map/ppermute | solution.py:276
  5.4 15.6 %all-to-all-start = ((f32[16,40,112]{2,1,0:T(8,128)}), f32[16,40,112]{2,1,0:T(8,128)S(1)}, u32[]{:S(2)}, u32[]{:S(2)}) async-start(f32[16,40,112]{2,1,0:T(8,128)} %shard_map.94), calls=%async_computation | async-start | bytes 655360 | tf_op jit(solution)/shard_map/all_to_all | solution.py:281
  12.5 1.6 %collective-permute-start.1 = (bf16[2,560,128]{2,1,0:T(8,128)(2,1)S(1)}, bf16[2,560,128]{2,1,0:T(8,128)(2,1)S(1)}, u32[]{:S(2)}, u32[]{:S(2)}) collective-permute-start(bf16[2,560,128]{2,1,0:T(8,128)(2,1)S(1)} %shard_map.95), channel_id=1, source_target_pairs={{0,8},{8,0},{1,9},{9,1},{2,10},{10,2},{3,11},{11,3},{4,12},{12,4},... | collective-permute-start | bytes 860168 | tf_op jit(solution)/shard_map/ppermute | solution.py:278
  22.7 20.1 %all-to-all-start.1 = ((f32[16,72,112]{2,1,0:T(8,128)}), f32[16,72,112]{2,1,0:T(8,128)S(1)}, u32[]{:S(2)}, u32[]{:S(2)}) async-start(f32[16,72,112]{2,1,0:T(8,128)} %get-tuple-element.17), calls=%async_computation.1 | async-start | bytes 1179648 | tf_op jit(solution)/shard_map/all_to_all | solution.py:281
  29.3 1.4 %copy-start.7 = (bf16[1,1,128,5632]{3,2,1,0:T(8,128)(2,1)S(1)}, bf16[1,1,128,5632]{3,2,1,0:T(8,128)(2,1)}, u32[]{:S(2)}) copy-start(bf16[1,1,128,5632]{3,2,1,0:T(8,128)(2,1)} %row.1) | copy-start | bytes 4325380
  31.6 21.8 %collective-permute-start.4 = (bf16[128,2816]{1,0:T(8,128)(2,1)}, bf16[128,2816]{1,0:T(8,128)(2,1)S(1)}, u32[]{:S(2)}, u32[]{:S(2)}) collective-permute-start(bf16[128,2816]{1,0:T(8,128)(2,1)} %get-tuple-element.29), channel_id=1, source_target_pairs={{0,1},{1,0},{2,3},{3,2},{4,5},{5,4},{6,7},{7,6},{8,9},{9,8},{10,11... | collective-permute-start | bytes 2162696 | tf_op jit(solution)/shard_map/ppermute | solution.py:259
  32.2 29.6 %collective-permute-start.6 = (bf16[128,2816]{1,0:T(8,128)(2,1)S(1)}, bf16[128,2816]{1,0:T(8,128)(2,1)}, u32[]{:S(2)}, u32[]{:S(2)}) collective-permute-start(bf16[128,2816]{1,0:T(8,128)(2,1)S(1)} %get-tuple-element.28.mine), channel_id=1, source_target_pairs={{2,0},{4,2},{6,4},{1,3},{3,5},{5,7},{10,8},{12,10},{14,12},{9,11},... | collective-permute-start | bytes 2162696 | tf_op jit(solution)/shard_map/ppermute | solution.py:260
  44.0 0.7 copy-start.8
  44.7 0.7 copy-start.9
  45.4 0.7 copy-start.11
  46.0 19.3 %all-to-all-start.2 = ((f32[16,40,112]{2,1,0:T(8,128)}), f32[16,40,112]{2,1,0:T(8,128)S(1)}, u32[]{:S(2)}, u32[]{:S(2)}) async-start(f32[16,40,112]{2,1,0:T(8,128)} %copy-done.8), calls=%async_computation.2 | async-start | bytes 655360 | tf_op jit(solution)/shard_map/all_to_all | solution.py:281
  52.9 12.4 %copy-start.2 = (bf16[1,1,128,1120]{2,3,1,0:T(8,128)(2,1)S(1)}, bf16[1,1,128,1120]{2,3,1,0:T(8,128)(2,1)}, u32[]{:S(2)}) copy-start(bf16[1,1,128,1120]{2,3,1,0:T(8,128)(2,1)} %param.7) | copy-start | bytes 860164
  52.9 12.4 %copy-start.4 = (bf16[1,1,128,1120]{2,3,1,0:T(8,128)(2,1)S(1)}, bf16[1,1,128,1120]{2,3,1,0:T(8,128)(2,1)}, u32[]{:S(2)}) copy-start(bf16[1,1,128,1120]{2,3,1,0:T(8,128)(2,1)} %param.8) | copy-start | bytes 860164
  53.0 13.0 %copy-start.12 = (bf16[560,128]{1,0:T(8,128)(2,1)S(1)}, bf16[560,128]{1,0:T(8,128)(2,1)}, u32[]{:S(2)}) copy-start(bf16[560,128]{1,0:T(8,128)(2,1)} %copy-done.11) | copy-start | bytes 430084
  53.5 20.6 %collective-permute-start.5 = (bf16[128,2816]{1,0:T(8,128)(2,1)S(1)}, bf16[128,2816]{1,0:T(8,128)(2,1)}, u32[]{:S(2)}, u32[]{:S(2)}) collective-permute-start(bf16[128,2816]{1,0:T(8,128)(2,1)S(1)} %collective-permute-done.4.got), channel_id=1, source_target_pairs={{0,2},{2,4},{4,6},{3,1},{5,3},{7,5},{8,10},{10,12},{12,14},{11,9},... | collective-permute-start | bytes 2162696 | tf_op jit(solution)/shard_map/ppermute | solution.py:261
  65.1 17.3 %collective-permute-start.7 = (bf16[128,2816]{1,0:T(8,128)(2,1)}, bf16[128,2816]{1,0:T(8,128)(2,1)}, u32[]{:S(2)}, u32[]{:S(2)}) collective-permute-start(bf16[128,2816]{1,0:T(8,128)(2,1)} %shard_map.101), channel_id=1, source_target_pairs={{0,1},{1,0},{2,3},{3,2},{4,5},{5,4},{6,7},{7,6},{8,9},{9,8},{10,11... | collective-permute-start | bytes 2162696 | tf_op jit(solution)/shard_map/ppermute | solution.py:267
  65.9 20.4 %collective-permute-start.3 = (bf16[2,560,128]{2,1,0:T(8,128)(2,1)S(1)}, bf16[2,560,128]{2,1,0:T(8,128)(2,1)S(1)}, u32[]{:S(2)}, u32[]{:S(2)}) collective-permute-start(bf16[2,560,128]{2,1,0:T(8,128)(2,1)S(1)} %get-tuple-element.24), channel_id=1, source_target_pairs={{0,8},{8,0},{1,9},{9,1},{2,10},{10,2},{3,11},{11,3},{4,12},{12,4},... | collective-permute-start | bytes 860168 | tf_op jit(solution)/shard_map/ppermute | solution.py:316
  65.9 20.3 %copy-start.10 = (bf16[560,128]{1,0:T(8,128)(2,1)S(1)}, bf16[560,128]{1,0:T(8,128)(2,1)}, u32[]{:S(2)}) copy-start(bf16[560,128]{1,0:T(8,128)(2,1)} %copy-done.9) | copy-start | bytes 430084
  66.0 20.3 %collective-permute-start.2 = (bf16[560,128]{1,0:T(8,128)(2,1)S(1)}, bf16[560,128]{1,0:T(8,128)(2,1)S(1)}, u32[]{:S(2)}, u32[]{:S(2)}) collective-permute-start(bf16[560,128]{1,0:T(8,128)(2,1)S(1)} %copy-done.12), channel_id=1, source_target_pairs={{0,8},{8,0},{1,9},{9,1},{2,10},{10,2},{3,11},{11,3},{4,12},{12,4},... | collective-permute-start | bytes 430088 | tf_op jit(solution)/shard_map/ppermute | solution.py:307

commit v3 on v2

--- a/solution.py
+++ b/solution.py
@@ -22,21 +22,51 @@
 NN = (((1,), (0,)), ((), ()))
 
 
-def vmem(n):
-    return [pl.BlockSpec(memory_space=pltpu.VMEM)] * n
-
-
-def call(body, out_shape, args, scratch=(), flops=0):
-    size = sum(math.prod(a.shape) * a.dtype.itemsize for a in list(args) + list(out_shape))
+def held_in_hbm(x):
+    return pltpu.with_memory_space_constraint(x, pltpu.HBM)
+
+
+def call(body, outs, args, scratch=(), flops=0, after=(), hbm_in=False, hbm_out=False, pinned=False):
+    size = sum(math.prod(a.shape) * a.dtype.itemsize for a in list(args) + list(outs))
+    fast = pl.BlockSpec(memory_space=pltpu.VMEM)
+    slow = pl.BlockSpec(memory_space=pltpu.HBM)
+    scratch = list(scratch)
+    if pinned:
+        scratch += [pltpu.VMEM(outs[0].shape, outs[0].dtype), pltpu.SemaphoreType.DMA((1,))]
+
+    def ordered(*refs):
+        ins = refs[: len(args)]
+        made = refs[len(args) + len(after) :][: len(outs)]
+        held = refs[len(args) + len(after) + len(outs) :]
+        if not pinned:
+            body(*ins, *made, *held)
+            return
+        first, sem = held[-2:]
+        body(*ins, first, *made[1:], *held[:-2])
+        copy_all([(first, made[0])], sem)
+
+    out_specs = [slow if hbm_out or (pinned and i == 0) else fast for i in range(len(outs))]
+    shapes = [
+        pltpu.HBM(o.shape, o.dtype) if hbm_out or (pinned and i == 0) else o
+        for i, o in enumerate(outs)
+    ]
     return pl.pallas_call(
-        body,
-        out_shape=out_shape,
-        in_specs=vmem(len(args)),
-        out_specs=vmem(len(out_shape)),
-        scratch_shapes=list(scratch),
-        compiler_params=pltpu.CompilerParams(vmem_limit_bytes=48 * 1024 * 1024),
+        ordered,
+        out_shape=shapes,
+        in_specs=[slow if hbm_in else fast] * len(args) + [pl.BlockSpec(memory_space=pl.ANY)] * len(after),
+        out_specs=out_specs,
+        scratch_shapes=scratch,
+        compiler_params=pltpu.CompilerParams(vmem_limit_bytes=16 * 1024 * 1024),
         cost_estimate=pl.CostEstimate(flops=flops, bytes_accessed=size, transcendentals=0),
-    )(*args)
+    )(*[held_in_hbm(a) if hbm_in else a for a in args], *after)
+
+
+def copy_all(pairs, sems):
+    copies = [pltpu.make_async_copy(a, b, sems.at[i]) for i, (a, b) in enumerate(pairs)]
+    for c in copies:
+        c.start()
+    for c in copies:
+        c.wait()
 
 
 def dot(a, b, dims):
@@ -60,12 +90,11 @@
     return jnp.sum(dot(stack, mat, dims), axis=0, keepdims=True)
 
 
-def send_half(a_ref, b_ref, send_ref):
+def send_half(a_ref, b_ref, send_ref, sems):
     there = 1 - lax.axis_index("c")
     size = send_ref.shape[1]
     part = pl.ds(pl.multiple_of(there * size, 16), size)
-    send_ref[0] = a_ref[part]
-    send_ref[1] = b_ref[part]
+    copy_all([(a_ref.at[part], send_ref.at[0]), (b_ref.at[part], send_ref.at[1])], sems)
 
 
 def merge_half(qm, qt, km, kt, q_ref, k_ref, v_ref):
@@ -193,18 +222,21 @@
     return (column(1) + shift(column(0), -1) + shift(column(2), 1)).astype(BF16)
 
 
-def halve_body(row, mine, send):
+def halve_body(row, weight, mine, send, weight_mine, sems):
     side = lax.axis_index("x")
     width = mine.shape[1]
-    for here in range(2):
-
-        @pl.when(side == here)
-        def _():
-            mine[...] = row[0, 0, :, here * width : (here + 1) * width]
-            send[...] = row[0, 0, :, (1 - here) * width : (2 - here) * width]
-
-
-def send_body(mine, got, far, weight, out):
+    here = pl.ds(pl.multiple_of(side * width, LANES), width)
+    there = pl.ds(pl.multiple_of((1 - side) * width, LANES), width)
+    pairs = [
+        (row.at[0, 0, :, there], send),
+        (row.at[0, 0, :, here], mine),
+        (weight.at[:, :, here], weight_mine),
+    ]
+    copy_all(pairs, sems)
+
+
+def send_body(mine, got, far, weight, out, token):
+    token[...] = jnp.zeros(token.shape, F32)
     side = lax.axis_index("x")
     width = mine.shape[1]
 
@@ -214,7 +246,8 @@
         out[:, lanes] = taps((got, mine, far), weight, (1, 2 - 2 * side, 2 * side), lanes)
 
 
-def keep_body(mine, got, far, back, weight, out):
+def keep_body(mine, got, far, back, weight, out, token):
+    token[...] = jnp.zeros(token.shape, F32)
     side = lax.axis_index("x")
     width = mine.shape[1]
 
@@ -237,6 +270,7 @@
     pay_one = -(-(rows + HALF) // 8) * 8
     pay_two = -(-2 * rows // 8) * 8
     swap = [(0, 1), (1, 0)]
+    two_sems = [pltpu.SemaphoreType.DMA((2,))]
     sd = jax.ShapeDtypeStruct
     scratch = [pltpu.VMEM((n * rows, HD), F32)]
     half = HALF * HD
@@ -255,26 +289,35 @@
     cols, ch = conv_grad.shape[2:]
     width = ch // 2
     half_shape = sd((cols, width), BF16)
-    row_mine, row_send = call(halve_body, [half_shape] * 2, (conv_grad,))
+    token = sd((8, LANES), F32)
+    row_mine, row_send, weight = call(
+        halve_body,
+        [half_shape, half_shape, sd((3, 3, width), F32)],
+        (conv_grad, conv_weight),
+        [pltpu.SemaphoreType.DMA((3,))],
+        hbm_in=True,
+        hbm_out=True,
+    )
     row_got = lax.ppermute(row_send, "x", swap)
     far_own = lax.ppermute(row_mine, ("z", "x"), even_down + odd_up)
     far_fwd = lax.ppermute(row_got, ("z", "x"), even_up + odd_down)
-    side = lax.axis_index("x")
-    weight = lax.dynamic_slice_in_dim(conv_weight, side * width, width, axis=2)
-    (out_send,) = call(
-        send_body, [half_shape], (row_mine, row_got, far_own, weight), flops=20 * cols * width
+    out_send, sent = call(
+        send_body,
+        [half_shape, token],
+        (row_mine, row_got, far_own, weight),
+        flops=20 * cols * width,
     )
     out_got = lax.ppermute(out_send, "x", swap)
-    (input_grad,) = call(
+    input_grad, kept = call(
         keep_body,
-        [sd(conv_grad.shape, BF16)],
+        [sd(conv_grad.shape, BF16), token],
         (row_mine, row_got, far_fwd, out_got, weight),
         flops=20 * cols * width,
     )
 
-    kv_send = call(send_half, [pair_shape], (k, v))[0]
+    kv_send = call(send_half, [pair_shape], (k, v), two_sems, hbm_in=True, hbm_out=True)[0]
     kv_got = lax.ppermute(kv_send, "c", swap)
-    qg_send = call(send_half, [pair_shape], (q, g))[0]
+    qg_send = call(send_half, [pair_shape], (q, g), two_sems, hbm_in=True, hbm_out=True)[0]
     qg_got = lax.ppermute(qg_send, "c", swap)
 
     def exchange(pay):
@@ -287,6 +330,7 @@
         (k, v, kv_got),
         scratch,
         flops=2 * macs,
+        pinned=True,
     )
     got = exchange(pay)
     pay, norm, inv = call(
@@ -295,6 +339,8 @@
         (got, q, g, qg_got),
         scratch,
         flops=4 * macs,
+        pinned=True,
+        after=(row_got, far_own),
     )
     got = exchange(pay)
     pay, query_mine, query_send = call(
@@ -303,6 +349,8 @@
         (got, q, g, qg_got, norm, inv),
         scratch,
         flops=4 * macs,
+        pinned=True,
+        after=(sent,),
     )
     query_got = lax.ppermute(query_send, "c", swap)
     got = exchange(pay)
@@ -312,6 +360,7 @@
         (got, k, v, kv_got),
         scratch,
         flops=8 * macs,
+        after=(kept,),
     )
     key_got = lax.ppermute(key_send, "c", swap)
     outs = call(

time: 87.8 us -> 142 us (1.62)
  the two profiles are of different devices: /device:TPU:18 before, /device:TPU:0 now
where the time goes in v3:
time: 142 us; the launch traced here: 141 us
  Pallas kernels  82.9 us (58%)
  waiting for transfers between devices  29.3 us (21%)
  starting transfers between devices  24.9 us (18%)
  local copies, waits for them, and re-layouts  3.37 us (2%)
    pallas_call x10, Pallas kernels, call(): pl.pallas_call(ordered, out_shape=shapes, in_specs=[slow if hbm_in else f...  82.9 us
    all_to_all x3, waiting for transfers between devices, exchange(): return lax.all_to_all(pay, CHIPS, split_axis=0, concat_axis=0, tiled=True)  23.2 us
    all_to_all x3, starting transfers between devices, exchange(): return lax.all_to_all(pay, CHIPS, split_axis=0, concat_axis=0, tiled=True)  15.2 us
    ppermute x1, starting transfers between devices, shards(): far_fwd = lax.ppermute(row_got, ('z', 'x'), even_up + odd_down)  4.65 us
    unnamed x22, local copies, waits for them, and re-layouts  3.37 us
  transfers between devices with their start and end apart: 11, of which 7 were waited for; matrix products, arithmetic and copies ran while one was open for 0% of the time, Pallas kernels for 49%

profile of v3, /device:TPU:0, one launch (start us, length us, event | category | flops | bytes accessed | tf_op | source)
XLA Modules:
  0.0 141.3 jit_solution(15927977821140789691)
XLA Ops:
  0.6 0.0 copy-start.4
  0.6 0.0 copy-start.3
  0.7 9.8 %shard_map.93 = bf16[2,560,128]{2,1,0:T(8,128)(2,1)} custom-call(bf16[1120,128]{1,0:T(8,128)(2,1)} %bitcast.27, bf16[1120,128]{1,0:T(8,128)(2,1)} %bitcast.30), custom_call_target="tpu_custom_call" | custom-call | bytes 860160 | tf_op jit(solution)/shard_map/pallas_call | solution.py:53
  10.5 0.5 collective-permute-start
  11.0 48.9 %shard_map.96 = (bf16[128,2816]{1,0:T(8,128)(2,1)}, bf16[128,2816]{1,0:T(8,128)(2,1)}, f32[3,3,2816]{2,1,0:T(4,128)}) custom-call(bf16[1,1,128,5632]{3,2,1,0:T(8,128)(2,1)} %refs_0_.1, f32[3,3,5632]{2,1,0:T(4,128)} %refs_1_.1), custom_call_target="tpu_custom_call" | custom-call | bytes 3187712 | tf_op jit(solution)/shard_map/pallas_call | solution.py:53
  59.9 0.0 copy-start.1
  59.9 0.0 copy-start.2
  59.9 2.6 %collective-permute-start.2 = (bf16[128,2816]{1,0:T(8,128)(2,1)}, bf16[128,2816]{1,0:T(8,128)(2,1)S(1)}, u32[]{:S(2)}, u32[]{:S(2)}) collective-permute-start(bf16[128,2816]{1,0:T(8,128)(2,1)} %get-tuple-element.22), channel_id=1, source_target_pairs={{0,1},{1,0},{2,3},{3,2},{4,5},{5,4},{6,7},{7,6},{8,9},{9,8},{10,11... | collective-permute-start | bytes 2162696 | tf_op jit(solution)/shard_map/ppermute | solution.py:301
  62.5 1.3 collective-permute-start.3
  63.8 0.0 collective-permute-done.refs_2_.refs_3_
  63.8 0.0 copy-done.4
  63.8 0.0 copy-done.3
  63.8 1.1 shard_map.94
  64.9 0.0 copy-start.5
  64.9 0.7 copy-done.5
  65.6 7.1 %all-to-all-start = ((f32[16,40,112]{2,1,0:T(8,128)}), f32[16,40,112]{2,1,0:T(8,128)}, u32[]{:S(2)}, u32[]{:S(2)}) async-start(f32[16,40,112]{2,1,0:T(8,128)} %shard_map.94), calls=%async_computation | async-start | bytes 655360 | tf_op jit(solution)/shard_map/all_to_all | solution.py:324
  72.8 0.0 copy-start.10
  72.8 9.8 %shard_map.95 = bf16[2,560,128]{2,1,0:T(8,128)(2,1)} custom-call(bf16[1120,128]{1,0:T(8,128)(2,1)} %bitcast.21, bf16[1120,128]{1,0:T(8,128)(2,1)} %bitcast.24), custom_call_target="tpu_custom_call" | custom-call | bytes 860160 | tf_op jit(solution)/shard_map/pallas_call | solution.py:53
  82.6 0.0 copy-start
  82.6 0.1 collective-permute-start.1
  82.7 1.8 %collective-permute-done.1.refs_3_ = bf16[2,560,128]{2,1,0:T(8,128)(2,1)S(1)} collective-permute-done((bf16[2,560,128]{2,1,0:T(8,128)(2,1)}, bf16[2,560,128]{2,1,0:T(8,128)(2,1)S(1)}, u32[]{:S(2)}, u32[]{:S(2)}) %collective-permute-start.1) | collective-permute-done | bytes 286752 | tf_op jit(solution)/shard_map/ppermute | solution.py:321
  84.5 0.7 copy-done.7
  85.2 0.0 collective-permute-done.2.refs_4_.refs_1_
  85.2 0.0 collective-permute-done.3.refs_5_.refs_2_
  85.2 6.0 %all-to-all-done.refs_0_ = f32[16,40,112]{2,1,0:T(8,128)} async-done(((f32[16,40,112]{2,1,0:T(8,128)}), f32[16,40,112]{2,1,0:T(8,128)}, u32[]{:S(2)}, u32[]{:S(2)}) %all-to-all-start) | async-done | bytes 286752 | tf_op jit(solution)/shard_map/all_to_all | solution.py:324
  91.2 0.0 copy-done.1
  91.2 1.0 copy-done.8
  92.2 2.7 %shard_map.97 = (f32[16,72,112]{2,1,0:T(8,128)}, f32[5,112]{1,0:T(8,128)S(1)}, f32[5,256]{1,0:T(8,128)S(1)}) custom-call(f32[16,40,112]{2,1,0:T(8,128)} %all-to-all-done.refs_0_, bf16[1120,128]{1,0:T(8,128)(2,1)S(1)} %bitcast.22, bf16[1120,128]{1,0:T(8,128)(2,1)S(1)} %bitcast.25, bf16[2,560,128]{2,1,0:T(8,128)(2,1)S(1)} %copy-done.8, ...), custom_call_target="tpu_custom_call" | custom-call | flops 64225280 | bytes 1670336 | tf_op jit(solution)/shard_map/pallas_call | solution.py:53
  94.9 4.4 %all-to-all-start.1 = ((f32[16,72,112]{2,1,0:T(8,128)}), f32[16,72,112]{2,1,0:T(8,128)}, u32[]{:S(2)}, u32[]{:S(2)}) async-start(f32[16,72,112]{2,1,0:T(8,128)} %get-tuple-element.24), calls=%async_computation.1 | async-start | bytes 1179648 | tf_op jit(solution)/shard_map/all_to_all | solution.py:324
  99.3 4.6 %collective-permute-start.5 = (bf16[128,2816]{1,0:T(8,128)(2,1)S(1)}, bf16[128,2816]{1,0:T(8,128)(2,1)}, u32[]{:S(2)}, u32[]{:S(2)}) collective-permute-start(bf16[128,2816]{1,0:T(8,128)(2,1)S(1)} %collective-permute-done.2.refs_4_.refs_1_), channel_id=1, source_target_pairs={{0,2},{2,4},{4,6},{3,1},{5,3},{7,5},{8,10},{10,12},{12,14},{11,9},... | collective-permute-start | bytes 2162696 | tf_op jit(solution)/shard_map/ppermute | solution.py:303
  104.0 0.0 copy-done.10
  104.0 2.2 %shard_map.98 = (bf16[128,2816]{1,0:T(8,128)(2,1)}, f32[8,128]{1,0:T(8,128)S(1)}) custom-call(bf16[128,2816]{1,0:T(8,128)(2,1)S(1)} %copy-done, bf16[128,2816]{1,0:T(8,128)(2,1)S(1)} %collective-permute-done.2.refs_4_.refs_1_, bf16[128,2816]{1,0:T(8,128)(2,1)S(1)} %collective-permute-done.3.refs_5_.refs_2_, f32[3,3,2816]{2,1,0:T(4,128)S(1)} %copy-done.10), custom_call_target="tpu_custom_call" | custom-call | flops 7208960 | bytes 2989056 | tf_op jit(solution)/shard_map/pallas_call | solution.py:53
  106.1 0.0 collective-permute-start.6
  106.1 9.8 %all-to-all-done.1.refs_0_ = f32[16,72,112]{2,1,0:T(8,128)} async-done(((f32[16,72,112]{2,1,0:T(8,128)}), f32[16,72,112]{2,1,0:T(8,128)}, u32[]{:S(2)}, u32[]{:S(2)}) %all-to-all-start.1) | async-done | bytes 516128 | tf_op jit(solution)/shard_map/all_to_all | solution.py:324
  116.0 1.0 copy-done.9
  116.9 3.0 %shard_map.99 = (f32[16,40,112]{2,1,0:T(8,128)}, bf16[560,128]{1,0:T(8,128)(2,1)S(1)}, bf16[560,128]{1,0:T(8,128)(2,1)S(1)}) custom-call(f32[16,72,112]{2,1,0:T(8,128)} %all-to-all-done.1.refs_0_, bf16[1120,128]{1,0:T(8,128)(2,1)S(1)} %bitcast.23, bf16[1120,128]{1,0:T(8,128)(2,1)S(1)} %bitcast.26, bf16[2,560,128]{2,1,0:T(8,128)(2,1)S(1)} %copy-done.9, ...), custom_call_target="tpu_custom_call" | custom-call | flops 64225280 | bytes 1957056 | tf_op jit(solution)/shard_map/pallas_call | solution.py:53
  120.0 3.7 %all-to-all-start.2 = ((f32[16,40,112]{2,1,0:T(8,128)}), f32[16,40,112]{2,1,0:T(8,128)S(1)}, u32[]{:S(2)}, u32[]{:S(2)}) async-start(f32[16,40,112]{2,1,0:T(8,128)} %get-tuple-element.31), calls=%async_computation.2 | async-start | bytes 655360 | tf_op jit(solution)/shard_map/all_to_all | solution.py:324
  123.7 0.0 copy-start.6
  123.7 1.5 %collective-permute-done.5.refs_2_ = bf16[128,2816]{1,0:T(8,128)(2,1)} collective-permute-done((bf16[128,2816]{1,0:T(8,128)(2,1)S(1)}, bf16[128,2816]{1,0:T(8,128)(2,1)}, u32[]{:S(2)}, u32[]{:S(2)}) %collective-permute-start.5) | collective-permute-done | bytes 720928 | tf_op jit(solution)/shard_map/ppermute | solution.py:303
  125.2 1.6 %collective-permute-done.6.refs_3_ = bf16[128,2816]{1,0:T(8,128)(2,1)} collective-permute-done((bf16[128,2816]{1,0:T(8,128)(2,1)}, bf16[128,2816]{1,0:T(8,128)(2,1)}, u32[]{:S(2)}, u32[]{:S(2)}) %collective-permute-start.6) | collective-permute-done | bytes 720928 | tf_op jit(solution)/shard_map/ppermute | solution.py:310
  126.8 3.8 %shard_map.100 = (bf16[1,1,128,5632]{3,2,1,0:T(8,128)(2,1)}, f32[8,128]{1,0:T(8,128)S(1)}) custom-call(bf16[128,2816]{1,0:T(8,128)(2,1)S(1)} %copy-done, bf16[128,2816]{1,0:T(8,128)(2,1)S(1)} %collective-permute-done.2.refs_4_.refs_1_, bf16[128,2816]{1,0:T(8,128)(2,1)} %collective-permute-done.5.refs_2_, bf16[128,2816]{1,0:T(8,128)(2,1)} %collective-permute-done.6.refs_3_, ...), custom_call_target="tpu_custom_call" | custom-call | flops 7208960 | bytes 4430848 | tf_op jit(solution)/shard_map/pallas_call | solution.py:53
  130.6 7.4 %all-to-all-done.2.refs_0_ = f32[16,40,112]{2,1,0:T(8,128)S(1)} async-done(((f32[16,40,112]{2,1,0:T(8,128)}), f32[16,40,112]{2,1,0:T(8,128)S(1)}, u32[]{:S(2)}, u32[]{:S(2)}) %all-to-all-start.2) | async-done | bytes 286752 | tf_op jit(solution)/shard_map/all_to_all | solution.py:324
  138.0 0.5 shard_map.101
  138.5 0.1 collective-permute-start.7
  138.6 0.5 collective-permute-start.4
  139.1 1.3 collective-permute-done.4.refs_1_
  140.4 0.0 collective-permute-done.7.refs_3_
  140.4 1.0 shard_map.102
  (6 shorter events, 0.0 us)
Async XLA Ops:
  0.6 63.2 %copy-start.4 = (bf16[1,1,128,1120]{2,3,1,0:T(8,128)(2,1)S(1)}, bf16[1,1,128,1120]{2,3,1,0:T(8,128)(2,1)}, u32[]{:S(2)}) copy-start(bf16[1,1,128,1120]{2,3,1,0:T(8,128)(2,1)} %param.8) | copy-start | bytes 860164
  0.6 63.2 %copy-start.3 = (bf16[1,1,128,1120]{2,3,1,0:T(8,128)(2,1)S(1)}, bf16[1,1,128,1120]{2,3,1,0:T(8,128)(2,1)}, u32[]{:S(2)}) copy-start(bf16[1,1,128,1120]{2,3,1,0:T(8,128)(2,1)} %param.7) | copy-start | bytes 860164
  10.5 53.3 %collective-permute-start = (bf16[2,560,128]{2,1,0:T(8,128)(2,1)}, bf16[2,560,128]{2,1,0:T(8,128)(2,1)S(1)}, u32[]{:S(2)}, u32[]{:S(2)}) collective-permute-start(bf16[2,560,128]{2,1,0:T(8,128)(2,1)} %shard_map.93), channel_id=1, source_target_pairs={{0,8},{8,0},{1,9},{9,1},{2,10},{10,2},{3,11},{11,3},{4,12},{12,4},... | collective-permute-start | bytes 860168 | tf_op jit(solution)/shard_map/ppermute | solution.py:319
  59.9 31.3 %copy-start.1 = (bf16[1,1,128,1120]{2,3,1,0:T(8,128)(2,1)S(1)}, bf16[1,1,128,1120]{2,3,1,0:T(8,128)(2,1)}, u32[]{:S(2)}) copy-start(bf16[1,1,128,1120]{2,3,1,0:T(8,128)(2,1)} %param.6) | copy-start | bytes 860164
  59.9 31.3 %copy-start.2 = (bf16[1,1,128,1120]{2,3,1,0:T(8,128)(2,1)S(1)}, bf16[1,1,128,1120]{2,3,1,0:T(8,128)(2,1)}, u32[]{:S(2)}) copy-start(bf16[1,1,128,1120]{2,3,1,0:T(8,128)(2,1)} %param.9) | copy-start | bytes 860164
  59.9 25.3 %collective-permute-start.2 = (bf16[128,2816]{1,0:T(8,128)(2,1)}, bf16[128,2816]{1,0:T(8,128)(2,1)S(1)}, u32[]{:S(2)}, u32[]{:S(2)}) collective-permute-start(bf16[128,2816]{1,0:T(8,128)(2,1)} %get-tuple-element.22), channel_id=1, source_target_pairs={{0,1},{1,0},{2,3},{3,2},{4,5},{5,4},{6,7},{7,6},{8,9},{9,8},{10,11... | collective-permute-start | bytes 2162696 | tf_op jit(solution)/shard_map/ppermute | solution.py:301
  62.5 22.7 %collective-permute-start.3 = (bf16[128,2816]{1,0:T(8,128)(2,1)}, bf16[128,2816]{1,0:T(8,128)(2,1)S(1)}, u32[]{:S(2)}, u32[]{:S(2)}) collective-permute-start(bf16[128,2816]{1,0:T(8,128)(2,1)} %get-tuple-element.23.refs_0_), channel_id=1, source_target_pairs={{2,0},{4,2},{6,4},{1,3},{3,5},{5,7},{10,8},{12,10},{14,12},{9,11},... | collective-permute-start | bytes 2162696 | tf_op jit(solution)/shard_map/ppermute | solution.py:302
  64.9 0.7 copy-start.5
  65.6 25.5 %all-to-all-start = ((f32[16,40,112]{2,1,0:T(8,128)}), f32[16,40,112]{2,1,0:T(8,128)}, u32[]{:S(2)}, u32[]{:S(2)}) async-start(f32[16,40,112]{2,1,0:T(8,128)} %shard_map.94), calls=%async_computation | async-start | bytes 655360 | tf_op jit(solution)/shard_map/all_to_all | solution.py:324
  72.8 31.2 %copy-start.10 = (f32[3,3,2816]{2,1,0:T(4,128)S(1)}, f32[3,3,2816]{2,1,0:T(4,128)}, u32[]{:S(2)}) copy-start(f32[3,3,2816]{2,1,0:T(4,128)} %get-tuple-element.27.refs_3_.refs_4_) | copy-start | bytes 304132
  82.6 21.3 %copy-start = (bf16[128,2816]{1,0:T(8,128)(2,1)S(1)}, bf16[128,2816]{1,0:T(8,128)(2,1)}, u32[]{:S(2)}) copy-start(bf16[128,2816]{1,0:T(8,128)(2,1)} %get-tuple-element.23.refs_0_) | copy-start | bytes 2162692
  82.6 1.8 %collective-permute-start.1 = (bf16[2,560,128]{2,1,0:T(8,128)(2,1)}, bf16[2,560,128]{2,1,0:T(8,128)(2,1)S(1)}, u32[]{:S(2)}, u32[]{:S(2)}) collective-permute-start(bf16[2,560,128]{2,1,0:T(8,128)(2,1)} %shard_map.95), channel_id=1, source_target_pairs={{0,8},{8,0},{1,9},{9,1},{2,10},{10,2},{3,11},{11,3},{4,12},{12,4},... | collective-permute-start | bytes 860168 | tf_op jit(solution)/shard_map/ppermute | solution.py:321
  84.5 0.7 copy-start.7
  91.2 1.0 copy-start.8
  94.9 21.1 %all-to-all-start.1 = ((f32[16,72,112]{2,1,0:T(8,128)}), f32[16,72,112]{2,1,0:T(8,128)}, u32[]{:S(2)}, u32[]{:S(2)}) async-start(f32[16,72,112]{2,1,0:T(8,128)} %get-tuple-element.24), calls=%async_computation.1 | async-start | bytes 1179648 | tf_op jit(solution)/shard_map/all_to_all | solution.py:324
  99.3 25.9 %collective-permute-start.5 = (bf16[128,2816]{1,0:T(8,128)(2,1)S(1)}, bf16[128,2816]{1,0:T(8,128)(2,1)}, u32[]{:S(2)}, u32[]{:S(2)}) collective-permute-start(bf16[128,2816]{1,0:T(8,128)(2,1)S(1)} %collective-permute-done.2.refs_4_.refs_1_), channel_id=1, source_target_pairs={{0,2},{2,4},{4,6},{3,1},{5,3},{7,5},{8,10},{10,12},{12,14},{11,9},... | collective-permute-start | bytes 2162696 | tf_op jit(solution)/shard_map/ppermute | solution.py:303
  106.1 20.6 %collective-permute-start.6 = (bf16[128,2816]{1,0:T(8,128)(2,1)}, bf16[128,2816]{1,0:T(8,128)(2,1)}, u32[]{:S(2)}, u32[]{:S(2)}) collective-permute-start(bf16[128,2816]{1,0:T(8,128)(2,1)} %get-tuple-element.32), channel_id=1, source_target_pairs={{0,1},{1,0},{2,3},{3,2},{4,5},{5,4},{6,7},{7,6},{8,9},{9,8},{10,11... | collective-permute-start | bytes 2162696 | tf_op jit(solution)/shard_map/ppermute | solution.py:310
  116.0 1.0 copy-start.9
  120.0 18.0 %all-to-all-start.2 = ((f32[16,40,112]{2,1,0:T(8,128)}), f32[16,40,112]{2,1,0:T(8,128)S(1)}, u32[]{:S(2)}, u32[]{:S(2)}) async-start(f32[16,40,112]{2,1,0:T(8,128)} %get-tuple-element.31), calls=%async_computation.2 | async-start | bytes 655360 | tf_op jit(solution)/shard_map/all_to_all | solution.py:324
  123.7 14.3 %copy-start.6 = (bf16[2,560,128]{2,1,0:T(8,128)(2,1)S(1)}, bf16[2,560,128]{2,1,0:T(8,128)(2,1)}, u32[]{:S(2)}) copy-start(bf16[2,560,128]{2,1,0:T(8,128)(2,1)} %copy-done.5) | copy-start | bytes 860164
  138.5 1.8 %collective-permute-start.7 = (bf16[2,560,128]{2,1,0:T(8,128)(2,1)S(1)}, bf16[2,560,128]{2,1,0:T(8,128)(2,1)S(1)}, u32[]{:S(2)}, u32[]{:S(2)}) collective-permute-start(bf16[2,560,128]{2,1,0:T(8,128)(2,1)S(1)} %get-tuple-element.35), channel_id=1, source_target_pairs={{0,8},{8,0},{1,9},{9,1},{2,10},{10,2},{3,11},{11,3},{4,12},{12,4},... | collective-permute-start | bytes 860168 | tf_op jit(solution)/shard_map/ppermute | solution.py:365
  138.6 1.8 %collective-permute-start.4 = (bf16[560,128]{1,0:T(8,128)(2,1)S(1)}, bf16[560,128]{1,0:T(8,128)(2,1)S(1)}, u32[]{:S(2)}, u32[]{:S(2)}) collective-permute-start(bf16[560,128]{1,0:T(8,128)(2,1)S(1)} %get-tuple-element.30), channel_id=1, source_target_pairs={{0,8},{8,0},{1,9},{9,1},{2,10},{10,2},{3,11},{11,3},{4,12},{12,4},... | collective-permute-start | bytes 430088 | tf_op jit(solution)/shard_map/ppermute | solution.py:355

commit v4 on v3

--- a/solution.py
+++ b/solution.py
@@ -296,7 +296,6 @@
         (conv_grad, conv_weight),
         [pltpu.SemaphoreType.DMA((3,))],
         hbm_in=True,
-        hbm_out=True,
     )
     row_got = lax.ppermute(row_send, "x", swap)
     far_own = lax.ppermute(row_mine, ("z", "x"), even_down + odd_up)
@@ -315,9 +314,9 @@
         flops=20 * cols * width,
     )
 
-    kv_send = call(send_half, [pair_shape], (k, v), two_sems, hbm_in=True, hbm_out=True)[0]
+    kv_send = call(send_half, [pair_shape], (k, v), two_sems, hbm_in=True)[0]
     kv_got = lax.ppermute(kv_send, "c", swap)
-    qg_send = call(send_half, [pair_shape], (q, g), two_sems, hbm_in=True, hbm_out=True)[0]
+    qg_send = call(send_half, [pair_shape], (q, g), two_sems, hbm_in=True)[0]
     qg_got = lax.ppermute(qg_send, "c", swap)
 
     def exchange(pay):

time: 142 us -> 86.4 us (0.61)
  Pallas kernels: 82.9 us -> 18.6 us
  waiting for transfers between devices: 29.3 us -> 38 us
    pallas_call x10, Pallas kernels: 82.9 us -> 18.6 us  [call(): pl.pallas_call(ordered, out_shape=shapes, in_specs=[slow if hbm_in else f...]
    ppermute x1, waiting for transfers between devices: 0.01 us -> 5.4 us  [shards(): row_got = lax.ppermute(row_send, 'x', swap)]
    ppermute x1, waiting for transfers between devices: 0.01 us -> 2.02 us  [shards(): far_own = lax.ppermute(row_mine, ('z', 'x'), even_down + odd_up)]
    all_to_all x3, waiting for transfers between devices: 23.2 us -> 24.7 us  [exchange(): return lax.all_to_all(pay, CHIPS, split_axis=0, concat_axis=0, tiled=True)]
    unnamed x22 -> x18, local copies, waits for them, and re-layouts: 3.37 us -> 3.36 us
  transfers between devices with their start and end apart: 11 -> 11, of which waited for: 7 -> 9; matrix products, arithmetic and copies ran while one was open for 0% -> 0% of each run, Pallas kernels for 49% -> 16%
where the time goes in v4:
time: 86.4 us; the launch traced here: 85.7 us
  waiting for transfers between devices  38 us (44%)
  starting transfers between devices  24.9 us (29%)
  Pallas kernels  18.6 us (22%)
  local copies, waits for them, and re-layouts  3.36 us (4%)
    all_to_all x3, waiting for transfers between devices, exchange(): return lax.all_to_all(pay, CHIPS, split_axis=0, concat_axis=0, tiled=True)  24.7 us
    pallas_call x10, Pallas kernels, call(): pl.pallas_call(ordered, out_shape=shapes, in_specs=[slow if hbm_in else f...  18.6 us
    all_to_all x3, starting transfers between devices, exchange(): return lax.all_to_all(pay, CHIPS, split_axis=0, concat_axis=0, tiled=True)  15.2 us
    ppermute x1, waiting for transfers between devices, shards(): row_got = lax.ppermute(row_send, 'x', swap)  5.4 us
    ppermute x1, starting transfers between devices, shards(): far_fwd = lax.ppermute(row_got, ('z', 'x'), even_up + odd_down)  4.64 us
    unnamed x18, local copies, waits for them, and re-layouts  3.36 us
    ppermute x1, starting transfers between devices, shards(): row_got = lax.ppermute(row_send, 'x', swap)  2.58 us
    ppermute x1, waiting for transfers between devices, shards(): far_own = lax.ppermute(row_mine, ('z', 'x'), even_down + odd_up)  2.02 us
  transfers between devices with their start and end apart: 11, of which 9 were waited for; matrix products, arithmetic and copies ran while one was open for 0% of the time, Pallas kernels for 16%

profile of v4, /device:TPU:0, one launch (start us, length us, event | category | flops | bytes accessed | tf_op | source)
XLA Modules:
  0.0 85.7 jit_solution(11586692961215832493)
XLA Ops:
  0.6 0.0 copy-start.3
  0.6 0.0 copy-start.2
  0.7 1.1 %shard_map.93 = bf16[2,560,128]{2,1,0:T(8,128)(2,1)S(1)} custom-call(bf16[1120,128]{1,0:T(8,128)(2,1)} %bitcast.27, bf16[1120,128]{1,0:T(8,128)(2,1)} %bitcast.30), custom_call_target="tpu_custom_call" | custom-call | bytes 860160 | tf_op jit(solution)/shard_map/pallas_call | solution.py:53
  1.7 0.5 collective-permute-start
  2.2 2.2 %shard_map.96 = (bf16[128,2816]{1,0:T(8,128)(2,1)S(1)}, bf16[128,2816]{1,0:T(8,128)(2,1)}, f32[3,3,2816]{2,1,0:T(4,128)S(1)}) custom-call(bf16[1,1,128,5632]{3,2,1,0:T(8,128)(2,1)} %refs_0_.1, f32[3,3,5632]{2,1,0:T(4,128)} %refs_1_.1), custom_call_target="tpu_custom_call" | custom-call | bytes 3187712 | tf_op jit(solution)/shard_map/pallas_call | solution.py:53
  4.5 0.0 copy-start
  4.5 0.0 copy-start.1
  4.5 2.6 %collective-permute-start.2 = (bf16[128,2816]{1,0:T(8,128)(2,1)}, bf16[128,2816]{1,0:T(8,128)(2,1)S(1)}, u32[]{:S(2)}, u32[]{:S(2)}) collective-permute-start(bf16[128,2816]{1,0:T(8,128)(2,1)} %get-tuple-element.22), channel_id=1, source_target_pairs={{0,1},{1,0},{2,3},{3,2},{4,5},{5,4},{6,7},{7,6},{8,9},{9,8},{10,11... | collective-permute-start | bytes 2162696 | tf_op jit(solution)/shard_map/ppermute | solution.py:300
  7.1 1.3 %collective-permute-start.3 = (bf16[128,2816]{1,0:T(8,128)(2,1)S(1)}, bf16[128,2816]{1,0:T(8,128)(2,1)S(1)}, u32[]{:S(2)}, u32[]{:S(2)}) collective-permute-start(bf16[128,2816]{1,0:T(8,128)(2,1)S(1)} %get-tuple-element.23.refs_0_), channel_id=1, source_target_pairs={{2,0},{4,2},{6,4},{1,3},{3,5},{5,7},{10,8},{12,10},{14,12},{9,11},... | collective-permute-start | bytes 2162696 | tf_op jit(solution)/shard_map/ppermute | solution.py:301
  8.4 0.0 collective-permute-done.refs_2_.refs_3_
  8.4 0.0 copy-done.3
  8.4 0.0 copy-done.2
  8.4 1.1 %shard_map.94 = f32[16,40,112]{2,1,0:T(8,128)} custom-call(bf16[1120,128]{1,0:T(8,128)(2,1)S(1)} %bitcast.28, bf16[1120,128]{1,0:T(8,128)(2,1)S(1)} %bitcast.31, bf16[2,560,128]{2,1,0:T(8,128)(2,1)S(1)} %collective-permute-done.refs_2_.refs_3_), custom_call_target="tpu_custom_call" | custom-call | flops 32112640 | bytes 1146880 | tf_op jit(solution)/shard_map/pallas_call | solution.py:53
  9.5 0.0 copy-start.4
  9.5 0.7 copy-done.4
  10.2 7.1 %all-to-all-start = ((f32[16,40,112]{2,1,0:T(8,128)}), f32[16,40,112]{2,1,0:T(8,128)}, u32[]{:S(2)}, u32[]{:S(2)}) async-start(f32[16,40,112]{2,1,0:T(8,128)} %shard_map.94), calls=%async_computation | async-start | bytes 655360 | tf_op jit(solution)/shard_map/all_to_all | solution.py:323
  17.4 1.0 %shard_map.95 = bf16[2,560,128]{2,1,0:T(8,128)(2,1)S(1)} custom-call(bf16[1120,128]{1,0:T(8,128)(2,1)} %bitcast.21, bf16[1120,128]{1,0:T(8,128)(2,1)} %bitcast.24), custom_call_target="tpu_custom_call" | custom-call | bytes 860160 | tf_op jit(solution)/shard_map/pallas_call | solution.py:53
  18.4 0.1 collective-permute-start.1
  18.4 1.6 %collective-permute-done.1.refs_3_ = bf16[2,560,128]{2,1,0:T(8,128)(2,1)S(1)} collective-permute-done((bf16[2,560,128]{2,1,0:T(8,128)(2,1)S(1)}, bf16[2,560,128]{2,1,0:T(8,128)(2,1)S(1)}, u32[]{:S(2)}, u32[]{:S(2)}) %collective-permute-start.1) | collective-permute-done | bytes 286752 | tf_op jit(solution)/shard_map/ppermute | solution.py:320
  20.0 0.0 copy-start.6
  20.0 0.7 copy-done.6
  20.7 5.4 %collective-permute-done.2.refs_4_.refs_1_ = bf16[128,2816]{1,0:T(8,128)(2,1)S(1)} collective-permute-done((bf16[128,2816]{1,0:T(8,128)(2,1)}, bf16[128,2816]{1,0:T(8,128)(2,1)S(1)}, u32[]{:S(2)}, u32[]{:S(2)}) %collective-permute-start.2) | collective-permute-done | bytes 720928 | tf_op jit(solution)/shard_map/ppermute | solution.py:300
  26.1 2.0 %collective-permute-done.3.refs_5_.refs_2_ = bf16[128,2816]{1,0:T(8,128)(2,1)S(1)} collective-permute-done((bf16[128,2816]{1,0:T(8,128)(2,1)S(1)}, bf16[128,2816]{1,0:T(8,128)(2,1)S(1)}, u32[]{:S(2)}, u32[]{:S(2)}) %collective-permute-start.3) | collective-permute-done | bytes 720928 | tf_op jit(solution)/shard_map/ppermute | solution.py:301
  28.1 7.4 %all-to-all-done.refs_0_ = f32[16,40,112]{2,1,0:T(8,128)} async-done(((f32[16,40,112]{2,1,0:T(8,128)}), f32[16,40,112]{2,1,0:T(8,128)}, u32[]{:S(2)}, u32[]{:S(2)}) %all-to-all-start) | async-done | bytes 286752 | tf_op jit(solution)/shard_map/all_to_all | solution.py:323
  35.6 0.0 copy-done
  35.6 0.0 copy-done.1
  35.6 1.0 %copy-done.7 = bf16[2,560,128]{2,1,0:T(8,128)(2,1)S(1)} copy-done((bf16[2,560,128]{2,1,0:T(8,128)(2,1)S(1)}, bf16[2,560,128]{2,1,0:T(8,128)(2,1)}, u32[]{:S(2)}) %copy-start.7) | copy-done | bytes 286744
  36.5 2.7 %shard_map.97 = (f32[16,72,112]{2,1,0:T(8,128)}, f32[5,112]{1,0:T(8,128)S(1)}, f32[5,256]{1,0:T(8,128)S(1)}) custom-call(f32[16,40,112]{2,1,0:T(8,128)} %all-to-all-done.refs_0_, bf16[1120,128]{1,0:T(8,128)(2,1)S(1)} %bitcast.22, bf16[1120,128]{1,0:T(8,128)(2,1)S(1)} %bitcast.25, bf16[2,560,128]{2,1,0:T(8,128)(2,1)S(1)} %copy-done.7, ...), custom_call_target="tpu_custom_call" | custom-call | flops 64225280 | bytes 1670336 | tf_op jit(solution)/shard_map/pallas_call | solution.py:53
  39.3 4.4 %all-to-all-start.1 = ((f32[16,72,112]{2,1,0:T(8,128)}), f32[16,72,112]{2,1,0:T(8,128)}, u32[]{:S(2)}, u32[]{:S(2)}) async-start(f32[16,72,112]{2,1,0:T(8,128)} %get-tuple-element.24), calls=%async_computation.1 | async-start | bytes 1179648 | tf_op jit(solution)/shard_map/all_to_all | solution.py:323
  43.7 4.6 %collective-permute-start.5 = (bf16[128,2816]{1,0:T(8,128)(2,1)S(1)}, bf16[128,2816]{1,0:T(8,128)(2,1)}, u32[]{:S(2)}, u32[]{:S(2)}) collective-permute-start(bf16[128,2816]{1,0:T(8,128)(2,1)S(1)} %collective-permute-done.2.refs_4_.refs_1_), channel_id=1, source_target_pairs={{0,2},{2,4},{4,6},{3,1},{5,3},{7,5},{8,10},{10,12},{12,14},{11,9},... | collective-permute-start | bytes 2162696 | tf_op jit(solution)/shard_map/ppermute | solution.py:302
  48.3 2.2 %shard_map.98 = (bf16[128,2816]{1,0:T(8,128)(2,1)}, f32[8,128]{1,0:T(8,128)S(1)}) custom-call(bf16[128,2816]{1,0:T(8,128)(2,1)S(1)} %get-tuple-element.23.refs_0_, bf16[128,2816]{1,0:T(8,128)(2,1)S(1)} %collective-permute-done.2.refs_4_.refs_1_, bf16[128,2816]{1,0:T(8,128)(2,1)S(1)} %collective-permute-done.3.refs_5_.refs_2_, ...), custom_call_target="tpu_custom_call" | custom-call | flops 7208960 | bytes 2989056 | tf_op jit(solution)/shard_map/pallas_call | solution.py:53
  50.5 0.0 collective-permute-start.6
  50.5 9.8 %all-to-all-done.1.refs_0_ = f32[16,72,112]{2,1,0:T(8,128)} async-done(((f32[16,72,112]{2,1,0:T(8,128)}), f32[16,72,112]{2,1,0:T(8,128)}, u32[]{:S(2)}, u32[]{:S(2)}) %all-to-all-start.1) | async-done | bytes 516128 | tf_op jit(solution)/shard_map/all_to_all | solution.py:323
  60.3 1.0 %copy-done.8 = bf16[2,560,128]{2,1,0:T(8,128)(2,1)S(1)} copy-done((bf16[2,560,128]{2,1,0:T(8,128)(2,1)S(1)}, bf16[2,560,128]{2,1,0:T(8,128)(2,1)}, u32[]{:S(2)}) %copy-start.8) | copy-done | bytes 286744
  61.3 3.0 %shard_map.99 = (f32[16,40,112]{2,1,0:T(8,128)}, bf16[560,128]{1,0:T(8,128)(2,1)S(1)}, bf16[560,128]{1,0:T(8,128)(2,1)S(1)}) custom-call(f32[16,72,112]{2,1,0:T(8,128)} %all-to-all-done.1.refs_0_, bf16[1120,128]{1,0:T(8,128)(2,1)S(1)} %bitcast.23, bf16[1120,128]{1,0:T(8,128)(2,1)S(1)} %bitcast.26, bf16[2,560,128]{2,1,0:T(8,128)(2,1)S(1)} %copy-done.8, ...), custom_call_target="tpu_custom_call" | custom-call | flops 64225280 | bytes 1957056 | tf_op jit(solution)/shard_map/pallas_call | solution.py:53
  64.3 3.7 %all-to-all-start.2 = ((f32[16,40,112]{2,1,0:T(8,128)}), f32[16,40,112]{2,1,0:T(8,128)S(1)}, u32[]{:S(2)}, u32[]{:S(2)}) async-start(f32[16,40,112]{2,1,0:T(8,128)} %get-tuple-element.31), calls=%async_computation.2 | async-start | bytes 655360 | tf_op jit(solution)/shard_map/all_to_all | solution.py:323
  68.0 0.0 copy-start.5
  68.1 1.5 %collective-permute-done.5.refs_2_ = bf16[128,2816]{1,0:T(8,128)(2,1)} collective-permute-done((bf16[128,2816]{1,0:T(8,128)(2,1)S(1)}, bf16[128,2816]{1,0:T(8,128)(2,1)}, u32[]{:S(2)}, u32[]{:S(2)}) %collective-permute-start.5) | collective-permute-done | bytes 720928 | tf_op jit(solution)/shard_map/ppermute | solution.py:302
  69.5 1.6 %collective-permute-done.6.refs_3_ = bf16[128,2816]{1,0:T(8,128)(2,1)} collective-permute-done((bf16[128,2816]{1,0:T(8,128)(2,1)}, bf16[128,2816]{1,0:T(8,128)(2,1)}, u32[]{:S(2)}, u32[]{:S(2)}) %collective-permute-start.6) | collective-permute-done | bytes 720928 | tf_op jit(solution)/shard_map/ppermute | solution.py:309
  71.1 3.8 %shard_map.100 = (bf16[1,1,128,5632]{3,2,1,0:T(8,128)(2,1)}, f32[8,128]{1,0:T(8,128)S(1)}) custom-call(bf16[128,2816]{1,0:T(8,128)(2,1)S(1)} %get-tuple-element.23.refs_0_, bf16[128,2816]{1,0:T(8,128)(2,1)S(1)} %collective-permute-done.2.refs_4_.refs_1_, bf16[128,2816]{1,0:T(8,128)(2,1)} %collective-permute-done.5.refs_2_, ...), custom_call_target="tpu_custom_call" | custom-call | flops 7208960 | bytes 4430848 | tf_op jit(solution)/shard_map/pallas_call | solution.py:53
  75.0 7.4 %all-to-all-done.2.refs_0_ = f32[16,40,112]{2,1,0:T(8,128)S(1)} async-done(((f32[16,40,112]{2,1,0:T(8,128)}), f32[16,40,112]{2,1,0:T(8,128)S(1)}, u32[]{:S(2)}, u32[]{:S(2)}) %all-to-all-start.2) | async-done | bytes 286752 | tf_op jit(solution)/shard_map/all_to_all | solution.py:323
  82.4 0.0 copy-done.5
  82.4 0.5 shard_map.101
  82.9 0.1 collective-permute-start.7
  83.0 0.5 collective-permute-start.4
  83.5 1.3 %collective-permute-done.4.refs_1_ = bf16[560,128]{1,0:T(8,128)(2,1)S(1)} collective-permute-done((bf16[560,128]{1,0:T(8,128)(2,1)S(1)}, bf16[560,128]{1,0:T(8,128)(2,1)S(1)}, u32[]{:S(2)}, u32[]{:S(2)}) %collective-permute-start.4) | collective-permute-done | bytes 143392 | tf_op jit(solution)/shard_map/ppermute | solution.py:354
  84.7 0.0 collective-permute-done.7.refs_3_
  84.7 1.0 %shard_map.102 = (bf16[1120,128]{1,0:T(8,128)(2,1)}, bf16[1120,128]{1,0:T(8,128)(2,1)}, bf16[1120,128]{1,0:T(8,128)(2,1)}) custom-call(bf16[560,128]{1,0:T(8,128)(2,1)S(1)} %get-tuple-element.29.refs_0_, bf16[560,128]{1,0:T(8,128)(2,1)S(1)} %collective-permute-done.4.refs_1_, bf16[2,560,128]{2,1,0:T(8,128)(2,1)S(1)} %get-tuple-element.34.refs_2_, ...), custom_call_target="tpu_custom_call" | custom-call | bytes 1720320 | tf_op jit(solution)/shard_map/pallas_call | solution.py:53
  (2 shorter events, 0.0 us)
Async XLA Ops:
  0.6 7.7 %copy-start.3 = (bf16[1,1,128,1120]{2,3,1,0:T(8,128)(2,1)S(1)}, bf16[1,1,128,1120]{2,3,1,0:T(8,128)(2,1)}, u32[]{:S(2)}) copy-start(bf16[1,1,128,1120]{2,3,1,0:T(8,128)(2,1)} %param.8) | copy-start | bytes 860164
  0.6 7.7 %copy-start.2 = (bf16[1,1,128,1120]{2,3,1,0:T(8,128)(2,1)S(1)}, bf16[1,1,128,1120]{2,3,1,0:T(8,128)(2,1)}, u32[]{:S(2)}) copy-start(bf16[1,1,128,1120]{2,3,1,0:T(8,128)(2,1)} %param.7) | copy-start | bytes 860164
  1.7 6.6 %collective-permute-start = (bf16[2,560,128]{2,1,0:T(8,128)(2,1)S(1)}, bf16[2,560,128]{2,1,0:T(8,128)(2,1)S(1)}, u32[]{:S(2)}, u32[]{:S(2)}) collective-permute-start(bf16[2,560,128]{2,1,0:T(8,128)(2,1)S(1)} %shard_map.93), channel_id=1, source_target_pairs={{0,8},{8,0},{1,9},{9,1},{2,10},{10,2},{3,11},{11,3},{4,12},{12,4},... | collective-permute-start | bytes 860168 | tf_op jit(solution)/shard_map/ppermute | solution.py:318
  4.5 31.1 %copy-start = (bf16[1,1,128,1120]{2,3,1,0:T(8,128)(2,1)S(1)}, bf16[1,1,128,1120]{2,3,1,0:T(8,128)(2,1)}, u32[]{:S(2)}) copy-start(bf16[1,1,128,1120]{2,3,1,0:T(8,128)(2,1)} %param.6) | copy-start | bytes 860164
  4.5 31.1 %copy-start.1 = (bf16[1,1,128,1120]{2,3,1,0:T(8,128)(2,1)S(1)}, bf16[1,1,128,1120]{2,3,1,0:T(8,128)(2,1)}, u32[]{:S(2)}) copy-start(bf16[1,1,128,1120]{2,3,1,0:T(8,128)(2,1)} %param.9) | copy-start | bytes 860164
  4.5 21.6 %collective-permute-start.2 = (bf16[128,2816]{1,0:T(8,128)(2,1)}, bf16[128,2816]{1,0:T(8,128)(2,1)S(1)}, u32[]{:S(2)}, u32[]{:S(2)}) collective-permute-start(bf16[128,2816]{1,0:T(8,128)(2,1)} %get-tuple-element.22), channel_id=1, source_target_pairs={{0,1},{1,0},{2,3},{3,2},{4,5},{5,4},{6,7},{7,6},{8,9},{9,8},{10,11... | collective-permute-start | bytes 2162696 | tf_op jit(solution)/shard_map/ppermute | solution.py:300
  7.1 21.1 %collective-permute-start.3 = (bf16[128,2816]{1,0:T(8,128)(2,1)S(1)}, bf16[128,2816]{1,0:T(8,128)(2,1)S(1)}, u32[]{:S(2)}, u32[]{:S(2)}) collective-permute-start(bf16[128,2816]{1,0:T(8,128)(2,1)S(1)} %get-tuple-element.23.refs_0_), channel_id=1, source_target_pairs={{2,0},{4,2},{6,4},{1,3},{3,5},{5,7},{10,8},{12,10},{14,12},{9,11},... | collective-permute-start | bytes 2162696 | tf_op jit(solution)/shard_map/ppermute | solution.py:301
  9.5 0.7 copy-start.4
  10.2 25.3 %all-to-all-start = ((f32[16,40,112]{2,1,0:T(8,128)}), f32[16,40,112]{2,1,0:T(8,128)}, u32[]{:S(2)}, u32[]{:S(2)}) async-start(f32[16,40,112]{2,1,0:T(8,128)} %shard_map.94), calls=%async_computation | async-start | bytes 655360 | tf_op jit(solution)/shard_map/all_to_all | solution.py:323
  18.4 1.6 %collective-permute-start.1 = (bf16[2,560,128]{2,1,0:T(8,128)(2,1)S(1)}, bf16[2,560,128]{2,1,0:T(8,128)(2,1)S(1)}, u32[]{:S(2)}, u32[]{:S(2)}) collective-permute-start(bf16[2,560,128]{2,1,0:T(8,128)(2,1)S(1)} %shard_map.95), channel_id=1, source_target_pairs={{0,8},{8,0},{1,9},{9,1},{2,10},{10,2},{3,11},{11,3},{4,12},{12,4},... | collective-permute-start | bytes 860168 | tf_op jit(solution)/shard_map/ppermute | solution.py:320
  20.0 0.7 copy-start.6
  35.6 1.0 %copy-start.7 = (bf16[2,560,128]{2,1,0:T(8,128)(2,1)S(1)}, bf16[2,560,128]{2,1,0:T(8,128)(2,1)}, u32[]{:S(2)}) copy-start(bf16[2,560,128]{2,1,0:T(8,128)(2,1)} %copy-done.6) | copy-start | bytes 860164
  39.3 21.1 %all-to-all-start.1 = ((f32[16,72,112]{2,1,0:T(8,128)}), f32[16,72,112]{2,1,0:T(8,128)}, u32[]{:S(2)}, u32[]{:S(2)}) async-start(f32[16,72,112]{2,1,0:T(8,128)} %get-tuple-element.24), calls=%async_computation.1 | async-start | bytes 1179648 | tf_op jit(solution)/shard_map/all_to_all | solution.py:323
  43.7 25.9 %collective-permute-start.5 = (bf16[128,2816]{1,0:T(8,128)(2,1)S(1)}, bf16[128,2816]{1,0:T(8,128)(2,1)}, u32[]{:S(2)}, u32[]{:S(2)}) collective-permute-start(bf16[128,2816]{1,0:T(8,128)(2,1)S(1)} %collective-permute-done.2.refs_4_.refs_1_), channel_id=1, source_target_pairs={{0,2},{2,4},{4,6},{3,1},{5,3},{7,5},{8,10},{10,12},{12,14},{11,9},... | collective-permute-start | bytes 2162696 | tf_op jit(solution)/shard_map/ppermute | solution.py:302
  50.5 20.6 %collective-permute-start.6 = (bf16[128,2816]{1,0:T(8,128)(2,1)}, bf16[128,2816]{1,0:T(8,128)(2,1)}, u32[]{:S(2)}, u32[]{:S(2)}) collective-permute-start(bf16[128,2816]{1,0:T(8,128)(2,1)} %get-tuple-element.32), channel_id=1, source_target_pairs={{0,1},{1,0},{2,3},{3,2},{4,5},{5,4},{6,7},{7,6},{8,9},{9,8},{10,11... | collective-permute-start | bytes 2162696 | tf_op jit(solution)/shard_map/ppermute | solution.py:309
  60.3 1.0 %copy-start.8 = (bf16[2,560,128]{2,1,0:T(8,128)(2,1)S(1)}, bf16[2,560,128]{2,1,0:T(8,128)(2,1)}, u32[]{:S(2)}) copy-start(bf16[2,560,128]{2,1,0:T(8,128)(2,1)} %copy-done.6) | copy-start | bytes 860164
  64.3 18.0 %all-to-all-start.2 = ((f32[16,40,112]{2,1,0:T(8,128)}), f32[16,40,112]{2,1,0:T(8,128)S(1)}, u32[]{:S(2)}, u32[]{:S(2)}) async-start(f32[16,40,112]{2,1,0:T(8,128)} %get-tuple-element.31), calls=%async_computation.2 | async-start | bytes 655360 | tf_op jit(solution)/shard_map/all_to_all | solution.py:323
  68.0 14.3 %copy-start.5 = (bf16[2,560,128]{2,1,0:T(8,128)(2,1)S(1)}, bf16[2,560,128]{2,1,0:T(8,128)(2,1)}, u32[]{:S(2)}) copy-start(bf16[2,560,128]{2,1,0:T(8,128)(2,1)} %copy-done.4) | copy-start | bytes 860164
  82.9 1.8 %collective-permute-start.7 = (bf16[2,560,128]{2,1,0:T(8,128)(2,1)S(1)}, bf16[2,560,128]{2,1,0:T(8,128)(2,1)S(1)}, u32[]{:S(2)}, u32[]{:S(2)}) collective-permute-start(bf16[2,560,128]{2,1,0:T(8,128)(2,1)S(1)} %get-tuple-element.35), channel_id=1, source_target_pairs={{0,8},{8,0},{1,9},{9,1},{2,10},{10,2},{3,11},{11,3},{4,12},{12,4},... | collective-permute-start | bytes 860168 | tf_op jit(solution)/shard_map/ppermute | solution.py:364
  83.0 1.8 %collective-permute-start.4 = (bf16[560,128]{1,0:T(8,128)(2,1)S(1)}, bf16[560,128]{1,0:T(8,128)(2,1)S(1)}, u32[]{:S(2)}, u32[]{:S(2)}) collective-permute-start(bf16[560,128]{1,0:T(8,128)(2,1)S(1)} %get-tuple-element.30), channel_id=1, source_target_pairs={{0,8},{8,0},{1,9},{9,1},{2,10},{10,2},{3,11},{11,3},{4,12},{12,4},... | collective-permute-start | bytes 430088 | tf_op jit(solution)/shard_map/ppermute | solution.py:354

commit v5 on v4

--- a/solution.py
+++ b/solution.py
@@ -13,6 +13,7 @@
 EPSILON = 1e-06
 HALF = HEADS // 2
 LANES = 128
+CHUNKS = 2
 CHIPS = ("y", "z", "x")
 F32 = jnp.float32
 BF16 = jnp.bfloat16
@@ -26,10 +27,11 @@
     return pltpu.with_memory_space_constraint(x, pltpu.HBM)
 
 
-def call(body, outs, args, scratch=(), flops=0, after=(), hbm_in=False, hbm_out=False, pinned=False):
+def call(body, outs, args, scratch=(), flops=0, after=(), any_in=False, hbm_out=0, pinned=False, alias=None):
     size = sum(math.prod(a.shape) * a.dtype.itemsize for a in list(args) + list(outs))
     fast = pl.BlockSpec(memory_space=pltpu.VMEM)
     slow = pl.BlockSpec(memory_space=pltpu.HBM)
+    free = pl.BlockSpec(memory_space=pl.ANY)
     scratch = list(scratch)
     if pinned:
         scratch += [pltpu.VMEM(outs[0].shape, outs[0].dtype), pltpu.SemaphoreType.DMA((1,))]
@@ -45,20 +47,21 @@
         body(*ins, first, *made[1:], *held[:-2])
         copy_all([(first, made[0])], sem)
 
-    out_specs = [slow if hbm_out or (pinned and i == 0) else fast for i in range(len(outs))]
+    out_specs = [slow if i < max(hbm_out, pinned) else fast for i in range(len(outs))]
     shapes = [
-        pltpu.HBM(o.shape, o.dtype) if hbm_out or (pinned and i == 0) else o
+        pltpu.HBM(o.shape, o.dtype) if i < max(hbm_out, pinned) else o
         for i, o in enumerate(outs)
     ]
     return pl.pallas_call(
         ordered,
         out_shape=shapes,
-        in_specs=[slow if hbm_in else fast] * len(args) + [pl.BlockSpec(memory_space=pl.ANY)] * len(after),
+        in_specs=[free if any_in else fast] * len(args) + [free] * len(after),
         out_specs=out_specs,
         scratch_shapes=scratch,
         compiler_params=pltpu.CompilerParams(vmem_limit_bytes=16 * 1024 * 1024),
         cost_estimate=pl.CostEstimate(flops=flops, bytes_accessed=size, transcendentals=0),
-    )(*[held_in_hbm(a) if hbm_in else a for a in args], *after)
+        input_output_aliases=alias or {},
+    )(*args, *after)
 
 
 def copy_all(pairs, sems):
@@ -97,17 +100,25 @@
     copy_all([(a_ref.at[part], send_ref.at[0]), (b_ref.at[part], send_ref.at[1])], sems)
 
 
-def merge_half(qm, qt, km, kt, q_ref, k_ref, v_ref):
+def halves(size):
     core = lax.axis_index("c")
-    size = qm.shape[0]
     mine = pl.ds(pl.multiple_of(core * size, 16), size)
     theirs = pl.ds(pl.multiple_of((1 - core) * size, 16), size)
-    q_ref[mine] = qm[...]
-    q_ref[theirs] = qt[...]
-    k_ref[mine] = km[0]
-    k_ref[theirs] = kt[0]
-    v_ref[mine] = km[1]
-    v_ref[theirs] = kt[1]
+    return mine, theirs
+
+
+def merge_query(own, far, out, token):
+    token[...] = jnp.zeros(token.shape, F32)
+    mine, theirs = halves(own.shape[0])
+    out[mine] = own[...]
+    out[theirs] = far[...]
+
+
+def merge_pair(own, far, first, second):
+    mine, theirs = halves(own.shape[1])
+    for i, out in enumerate((first, second)):
+        out[mine] = own[i]
+        out[theirs] = far[i]
 
 
 def head_of(ref, got, i, h):
@@ -133,7 +144,8 @@
     return total
 
 
-def state_body(n, rows, k_ref, v_ref, kv_got, pay, whole):
+def state_body(n, rows, k_ref, v_ref, kv_got, pay, token, whole):
+    token[...] = jnp.zeros(token.shape, F32)
     for h in range(HALF):
         key = jnp.maximum(head_of(k_ref, kv_got, 0, h), 0)
         val = head_of(v_ref, kv_got, 1, h)
@@ -213,52 +225,69 @@
     return jnp.where(rows == edge, 0.0, moved)
 
 
-def taps(sources, weight, picks, lanes):
+def taps(sources, weight, picks, lanes, near):
     planes = [ref[:, lanes].astype(F32) for ref in sources]
 
     def column(j):
-        return sum(p * weight[i, pl.ds(j, 1), lanes] for p, i in zip(planes, picks))
+        return sum(p * weight[i, pl.ds(j, 1), near] for p, i in zip(planes, picks))
 
     return (column(1) + shift(column(0), -1) + shift(column(2), 1)).astype(BF16)
 
 
-def halve_body(row, weight, mine, send, weight_mine, sems):
+def columns_at(start, width):
+    return pl.ds(pl.multiple_of(start, LANES), width)
+
+
+def halve_body(row, weight, *refs):
+    outs, token, held, sems = refs[:5], refs[5], refs[6:11], refs[11]
+    token[...] = jnp.zeros(token.shape, F32)
+    side = lax.axis_index("x")
+    width = outs[0].shape[1]
+    pairs = []
+    for i in range(CHUNKS):
+        send = columns_at((1 - side) * CHUNKS * width + i * width, width)
+        mine = columns_at(side * CHUNKS * width + i * width, width)
+        pairs += [row.at[0, 0, :, send], row.at[0, 0, :, mine]]
+    pairs.append(weight.at[:, :, columns_at(side * CHUNKS * width, CHUNKS * width)])
+    copy_all(list(zip(pairs, held)), sems)
+    copy_all(list(zip(held, outs)), sems)
+
+
+def send_body(at, mine, got, far, weight, out, token, *held):
+    *held, made, sems = held
+    token[...] = jnp.zeros(token.shape, F32)
+    copy_all(list(zip((mine, got, far, weight), held)), sems)
+    mine, got, far, weight = held
     side = lax.axis_index("x")
     width = mine.shape[1]
-    here = pl.ds(pl.multiple_of(side * width, LANES), width)
-    there = pl.ds(pl.multiple_of((1 - side) * width, LANES), width)
-    pairs = [
-        (row.at[0, 0, :, there], send),
-        (row.at[0, 0, :, here], mine),
-        (weight.at[:, :, here], weight_mine),
-    ]
-    copy_all(pairs, sems)
-
-
-def send_body(mine, got, far, weight, out, token):
+
+    @pl.loop(0, width // LANES)
+    def _(t):
+        lanes = columns_at(t * LANES, LANES)
+        near = columns_at(at + t * LANES, LANES)
+        made[:, lanes] = taps((got, mine, far), weight, (1, 2 - 2 * side, 2 * side), lanes, near)
+
+    copy_all([(made, out)], sems)
+
+
+def keep_body(at, mine, got, far, back, weight, *refs):
+    out, token, *held = refs[-9:]
+    *held, made, sems = held
     token[...] = jnp.zeros(token.shape, F32)
+    copy_all(list(zip((mine, got, far, back, weight), held)), sems)
+    mine, got, far, back, weight = held
     side = lax.axis_index("x")
     width = mine.shape[1]
 
     @pl.loop(0, width // LANES)
     def _(t):
-        lanes = pl.ds(pl.multiple_of(t * LANES, LANES), LANES)
-        out[:, lanes] = taps((got, mine, far), weight, (1, 2 - 2 * side, 2 * side), lanes)
-
-
-def keep_body(mine, got, far, back, weight, out, token):
-    token[...] = jnp.zeros(token.shape, F32)
-    side = lax.axis_index("x")
-    width = mine.shape[1]
-
-    @pl.loop(0, width // LANES)
-    def _(t):
-        at = t * LANES
-        lanes = pl.ds(pl.multiple_of(at, LANES), LANES)
-        here = pl.ds(pl.multiple_of(side * width + at, LANES), LANES)
-        there = pl.ds(pl.multiple_of((1 - side) * width + at, LANES), LANES)
-        out[0, 0, :, here] = taps((mine, got, far), weight, (1, 2 * side, 2 - 2 * side), lanes)
-        out[0, 0, :, there] = back[:, lanes]
+        lanes = columns_at(t * LANES, LANES)
+        near = columns_at(at + t * LANES, LANES)
+        made[:, lanes] = taps((mine, got, far), weight, (1, 2 * side, 2 - 2 * side), lanes, near)
+
+    here = columns_at(side * CHUNKS * width + at, width)
+    there = columns_at((1 - side) * CHUNKS * width + at, width)
+    copy_all([(made, out.at[0, 0, :, here]), (back, out.at[0, 0, :, there])], sems)
 
 
 def shards(queries, key_proj, value_proj, attn_grad, conv_grad, conv_weight):
@@ -287,51 +316,74 @@
     odd_up = [(2 * i + 1, 2 * j + 1) for i, j in ahead]
     odd_down = [(2 * j + 1, 2 * i + 1) for i, j in ahead]
     cols, ch = conv_grad.shape[2:]
-    width = ch // 2
+    width = ch // (2 * CHUNKS)
     half_shape = sd((cols, width), BF16)
     token = sd((8, LANES), F32)
-    row_mine, row_send, weight = call(
-        halve_body,
-        [half_shape, half_shape, sd((3, 3, width), F32)],
-        (conv_grad, conv_weight),
-        [pltpu.SemaphoreType.DMA((3,))],
-        hbm_in=True,
-    )
-    row_got = lax.ppermute(row_send, "x", swap)
-    far_own = lax.ppermute(row_mine, ("z", "x"), even_down + odd_up)
-    far_fwd = lax.ppermute(row_got, ("z", "x"), even_up + odd_down)
-    out_send, sent = call(
-        send_body,
-        [half_shape, token],
-        (row_mine, row_got, far_own, weight),
-        flops=20 * cols * width,
-    )
-    out_got = lax.ppermute(out_send, "x", swap)
-    input_grad, kept = call(
-        keep_body,
-        [sd(conv_grad.shape, BF16), token],
-        (row_mine, row_got, far_fwd, out_got, weight),
-        flops=20 * cols * width,
-    )
-
-    kv_send = call(send_half, [pair_shape], (k, v), two_sems, hbm_in=True)[0]
+    held = [pltpu.VMEM((cols, width), BF16)]
+    held_weight = [pltpu.VMEM((3, 3, CHUNKS * width), F32)]
+
+    def sems(count):
+        return [pltpu.SemaphoreType.DMA((count,))]
+
+    kv_send = call(send_half, [pair_shape], (held_in_hbm(k), held_in_hbm(v)), two_sems, any_in=True)[0]
     kv_got = lax.ppermute(kv_send, "c", swap)
-    qg_send = call(send_half, [pair_shape], (q, g), two_sems, hbm_in=True)[0]
+    qg_send = call(send_half, [pair_shape], (held_in_hbm(q), held_in_hbm(g)), two_sems, any_in=True)[0]
     qg_got = lax.ppermute(qg_send, "c", swap)
 
     def exchange(pay):
         return lax.all_to_all(pay, CHIPS, split_axis=0, concat_axis=0, tiled=True)
 
     macs = HALF * 2 * tok * HD * HD
-    (pay,) = call(
+    pay, started = call(
         functools.partial(state_body, n, rows),
-        [sd((n, pay_one, HD), F32)],
+        [sd((n, pay_one, HD), F32), token],
         (k, v, kv_got),
         scratch,
         flops=2 * macs,
         pinned=True,
     )
     got = exchange(pay)
+    *parts, weight, halved = call(
+        halve_body,
+        [half_shape] * (2 * CHUNKS) + [sd((3, 3, CHUNKS * width), F32), token],
+        (held_in_hbm(conv_grad), held_in_hbm(conv_weight)),
+        held * (2 * CHUNKS) + held_weight + sems(5),
+        after=(started,),
+        any_in=True,
+        hbm_out=5,
+    )
+    row_send, row_mine = parts[::2], parts[1::2]
+
+    def move_in(i):
+        near = lax.ppermute(row_send[i], "x", swap)
+        return near, lax.ppermute(row_mine[i], ("z", "x"), even_down + odd_up)
+
+    def move_on(i, near, far):
+        onward = lax.ppermute(near, ("z", "x"), even_up + odd_down)
+        out_send, sent = call(
+            functools.partial(send_body, i * width),
+            [half_shape, token],
+            (row_mine[i], near, far, weight),
+            held * 3 + held_weight + held + sems(4),
+            flops=20 * cols * width,
+            any_in=True,
+            hbm_out=1,
+        )
+        return onward, lax.ppermute(out_send, "x", swap), sent
+
+    def finish(i, near, onward, back, before=()):
+        return call(
+            functools.partial(keep_body, i * width),
+            [sd(conv_grad.shape, BF16), token],
+            (row_mine[i], near, onward, back, weight, *before),
+            held * 4 + held_weight + held + sems(5),
+            flops=20 * cols * width,
+            any_in=True,
+            hbm_out=1,
+            alias={5: 0} if before else None,
+        )
+
+    near_a, far_a = move_in(0)
     pay, norm, inv = call(
         functools.partial(grad_body, n, rows, scale),
         [sd((n, pay_two, HD), F32), sd((HALF, HD), F32), sd((HALF, 2 * tok), F32)],
@@ -339,8 +391,10 @@
         scratch,
         flops=4 * macs,
         pinned=True,
-        after=(row_got, far_own),
-    )
+        after=(near_a, far_a),
+    )
+    near_b, far_b = move_in(1)
+    onward_a, back_a, sent_a = move_on(0, near_a, far_a)
     got = exchange(pay)
     pay, query_mine, query_send = call(
         functools.partial(query_body, n, rows, scale),
@@ -349,9 +403,13 @@
         scratch,
         flops=4 * macs,
         pinned=True,
-        after=(sent,),
+        after=(near_b, far_b, sent_a),
     )
     query_got = lax.ppermute(query_send, "c", swap)
+    onward_b, back_b, sent_b = move_on(1, near_b, far_b)
+    input_grad, kept = finish(0, near_a, onward_a, back_a)
+    whole_shape = sd((2 * half, tok), BF16)
+    query_out, merged = call(merge_query, [whole_shape, token], (query_mine, query_got))
     got = exchange(pay)
     key_mine, key_send = call(
         functools.partial(key_body, n, rows),
@@ -359,14 +417,11 @@
         (got, k, v, kv_got),
         scratch,
         flops=8 * macs,
-        after=(kept,),
+        after=(kept, merged, sent_b),
     )
     key_got = lax.ppermute(key_send, "c", swap)
-    outs = call(
-        merge_half,
-        [sd((2 * half, tok), BF16)] * 3,
-        (query_mine, query_got, key_mine, key_got),
-    )
+    input_grad, _ = finish(1, near_b, onward_b, back_b, (input_grad,))
+    outs = query_out, *call(merge_pair, [whole_shape] * 2, (key_mine, key_got))
     outs = [jnp.swapaxes(o.reshape(*queries.shape[:2], 2 * half, -1), 2, 3) for o in outs]
     return (*outs, input_grad)
 

time: 86.4 us -> 95.6 us (1.11)
  starting transfers between devices: 24.9 us -> 36.8 us
  waiting for transfers between devices: 38 us -> 32.1 us
  Pallas kernels: 18.6 us -> 22 us
    all_to_all x3, waiting for transfers between devices: 24.7 us -> 0.01 us  [exchange(): return lax.all_to_all(pay, CHIPS, split_axis=0, concat_axis=0, tiled=True)]
    ppermute x4 -> x8, waiting for transfers between devices: 10.5 us -> 29.3 us  [the longest x2 15.5 us: move_in(): near = lax.ppermute(row_send[i], 'x', swap)]
    ppermute x4 -> x8, starting transfers between devices: 8.5 us -> 15.2 us  [the longest x2 8.59 us: move_on(): onward = lax.ppermute(near, ('z', 'x'), even_up + odd_down)]
    all_to_all x3, starting transfers between devices: 15.2 us -> 20.8 us  [exchange(): return lax.all_to_all(pay, CHIPS, split_axis=0, concat_axis=0, tiled=True)]
    pallas_call x10 -> x13, Pallas kernels: 18.6 us -> 22 us  [call(): pl.pallas_call(ordered, out_shape=shapes, in_specs=[free if any_in else f...]
    ppermute x1, waiting for transfers between devices: 1.26 us -> 0.01 us  [shards(): query_got = lax.ppermute(query_send, 'c', swap)]
    ppermute x1, waiting for transfers between devices: 0.01 us -> 1.2 us  [shards(): kv_got = lax.ppermute(kv_send, 'c', swap)]
    unnamed x18 -> x28, local copies, waits for them, and re-layouts: 3.36 us -> 2.94 us
  transfers between devices with their start and end apart: 11 -> 15, of which waited for: 9 -> 10; matrix products, arithmetic and copies ran while one was open for 0% -> 0% of each run, Pallas kernels for 16% -> 16%
where the time goes in v5:
time: 95.6 us; the launch traced here: 94.8 us
  starting transfers between devices  36.8 us (38%)
  waiting for transfers between devices  32.1 us (34%)
  Pallas kernels  22 us (23%)
  local copies, waits for them, and re-layouts  2.94 us (3%)
  between operations  0.96 us (1%)
    pallas_call x13, Pallas kernels, call(): pl.pallas_call(ordered, out_shape=shapes, in_specs=[free if any_in else f...  22 us
    all_to_all x3, starting transfers between devices, exchange(): return lax.all_to_all(pay, CHIPS, split_axis=0, concat_axis=0, tiled=True)  20.8 us
    ppermute x2, waiting for transfers between devices, move_in(): near = lax.ppermute(row_send[i], 'x', swap)  15.5 us
    ppermute x2, starting transfers between devices, move_on(): onward = lax.ppermute(near, ('z', 'x'), even_up + odd_down)  8.59 us
    ppermute x2, waiting for transfers between devices, move_in(): return (near, lax.ppermute(row_mine[i], ('z', 'x'), even_down + odd_up))  5.93 us
    ppermute x2, waiting for transfers between devices, move_on(): onward = lax.ppermute(near, ('z', 'x'), even_up + odd_down)  4.01 us
    ppermute x2, waiting for transfers between devices, move_on(): return (onward, lax.ppermute(out_send, 'x', swap), sent)  3.92 us
    ppermute x2, starting transfers between devices, move_in(): near = lax.ppermute(row_send[i], 'x', swap)  3.91 us
  transfers between devices with their start and end apart: 15, of which 10 were waited for; matrix products, arithmetic and copies ran while one was open for 0% of the time, Pallas kernels for 16%

profile of v5, /device:TPU:0, one launch (start us, length us, event | category | flops | bytes accessed | tf_op | source)
XLA Modules:
  0.0 94.8 jit_solution(10502518760966074589)
XLA Ops:
  0.6 1.0 %shard_map.93 = bf16[2,560,128]{2,1,0:T(8,128)(2,1)S(1)} custom-call(bf16[1120,128]{1,0:T(8,128)(2,1)} %bitcast.27, bf16[1120,128]{1,0:T(8,128)(2,1)} %bitcast.30), custom_call_target="tpu_custom_call" | custom-call | bytes 860160 | tf_op jit(solution)/shard_map/pallas_call | solution.py:55
  1.6 0.5 collective-permute-start
  2.2 1.2 %collective-permute-done.refs_2_.refs_3_ = bf16[2,560,128]{2,1,0:T(8,128)(2,1)S(1)} collective-permute-done((bf16[2,560,128]{2,1,0:T(8,128)(2,1)S(1)}, bf16[2,560,128]{2,1,0:T(8,128)(2,1)S(1)}, u32[]{:S(2)}, u32[]{:S(2)}) %collective-permute-start) | collective-permute-done | bytes 286752 | tf_op jit(solution)/shard_map/ppermute | solution.py:329
  3.4 1.0 %copy-done.2 = bf16[1,1,128,1120]{2,3,1,0:T(8,128)(2,1)S(1)} copy-done((bf16[1,1,128,1120]{2,3,1,0:T(8,128)(2,1)S(1)}, bf16[1,1,128,1120]{2,3,1,0:T(8,128)(2,1)}, u32[]{:S(2)}) %copy-start.2) | copy-done | bytes 286744
  4.3 1.0 %copy-done.4 = bf16[1,1,128,1120]{2,3,1,0:T(8,128)(2,1)S(1)} copy-done((bf16[1,1,128,1120]{2,3,1,0:T(8,128)(2,1)S(1)}, bf16[1,1,128,1120]{2,3,1,0:T(8,128)(2,1)}, u32[]{:S(2)}) %copy-start.4) | copy-done | bytes 286744
  5.3 1.1 %shard_map.94 = (f32[16,40,112]{2,1,0:T(8,128)}, f32[8,128]{1,0:T(8,128)S(1)}) custom-call(bf16[1120,128]{1,0:T(8,128)(2,1)S(1)} %bitcast.28, bf16[1120,128]{1,0:T(8,128)(2,1)S(1)} %bitcast.31, bf16[2,560,128]{2,1,0:T(8,128)(2,1)S(1)} %collective-permute-done.refs_2_.refs_3_), custom_call_target="tpu_custom_call" | custom-call | flops 32112640 | bytes 1150976 | tf_op jit(solution)/shard_map/pallas_call | solution.py:55
  6.4 8.2 %all-to-all-start = ((f32[16,40,112]{2,1,0:T(8,128)}), f32[16,40,112]{2,1,0:T(8,128)S(1)}, u32[]{:S(2)}, u32[]{:S(2)}) async-start(f32[16,40,112]{2,1,0:T(8,128)} %get-tuple-element.30), calls=%async_computation | async-start | bytes 655360 | tf_op jit(solution)/shard_map/all_to_all | solution.py:334
  14.7 0.0 copy-start
  14.7 0.0 copy-start.1
  14.7 3.2 %shard_map.96 = (bf16[128,1408]{1,0:T(8,128)(2,1)}, bf16[128,1408]{1,0:T(8,128)(2,1)}, bf16[128,1408]{1,0:T(8,128)(2,1)}, bf16[128,1408]{1,0:T(8,128)(2,1)}, f32[3,3,2816]{2,1,0:T(4,128)}, /*index=5*/f32[8,128]{1,0:T(8,128)}) custom-call(bf16[1,1,128,5632]{3,2,1,0:T(8,128)(2,1)} %refs_0_.1, f32[3,3,5632]{2,1,0:T(4,128)} %refs_1_.1, ...), custom_call_target="tpu_custom_call" | custom-call | bytes 3191808 | tf_op jit(solution)/shard_map/pallas_call | solution.py:55
  17.9 2.0 %collective-permute-start.2 = (bf16[128,1408]{1,0:T(8,128)(2,1)}, bf16[128,1408]{1,0:T(8,128)(2,1)S(1)}, u32[]{:S(2)}, u32[]{:S(2)}) collective-permute-start(bf16[128,1408]{1,0:T(8,128)(2,1)} %get-tuple-element.32), channel_id=1, source_target_pairs={{0,1},{1,0},{2,3},{3,2},{4,5},{5,4},{6,7},{7,6},{8,9},{9,8},{10,11... | collective-permute-start | bytes 1081352 | tf_op jit(solution)/shard_map/ppermute | solution.py:358
  19.9 1.3 %collective-permute-start.3 = (bf16[128,1408]{1,0:T(8,128)(2,1)}, bf16[128,1408]{1,0:T(8,128)(2,1)S(1)}, u32[]{:S(2)}, u32[]{:S(2)}) collective-permute-start(bf16[128,1408]{1,0:T(8,128)(2,1)} %get-tuple-element.33.refs_0_), channel_id=1, source_target_pairs={{2,0},{4,2},{6,4},{1,3},{3,5},{5,7},{10,8},{12,10},{14,12},{9,11},... | collective-permute-start | bytes 1081352 | tf_op jit(solution)/shard_map/ppermute | solution.py:359
  21.1 1.0 %shard_map.95 = bf16[2,560,128]{2,1,0:T(8,128)(2,1)S(1)} custom-call(bf16[1120,128]{1,0:T(8,128)(2,1)} %bitcast.21, bf16[1120,128]{1,0:T(8,128)(2,1)} %bitcast.24), custom_call_target="tpu_custom_call" | custom-call | bytes 860160 | tf_op jit(solution)/shard_map/pallas_call | solution.py:55
  22.2 0.0 copy-start.6
  22.2 0.1 collective-permute-start.1
  22.3 1.6 %collective-permute-done.1.refs_3_ = bf16[2,560,128]{2,1,0:T(8,128)(2,1)S(1)} collective-permute-done((bf16[2,560,128]{2,1,0:T(8,128)(2,1)S(1)}, bf16[2,560,128]{2,1,0:T(8,128)(2,1)S(1)}, u32[]{:S(2)}, u32[]{:S(2)}) %collective-permute-start.1) | collective-permute-done | bytes 286752 | tf_op jit(solution)/shard_map/ppermute | solution.py:331
  23.8 6.3 %collective-permute-done.2.refs_4_.refs_1_ = bf16[128,1408]{1,0:T(8,128)(2,1)S(1)} collective-permute-done((bf16[128,1408]{1,0:T(8,128)(2,1)}, bf16[128,1408]{1,0:T(8,128)(2,1)S(1)}, u32[]{:S(2)}, u32[]{:S(2)}) %collective-permute-start.2) | collective-permute-done | bytes 360480 | tf_op jit(solution)/shard_map/ppermute | solution.py:358
  30.1 2.1 %collective-permute-done.3.refs_5_.refs_2_ = bf16[128,1408]{1,0:T(8,128)(2,1)S(1)} collective-permute-done((bf16[128,1408]{1,0:T(8,128)(2,1)}, bf16[128,1408]{1,0:T(8,128)(2,1)S(1)}, u32[]{:S(2)}, u32[]{:S(2)}) %collective-permute-start.3) | collective-permute-done | bytes 360480 | tf_op jit(solution)/shard_map/ppermute | solution.py:359
  32.2 1.8 %shard_map.97 = (f32[16,72,112]{2,1,0:T(8,128)}, f32[5,112]{1,0:T(8,128)S(1)}, f32[5,256]{1,0:T(8,128)S(1)}) custom-call(f32[16,40,112]{2,1,0:T(8,128)S(1)} %all-to-all-done.refs_0_, bf16[1120,128]{1,0:T(8,128)(2,1)S(1)} %bitcast.22, bf16[1120,128]{1,0:T(8,128)(2,1)S(1)} %bitcast.25, bf16[2,560,128]{2,1,0:T(8,128)(2,1)S(1)} %collective-permute-done.1.refs_3_, ...), custom_call_target="tpu_custom_call" | custom-call | flops 64225280 | bytes 1670336 | tf_op jit(solution)/shard_map/pallas_call | solution.py:55
  34.0 5.0 %all-to-all-start.1 = ((f32[16,72,112]{2,1,0:T(8,128)}), f32[16,72,112]{2,1,0:T(8,128)S(1)}, u32[]{:S(2)}, u32[]{:S(2)}) async-start(f32[16,72,112]{2,1,0:T(8,128)} %get-tuple-element.34), calls=%async_computation.1 | async-start | bytes 1179648 | tf_op jit(solution)/shard_map/all_to_all | solution.py:334
  39.0 1.9 %collective-permute-start.4 = (bf16[128,1408]{1,0:T(8,128)(2,1)}, bf16[128,1408]{1,0:T(8,128)(2,1)S(1)}, u32[]{:S(2)}, u32[]{:S(2)}) collective-permute-start(bf16[128,1408]{1,0:T(8,128)(2,1)} %get-tuple-element.37), channel_id=1, source_target_pairs={{0,1},{1,0},{2,3},{3,2},{4,5},{5,4},{6,7},{7,6},{8,9},{9,8},{10,11... | collective-permute-start | bytes 1081352 | tf_op jit(solution)/shard_map/ppermute | solution.py:358
  40.9 1.3 %collective-permute-start.5 = (bf16[128,1408]{1,0:T(8,128)(2,1)S(1)}, bf16[128,1408]{1,0:T(8,128)(2,1)S(1)}, u32[]{:S(2)}, u32[]{:S(2)}) collective-permute-start(bf16[128,1408]{1,0:T(8,128)(2,1)S(1)} %copy-done.7), channel_id=1, source_target_pairs={{2,0},{4,2},{6,4},{1,3},{3,5},{5,7},{10,8},{12,10},{14,12},{9,11},... | collective-permute-start | bytes 1081352 | tf_op jit(solution)/shard_map/ppermute | solution.py:359
  42.2 2.1 %shard_map.98 = (bf16[128,1408]{1,0:T(8,128)(2,1)}, f32[8,128]{1,0:T(8,128)S(1)}) custom-call(bf16[128,1408]{1,0:T(8,128)(2,1)S(1)} %copy-done.8, bf16[128,1408]{1,0:T(8,128)(2,1)S(1)} %collective-permute-done.2.refs_4_.refs_1_, bf16[128,1408]{1,0:T(8,128)(2,1)S(1)} %collective-permute-done.3.refs_5_.refs_2_, f32[3,3,2816]{2,1,0:T(4,128)S(1)} %copy-done.6), custom_call_target="tpu_custom_call" | custom-call | flops 3604480 | bytes 1547264 | tf_op jit(solution)/shard_map/pallas_call | solution.py:55
  44.3 9.2 %collective-permute-done.4.refs_6_.refs_1_ = bf16[128,1408]{1,0:T(8,128)(2,1)S(1)} collective-permute-done((bf16[128,1408]{1,0:T(8,128)(2,1)}, bf16[128,1408]{1,0:T(8,128)(2,1)S(1)}, u32[]{:S(2)}, u32[]{:S(2)}) %collective-permute-start.4) | collective-permute-done | bytes 360480 | tf_op jit(solution)/shard_map/ppermute | solution.py:358
  53.6 3.8 %collective-permute-done.5.refs_7_.refs_2_ = bf16[128,1408]{1,0:T(8,128)(2,1)S(1)} collective-permute-done((bf16[128,1408]{1,0:T(8,128)(2,1)S(1)}, bf16[128,1408]{1,0:T(8,128)(2,1)S(1)}, u32[]{:S(2)}, u32[]{:S(2)}) %collective-permute-start.5) | collective-permute-done | bytes 360480 | tf_op jit(solution)/shard_map/ppermute | solution.py:359
  57.3 1.0 %copy-done.10 = bf16[2,560,128]{2,1,0:T(8,128)(2,1)S(1)} copy-done((bf16[2,560,128]{2,1,0:T(8,128)(2,1)S(1)}, bf16[2,560,128]{2,1,0:T(8,128)(2,1)}, u32[]{:S(2)}) %copy-start.10) | copy-done | bytes 286744
  58.3 2.0 %shard_map.99 = (f32[16,40,112]{2,1,0:T(8,128)}, bf16[560,128]{1,0:T(8,128)(2,1)S(1)}, bf16[560,128]{1,0:T(8,128)(2,1)S(1)}) custom-call(f32[16,72,112]{2,1,0:T(8,128)S(1)} %all-to-all-done.1.refs_0_, bf16[1120,128]{1,0:T(8,128)(2,1)S(1)} %bitcast.23, bf16[1120,128]{1,0:T(8,128)(2,1)S(1)} %bitcast.26, bf16[2,560,128]{2,1,0:T(8,128)(2,1)S(1)} %copy-done.10, ...), custom_call_target="tpu_custom_call" | custom-call | flops 64225280 | bytes 1957056 | tf_op jit(solution)/shard_map/pallas_call | solution.py:55
  60.3 0.0 copy-start.13
  60.3 7.6 %all-to-all-start.2 = ((f32[16,40,112]{2,1,0:T(8,128)}), f32[16,40,112]{2,1,0:T(8,128)S(1)}, u32[]{:S(2)}, u32[]{:S(2)}) async-start(f32[16,40,112]{2,1,0:T(8,128)} %get-tuple-element.44), calls=%async_computation.2 | async-start | bytes 655360 | tf_op jit(solution)/shard_map/all_to_all | solution.py:334
  67.9 3.8 %collective-permute-start.7 = (bf16[128,1408]{1,0:T(8,128)(2,1)S(1)}, bf16[128,1408]{1,0:T(8,128)(2,1)S(1)}, u32[]{:S(2)}, u32[]{:S(2)}) collective-permute-start(bf16[128,1408]{1,0:T(8,128)(2,1)S(1)} %collective-permute-done.2.refs_4_.refs_1_), channel_id=1, source_target_pairs={{0,2},{2,4},{4,6},{3,1},{5,3},{7,5},{8,10},{10,12},{12,14},{11,9},... | collective-permute-start | bytes 1081352 | tf_op jit(solution)/shard_map/ppermute | solution.py:362
  71.8 0.1 collective-permute-start.8
  71.8 0.0 copy-start.3
  71.9 0.0 copy-start.5
  71.9 0.0 copy-start.12
  71.9 0.1 collective-permute-start.6
  72.0 4.7 %collective-permute-start.10 = (bf16[128,1408]{1,0:T(8,128)(2,1)S(1)}, bf16[128,1408]{1,0:T(8,128)(2,1)}, u32[]{:S(2)}, u32[]{:S(2)}) collective-permute-start(bf16[128,1408]{1,0:T(8,128)(2,1)S(1)} %collective-permute-done.4.refs_6_.refs_1_), channel_id=1, source_target_pairs={{0,2},{2,4},{4,6},{3,1},{5,3},{7,5},{8,10},{10,12},{12,14},{11,9},... | collective-permute-start | bytes 1081352 | tf_op jit(solution)/shard_map/ppermute | solution.py:362
  76.7 2.1 %shard_map.102 = (bf16[128,1408]{1,0:T(8,128)(2,1)}, f32[8,128]{1,0:T(8,128)S(1)}) custom-call(bf16[128,1408]{1,0:T(8,128)(2,1)S(1)} %copy-done.7, bf16[128,1408]{1,0:T(8,128)(2,1)S(1)} %collective-permute-done.4.refs_6_.refs_1_, bf16[128,1408]{1,0:T(8,128)(2,1)S(1)} %collective-permute-done.5.refs_7_.refs_2_, f32[3,3,2816]{2,1,0:T(4,128)S(1)} %copy-done.6), custom_call_target="tpu_custom_call" | custom-call | flops 3604480 | bytes 1547264 | tf_op jit(solution)/shard_map/pallas_call | solution.py:55
  78.8 0.1 collective-permute-start.11
  78.8 3.3 %collective-permute-done.7.refs_2_ = bf16[128,1408]{1,0:T(8,128)(2,1)S(1)} collective-permute-done((bf16[128,1408]{1,0:T(8,128)(2,1)S(1)}, bf16[128,1408]{1,0:T(8,128)(2,1)S(1)}, u32[]{:S(2)}, u32[]{:S(2)}) %collective-permute-start.7) | collective-permute-done | bytes 360480 | tf_op jit(solution)/shard_map/ppermute | solution.py:362
  82.2 1.6 %collective-permute-done.8.refs_3_ = bf16[128,1408]{1,0:T(8,128)(2,1)S(1)} collective-permute-done((bf16[128,1408]{1,0:T(8,128)(2,1)}, bf16[128,1408]{1,0:T(8,128)(2,1)S(1)}, u32[]{:S(2)}, u32[]{:S(2)}) %collective-permute-start.8) | collective-permute-done | bytes 360480 | tf_op jit(solution)/shard_map/ppermute | solution.py:372
  83.7 2.3 %shard_map.101 = (bf16[1,1,128,5632]{3,2,1,0:T(8,128)(2,1)}, f32[8,128]{1,0:T(8,128)S(1)}) custom-call(bf16[128,1408]{1,0:T(8,128)(2,1)S(1)} %copy-done.8, bf16[128,1408]{1,0:T(8,128)(2,1)S(1)} %collective-permute-done.2.refs_4_.refs_1_, bf16[128,1408]{1,0:T(8,128)(2,1)S(1)} %collective-permute-done.7.refs_2_, ...), custom_call_target="tpu_custom_call" | custom-call | flops 3604480 | bytes 2989056 | tf_op jit(solution)/shard_map/pallas_call | solution.py:55
  86.1 0.7 shard_map.100
  86.8 0.5 shard_map.103
  87.3 0.1 collective-permute-start.9
  87.4 0.7 collective-permute-done.10.refs_2_
  88.1 2.4 %collective-permute-done.11.refs_3_ = bf16[128,1408]{1,0:T(8,128)(2,1)S(1)} collective-permute-done((bf16[128,1408]{1,0:T(8,128)(2,1)}, bf16[128,1408]{1,0:T(8,128)(2,1)S(1)}, u32[]{:S(2)}, u32[]{:S(2)}) %collective-permute-start.11) | collective-permute-done | bytes 360480 | tf_op jit(solution)/shard_map/ppermute | solution.py:372
  90.5 3.4 %shard_map.105 = (bf16[1,1,128,5632]{3,2,1,0:T(8,128)(2,1)}, f32[8,128]{1,0:T(8,128)}) custom-call(bf16[128,1408]{1,0:T(8,128)(2,1)S(1)} %copy-done.7, bf16[128,1408]{1,0:T(8,128)(2,1)S(1)} %collective-permute-done.4.refs_6_.refs_1_, bf16[128,1408]{1,0:T(8,128)(2,1)} %collective-permute-done.10.refs_2_, ...), custom_call_target="tpu_custom_call", output_to_operand_aliasing={{0}: (5, {})} | custom-call | flops 3604480 | bytes 4430848 | tf_op jit(solution)/shard_map/pallas_call | solution.py:55
  93.9 0.9 shard_map.104
  (23 shorter events, 0.0 us)
Async XLA Ops:
  1.6 1.7 %collective-permute-start = (bf16[2,560,128]{2,1,0:T(8,128)(2,1)S(1)}, bf16[2,560,128]{2,1,0:T(8,128)(2,1)S(1)}, u32[]{:S(2)}, u32[]{:S(2)}) collective-permute-start(bf16[2,560,128]{2,1,0:T(8,128)(2,1)S(1)} %shard_map.93), channel_id=1, source_target_pairs={{0,8},{8,0},{1,9},{9,1},{2,10},{10,2},{3,11},{11,3},{4,12},{12,4},... | collective-permute-start | bytes 860168 | tf_op jit(solution)/shard_map/ppermute | solution.py:329
  3.4 1.0 %copy-start.2 = (bf16[1,1,128,1120]{2,3,1,0:T(8,128)(2,1)S(1)}, bf16[1,1,128,1120]{2,3,1,0:T(8,128)(2,1)}, u32[]{:S(2)}) copy-start(bf16[1,1,128,1120]{2,3,1,0:T(8,128)(2,1)} %param.7) | copy-start | bytes 860164
  4.3 1.0 %copy-start.4 = (bf16[1,1,128,1120]{2,3,1,0:T(8,128)(2,1)S(1)}, bf16[1,1,128,1120]{2,3,1,0:T(8,128)(2,1)}, u32[]{:S(2)}) copy-start(bf16[1,1,128,1120]{2,3,1,0:T(8,128)(2,1)} %param.8) | copy-start | bytes 860164
  5.3 1.1 %copy-start.11 = (bf16[2,560,128]{2,1,0:T(8,128)(2,1)}, bf16[2,560,128]{2,1,0:T(8,128)(2,1)S(1)}, u32[]{:S(2)}) copy-start(bf16[2,560,128]{2,1,0:T(8,128)(2,1)S(1)} %collective-permute-done.refs_2_.refs_3_) | copy-start | bytes 860164
  6.4 25.8 %all-to-all-start = ((f32[16,40,112]{2,1,0:T(8,128)}), f32[16,40,112]{2,1,0:T(8,128)S(1)}, u32[]{:S(2)}, u32[]{:S(2)}) async-start(f32[16,40,112]{2,1,0:T(8,128)} %get-tuple-element.30), calls=%async_computation | async-start | bytes 655360 | tf_op jit(solution)/shard_map/all_to_all | solution.py:334
  14.7 17.6 %copy-start = (bf16[1,1,128,1120]{2,3,1,0:T(8,128)(2,1)S(1)}, bf16[1,1,128,1120]{2,3,1,0:T(8,128)(2,1)}, u32[]{:S(2)}) copy-start(bf16[1,1,128,1120]{2,3,1,0:T(8,128)(2,1)} %param.6) | copy-start | bytes 860164
  14.7 17.6 %copy-start.1 = (bf16[1,1,128,1120]{2,3,1,0:T(8,128)(2,1)S(1)}, bf16[1,1,128,1120]{2,3,1,0:T(8,128)(2,1)}, u32[]{:S(2)}) copy-start(bf16[1,1,128,1120]{2,3,1,0:T(8,128)(2,1)} %param.9) | copy-start | bytes 860164
  17.9 12.2 %collective-permute-start.2 = (bf16[128,1408]{1,0:T(8,128)(2,1)}, bf16[128,1408]{1,0:T(8,128)(2,1)S(1)}, u32[]{:S(2)}, u32[]{:S(2)}) collective-permute-start(bf16[128,1408]{1,0:T(8,128)(2,1)} %get-tuple-element.32), channel_id=1, source_target_pairs={{0,1},{1,0},{2,3},{3,2},{4,5},{5,4},{6,7},{7,6},{8,9},{9,8},{10,11... | collective-permute-start | bytes 1081352 | tf_op jit(solution)/shard_map/ppermute | solution.py:358
  19.9 12.4 %collective-permute-start.3 = (bf16[128,1408]{1,0:T(8,128)(2,1)}, bf16[128,1408]{1,0:T(8,128)(2,1)S(1)}, u32[]{:S(2)}, u32[]{:S(2)}) collective-permute-start(bf16[128,1408]{1,0:T(8,128)(2,1)} %get-tuple-element.33.refs_0_), channel_id=1, source_target_pairs={{2,0},{4,2},{6,4},{1,3},{3,5},{5,7},{10,8},{12,10},{14,12},{9,11},... | collective-permute-start | bytes 1081352 | tf_op jit(solution)/shard_map/ppermute | solution.py:359
  22.2 18.8 %copy-start.7 = (bf16[128,1408]{1,0:T(8,128)(2,1)S(1)}, bf16[128,1408]{1,0:T(8,128)(2,1)}, u32[]{:S(2)}) copy-start(bf16[128,1408]{1,0:T(8,128)(2,1)} %get-tuple-element.38.refs_0_) | copy-start | bytes 1081348
  22.2 20.1 %copy-start.6 = (f32[3,3,2816]{2,1,0:T(4,128)S(1)}, f32[3,3,2816]{2,1,0:T(4,128)}, u32[]{:S(2)}) copy-start(f32[3,3,2816]{2,1,0:T(4,128)} %get-tuple-element.39.refs_3_.refs_4_) | copy-start | bytes 304132
  22.2 20.1 %copy-start.8 = (bf16[128,1408]{1,0:T(8,128)(2,1)S(1)}, bf16[128,1408]{1,0:T(8,128)(2,1)}, u32[]{:S(2)}) copy-start(bf16[128,1408]{1,0:T(8,128)(2,1)} %get-tuple-element.33.refs_0_) | copy-start | bytes 1081348
  22.2 1.6 %collective-permute-start.1 = (bf16[2,560,128]{2,1,0:T(8,128)(2,1)S(1)}, bf16[2,560,128]{2,1,0:T(8,128)(2,1)S(1)}, u32[]{:S(2)}, u32[]{:S(2)}) collective-permute-start(bf16[2,560,128]{2,1,0:T(8,128)(2,1)S(1)} %shard_map.95), channel_id=1, source_target_pairs={{0,8},{8,0},{1,9},{9,1},{2,10},{10,2},{3,11},{11,3},{4,12},{12,4},... | collective-permute-start | bytes 860168 | tf_op jit(solution)/shard_map/ppermute | solution.py:331
  23.8 10.2 %copy-start.9 = (bf16[2,560,128]{2,1,0:T(8,128)(2,1)}, bf16[2,560,128]{2,1,0:T(8,128)(2,1)S(1)}, u32[]{:S(2)}) copy-start(bf16[2,560,128]{2,1,0:T(8,128)(2,1)S(1)} %collective-permute-done.1.refs_3_) | copy-start | bytes 860164
  34.0 23.3 %all-to-all-start.1 = ((f32[16,72,112]{2,1,0:T(8,128)}), f32[16,72,112]{2,1,0:T(8,128)S(1)}, u32[]{:S(2)}, u32[]{:S(2)}) async-start(f32[16,72,112]{2,1,0:T(8,128)} %get-tuple-element.34), calls=%async_computation.1 | async-start | bytes 1179648 | tf_op jit(solution)/shard_map/all_to_all | solution.py:334
  39.0 14.5 %collective-permute-start.4 = (bf16[128,1408]{1,0:T(8,128)(2,1)}, bf16[128,1408]{1,0:T(8,128)(2,1)S(1)}, u32[]{:S(2)}, u32[]{:S(2)}) collective-permute-start(bf16[128,1408]{1,0:T(8,128)(2,1)} %get-tuple-element.37), channel_id=1, source_target_pairs={{0,1},{1,0},{2,3},{3,2},{4,5},{5,4},{6,7},{7,6},{8,9},{9,8},{10,11... | collective-permute-start | bytes 1081352 | tf_op jit(solution)/shard_map/ppermute | solution.py:358
  40.9 16.4 %collective-permute-start.5 = (bf16[128,1408]{1,0:T(8,128)(2,1)S(1)}, bf16[128,1408]{1,0:T(8,128)(2,1)S(1)}, u32[]{:S(2)}, u32[]{:S(2)}) collective-permute-start(bf16[128,1408]{1,0:T(8,128)(2,1)S(1)} %copy-done.7), channel_id=1, source_target_pairs={{2,0},{4,2},{6,4},{1,3},{3,5},{5,7},{10,8},{12,10},{14,12},{9,11},... | collective-permute-start | bytes 1081352 | tf_op jit(solution)/shard_map/ppermute | solution.py:359
  57.3 1.0 %copy-start.10 = (bf16[2,560,128]{2,1,0:T(8,128)(2,1)S(1)}, bf16[2,560,128]{2,1,0:T(8,128)(2,1)}, u32[]{:S(2)}) copy-start(bf16[2,560,128]{2,1,0:T(8,128)(2,1)} %copy-done.9) | copy-start | bytes 860164
  60.3 11.5 %copy-start.13 = (bf16[560,128]{1,0:T(8,128)(2,1)}, bf16[560,128]{1,0:T(8,128)(2,1)S(1)}, u32[]{:S(2)}) copy-start(bf16[560,128]{1,0:T(8,128)(2,1)S(1)} %get-tuple-element.42) | copy-start | bytes 430084
  60.3 26.5 %all-to-all-start.2 = ((f32[16,40,112]{2,1,0:T(8,128)}), f32[16,40,112]{2,1,0:T(8,128)S(1)}, u32[]{:S(2)}, u32[]{:S(2)}) async-start(f32[16,40,112]{2,1,0:T(8,128)} %get-tuple-element.44), calls=%async_computation.2 | async-start | bytes 655360 | tf_op jit(solution)/shard_map/all_to_all | solution.py:334
  67.9 14.2 %collective-permute-start.7 = (bf16[128,1408]{1,0:T(8,128)(2,1)S(1)}, bf16[128,1408]{1,0:T(8,128)(2,1)S(1)}, u32[]{:S(2)}, u32[]{:S(2)}) collective-permute-start(bf16[128,1408]{1,0:T(8,128)(2,1)S(1)} %collective-permute-done.2.refs_4_.refs_1_), channel_id=1, source_target_pairs={{0,2},{2,4},{4,6},{3,1},{5,3},{7,5},{8,10},{10,12},{12,14},{11,9},... | collective-permute-start | bytes 1081352 | tf_op jit(solution)/shard_map/ppermute | solution.py:362
  71.8 12.0 %collective-permute-start.8 = (bf16[128,1408]{1,0:T(8,128)(2,1)}, bf16[128,1408]{1,0:T(8,128)(2,1)S(1)}, u32[]{:S(2)}, u32[]{:S(2)}) collective-permute-start(bf16[128,1408]{1,0:T(8,128)(2,1)} %get-tuple-element.45), channel_id=1, source_target_pairs={{0,1},{1,0},{2,3},{3,2},{4,5},{5,4},{6,7},{7,6},{8,9},{9,8},{10,11... | collective-permute-start | bytes 1081352 | tf_op jit(solution)/shard_map/ppermute | solution.py:372
  71.8 15.0 %copy-start.3 = (bf16[1,1,128,1120]{2,3,1,0:T(8,128)(2,1)S(1)}, bf16[1,1,128,1120]{2,3,1,0:T(8,128)(2,1)}, u32[]{:S(2)}) copy-start(bf16[1,1,128,1120]{2,3,1,0:T(8,128)(2,1)} %param.7) | copy-start | bytes 860164
  71.9 15.0 %copy-start.5 = (bf16[1,1,128,1120]{2,3,1,0:T(8,128)(2,1)S(1)}, bf16[1,1,128,1120]{2,3,1,0:T(8,128)(2,1)}, u32[]{:S(2)}) copy-start(bf16[1,1,128,1120]{2,3,1,0:T(8,128)(2,1)} %param.8) | copy-start | bytes 860164
  71.9 14.9 %copy-start.12 = (bf16[2,560,128]{2,1,0:T(8,128)(2,1)S(1)}, bf16[2,560,128]{2,1,0:T(8,128)(2,1)}, u32[]{:S(2)}) copy-start(bf16[2,560,128]{2,1,0:T(8,128)(2,1)} %copy-done.11) | copy-start | bytes 860164
  71.9 14.2 %collective-permute-start.6 = (bf16[560,128]{1,0:T(8,128)(2,1)}, bf16[560,128]{1,0:T(8,128)(2,1)S(1)}, u32[]{:S(2)}, u32[]{:S(2)}) collective-permute-start(bf16[560,128]{1,0:T(8,128)(2,1)} %copy-done.13), channel_id=1, source_target_pairs={{0,8},{8,0},{1,9},{9,1},{2,10},{10,2},{3,11},{11,3},{4,12},{12,4},... | collective-permute-start | bytes 430088 | tf_op jit(solution)/shard_map/ppermute | solution.py:408
  72.0 16.2 %collective-permute-start.10 = (bf16[128,1408]{1,0:T(8,128)(2,1)S(1)}, bf16[128,1408]{1,0:T(8,128)(2,1)}, u32[]{:S(2)}, u32[]{:S(2)}) collective-permute-start(bf16[128,1408]{1,0:T(8,128)(2,1)S(1)} %collective-permute-done.4.refs_6_.refs_1_), channel_id=1, source_target_pairs={{0,2},{2,4},{4,6},{3,1},{5,3},{7,5},{8,10},{10,12},{12,14},{11,9},... | collective-permute-start | bytes 1081352 | tf_op jit(solution)/shard_map/ppermute | solution.py:362
  78.8 11.7 %collective-permute-start.11 = (bf16[128,1408]{1,0:T(8,128)(2,1)}, bf16[128,1408]{1,0:T(8,128)(2,1)S(1)}, u32[]{:S(2)}, u32[]{:S(2)}) collective-permute-start(bf16[128,1408]{1,0:T(8,128)(2,1)} %get-tuple-element.53), channel_id=1, source_target_pairs={{0,1},{1,0},{2,3},{3,2},{4,5},{5,4},{6,7},{7,6},{8,9},{9,8},{10,11... | collective-permute-start | bytes 1081352 | tf_op jit(solution)/shard_map/ppermute | solution.py:372
  87.3 6.6 %collective-permute-start.9 = (bf16[2,560,128]{2,1,0:T(8,128)(2,1)S(1)}, bf16[2,560,128]{2,1,0:T(8,128)(2,1)S(1)}, u32[]{:S(2)}, u32[]{:S(2)}) collective-permute-start(bf16[2,560,128]{2,1,0:T(8,128)(2,1)S(1)} %get-tuple-element.50), channel_id=1, source_target_pairs={{0,8},{8,0},{1,9},{9,1},{2,10},{10,2},{3,11},{11,3},{4,12},{12,4},... | collective-permute-start | bytes 860168 | tf_op jit(solution)/shard_map/ppermute | solution.py:422

commit v6 on v5

--- a/solution.py
+++ b/solution.py
@@ -13,7 +13,10 @@
 EPSILON = 1e-06
 HALF = HEADS // 2
 LANES = 128
-CHUNKS = 2
+CUTS = (0,)
+CHUNKS = 1
+EARLY = 1
+ORDER = [[('near', 0), ('far', 0), ('sent', 0)], [], [('kept', 0)]]
 CHIPS = ("y", "z", "x")
 F32 = jnp.float32
 BF16 = jnp.bfloat16
@@ -93,11 +96,15 @@
     return jnp.sum(dot(stack, mat, dims), axis=0, keepdims=True)
 
 
-def send_half(a_ref, b_ref, send_ref, sems):
-    there = 1 - lax.axis_index("c")
-    size = send_ref.shape[1]
-    part = pl.ds(pl.multiple_of(there * size, 16), size)
-    copy_all([(a_ref.at[part], send_ref.at[0]), (b_ref.at[part], send_ref.at[1])], sems)
+def send_half(a_ref, b_ref, send_ref, own_ref, sems):
+    mine, theirs = halves(send_ref.shape[1])
+    pairs = [
+        (a_ref.at[theirs], send_ref.at[0]),
+        (b_ref.at[theirs], send_ref.at[1]),
+        (a_ref.at[mine], own_ref.at[0]),
+        (b_ref.at[mine], own_ref.at[1]),
+    ]
+    copy_all(pairs, sems)
 
 
 def halves(size):
@@ -121,10 +128,9 @@
         out[theirs] = far[i]
 
 
-def head_of(ref, got, i, h):
-    start = lax.axis_index("c") * (HALF * HD) + h * HD
-    own = ref[pl.ds(pl.multiple_of(start, 16), HD)]
-    return jnp.concatenate([own, got[i, h * HD : (h + 1) * HD]], axis=1)
+def head_of(own, got, i, h):
+    part = slice(h * HD, (h + 1) * HD)
+    return jnp.concatenate([own[i, part], got[i, part]], axis=1)
 
 
 def columns(rows):
@@ -144,11 +150,11 @@
     return total
 
 
-def state_body(n, rows, k_ref, v_ref, kv_got, pay, token, whole):
+def state_body(n, rows, kv, kv_got, pay, token, whole):
     token[...] = jnp.zeros(token.shape, F32)
     for h in range(HALF):
-        key = jnp.maximum(head_of(k_ref, kv_got, 0, h), 0)
-        val = head_of(v_ref, kv_got, 1, h)
+        key = jnp.maximum(head_of(kv, kv_got, 0, h), 0)
+        val = head_of(kv, kv_got, 1, h)
         whole[h * HD : (h + 1) * HD] = dot(key, val, NT)
         norm = dot(jnp.ones((8, key.shape[1]), BF16), key, NT)[:1]
         pay[:, rows + h : rows + h + 1] = spread(norm, n)
@@ -156,12 +162,12 @@
         pay[j, :rows] = whole[j * rows : (j + 1) * rows]
 
 
-def grad_body(n, rows, scale, got, q_ref, g_ref, qg_got, pay, norm_ref, inv_ref, whole):
+def grad_body(n, rows, scale, got, qg, qg_got, pay, norm_ref, inv_ref, whole):
     total = sum_of(got, n, 0, rows + HALF)
     norm_ref[...] = total[rows:]
     for h in range(HALF):
-        query = jnp.maximum(head_of(q_ref, qg_got, 0, h), 0)
-        grad = head_of(g_ref, qg_got, 1, h)
+        query = jnp.maximum(head_of(qg, qg_got, 0, h), 0)
+        grad = head_of(qg, qg_got, 1, h)
         inv = 1.0 / (exact_rows(total[rows + h : rows + h + 1], query, NN) + EPSILON)
         inv_ref[h : h + 1] = inv
         hi, lo = pieces(grad.astype(F32) * (inv * scale))
@@ -173,7 +179,7 @@
 
 
 def query_body(
-    n, rows, scale, got, q_ref, g_ref, qg_got, norm_ref, inv_ref, pay, out_mine, out_theirs, whole
+    n, rows, scale, got, qg, qg_got, norm_ref, inv_ref, pay, out_mine, out_theirs, whole
 ):
     total = sum_of(got, n, rows, 2 * rows)
     for j in range(n):
@@ -183,9 +189,9 @@
     tok = out_mine.shape[1]
     for h in range(HALF):
         part = slice(h * HD, (h + 1) * HD)
-        feat = jnp.maximum(head_of(q_ref, qg_got, 0, h), 0)
+        feat = jnp.maximum(head_of(qg, qg_got, 0, h), 0)
         query = feat.astype(F32)
-        grad = head_of(g_ref, qg_got, 1, h)
+        grad = head_of(qg, qg_got, 1, h)
         hi, lo = pieces(whole[part])
         prod = dot(hi, grad, NN) + dot(lo, grad, NN)
         inv = inv_ref[h : h + 1]
@@ -198,15 +204,15 @@
         out_theirs[part] = out[:, tok:]
 
 
-def key_body(n, rows, got, k_ref, v_ref, kv_got, out_mine, out_theirs, whole):
+def key_body(n, rows, got, kv, kv_got, out_mine, out_theirs, whole):
     for j in range(n):
         whole[j * rows : (j + 1) * rows] = got[j, :rows]
     norms = columns(sum_of(got, n, rows, rows + HALF))
     tok = out_mine.shape[2]
     for h in range(HALF):
         part = slice(h * HD, (h + 1) * HD)
-        key = head_of(k_ref, kv_got, 0, h)
-        val = head_of(v_ref, kv_got, 1, h)
+        key = head_of(kv, kv_got, 0, h)
+        val = head_of(kv, kv_got, 1, h)
         hi, lo = pieces(whole[part])
         k_out = dot(hi, val, NN) + dot(lo, val, NN) + norms[:HD, h : h + 1]
         k_out = jnp.where(key.astype(F32) > 0, k_out, 0.0).astype(BF16)
@@ -225,11 +231,11 @@
     return jnp.where(rows == edge, 0.0, moved)
 
 
-def taps(sources, weight, picks, lanes, near):
+def taps(sources, weight, picks, lanes):
     planes = [ref[:, lanes].astype(F32) for ref in sources]
 
     def column(j):
-        return sum(p * weight[i, pl.ds(j, 1), near] for p, i in zip(planes, picks))
+        return sum(p * weight[i, pl.ds(j, 1), lanes] for p, i in zip(planes, picks))
 
     return (column(1) + shift(column(0), -1) + shift(column(2), 1)).astype(BF16)
 
@@ -238,22 +244,19 @@
     return pl.ds(pl.multiple_of(start, LANES), width)
 
 
-def halve_body(row, weight, *refs):
-    outs, token, held, sems = refs[:5], refs[5], refs[6:11], refs[11]
+def halve_body(at, row, weight, send, mine, weight_mine, token, sems):
     token[...] = jnp.zeros(token.shape, F32)
     side = lax.axis_index("x")
-    width = outs[0].shape[1]
-    pairs = []
-    for i in range(CHUNKS):
-        send = columns_at((1 - side) * CHUNKS * width + i * width, width)
-        mine = columns_at(side * CHUNKS * width + i * width, width)
-        pairs += [row.at[0, 0, :, send], row.at[0, 0, :, mine]]
-    pairs.append(weight.at[:, :, columns_at(side * CHUNKS * width, CHUNKS * width)])
-    copy_all(list(zip(pairs, held)), sems)
-    copy_all(list(zip(held, outs)), sems)
-
-
-def send_body(at, mine, got, far, weight, out, token, *held):
+    half, width = row.shape[3] // 2, mine.shape[1]
+    pairs = [
+        row.at[0, 0, :, columns_at((1 - side) * half + at, width)],
+        row.at[0, 0, :, columns_at(side * half + at, width)],
+        weight.at[:, :, columns_at(side * half + at, width)],
+    ]
+    copy_all(list(zip(pairs, (send, mine, weight_mine))), sems)
+
+
+def send_body(mine, got, far, weight, out, token, *held):
     *held, made, sems = held
     token[...] = jnp.zeros(token.shape, F32)
     copy_all(list(zip((mine, got, far, weight), held)), sems)
@@ -264,8 +267,7 @@
     @pl.loop(0, width // LANES)
     def _(t):
         lanes = columns_at(t * LANES, LANES)
-        near = columns_at(at + t * LANES, LANES)
-        made[:, lanes] = taps((got, mine, far), weight, (1, 2 - 2 * side, 2 * side), lanes, near)
+        made[:, lanes] = taps((got, mine, far), weight, (1, 2 - 2 * side, 2 * side), lanes)
 
     copy_all([(made, out)], sems)
 
@@ -282,11 +284,11 @@
     @pl.loop(0, width // LANES)
     def _(t):
         lanes = columns_at(t * LANES, LANES)
-        near = columns_at(at + t * LANES, LANES)
-        made[:, lanes] = taps((mine, got, far), weight, (1, 2 * side, 2 - 2 * side), lanes, near)
-
-    here = columns_at(side * CHUNKS * width + at, width)
-    there = columns_at((1 - side) * CHUNKS * width + at, width)
+        made[:, lanes] = taps((mine, got, far), weight, (1, 2 * side, 2 - 2 * side), lanes)
+
+    half = out.shape[3] // 2
+    here = columns_at(side * half + at, width)
+    there = columns_at((1 - side) * half + at, width)
     copy_all([(made, out.at[0, 0, :, here]), (back, out.at[0, 0, :, there])], sems)
 
 
@@ -299,7 +301,6 @@
     pay_one = -(-(rows + HALF) // 8) * 8
     pay_two = -(-2 * rows // 8) * 8
     swap = [(0, 1), (1, 0)]
-    two_sems = [pltpu.SemaphoreType.DMA((2,))]
     sd = jax.ShapeDtypeStruct
     scratch = [pltpu.VMEM((n * rows, HD), F32)]
     half = HALF * HD
@@ -316,18 +317,80 @@
     odd_up = [(2 * i + 1, 2 * j + 1) for i, j in ahead]
     odd_down = [(2 * j + 1, 2 * i + 1) for i, j in ahead]
     cols, ch = conv_grad.shape[2:]
-    width = ch // (2 * CHUNKS)
-    half_shape = sd((cols, width), BF16)
+    tiles = ch // (2 * LANES)
+    cuts = [tiles * part // 22 for part in CUTS] + [tiles]
+    starts = [LANES * c for c in cuts[:-1]]
+    widths = [LANES * (d - c) for c, d in zip(cuts, cuts[1:])]
     token = sd((8, LANES), F32)
-    held = [pltpu.VMEM((cols, width), BF16)]
-    held_weight = [pltpu.VMEM((3, 3, CHUNKS * width), F32)]
+
+    def hold(i, count):
+        return [pltpu.VMEM((cols, widths[i]), BF16)] * count
+
+    def hold_weight(i):
+        return [pltpu.VMEM((3, 3, widths[i]), F32)]
 
     def sems(count):
         return [pltpu.SemaphoreType.DMA((count,))]
 
-    kv_send = call(send_half, [pair_shape], (held_in_hbm(k), held_in_hbm(v)), two_sems, any_in=True)[0]
+    def halve(i, after):
+        return call(
+            functools.partial(halve_body, starts[i]),
+            [sd((cols, widths[i]), BF16)] * 2 + [sd((3, 3, widths[i]), F32), token],
+            (held_in_hbm(conv_grad), held_in_hbm(conv_weight)),
+            sems(3),
+            after=after,
+            any_in=True,
+        )
+
+    def move_in(i):
+        near = lax.ppermute(row_send[i], "x", swap)
+        return held_in_hbm(near), held_in_hbm(lax.ppermute(row_mine[i], ("z", "x"), even_down + odd_up))
+
+    def send_out(i):
+        return call(
+            send_body,
+            [sd((cols, widths[i]), BF16), token],
+            (row_mine[i], near[i], far[i], weight[i]),
+            hold(i, 3) + hold_weight(i) + hold(i, 1) + sems(4),
+            flops=20 * cols * widths[i],
+            any_in=True,
+            hbm_out=1,
+        )
+
+    def finish(i, before=()):
+        return call(
+            functools.partial(keep_body, starts[i]),
+            [sd(conv_grad.shape, BF16), token],
+            (row_mine[i], near[i], onward[i], back[i], weight[i], *before),
+            hold(i, 4) + hold_weight(i) + hold(i, 1) + sems(5),
+            flops=20 * cols * widths[i],
+            any_in=True,
+            hbm_out=1,
+            alias={5: 0} if before else None,
+        )
+
+    row_mine, row_send, weight, halved, near, far = {}, {}, {}, {}, {}, {}
+    sent, onward, back, kept = {}, {}, {}, {}
+    for i in range(CHUNKS):
+        row_send[i], row_mine[i], weight[i], halved[i] = halve(i, ())
+        near[i], far[i] = move_in(i)
+        onward[i] = lax.ppermute(near[i], ("z", "x"), even_up + odd_down)
+        out_send, sent[i] = send_out(i)
+        back[i] = lax.ppermute(out_send, "x", swap)
+        input_grad, kept[i] = finish(i, (input_grad,) if i else ())
+    def part(first, second, after=()):
+        return call(
+            send_half,
+            [pair_shape] * 2,
+            (held_in_hbm(first), held_in_hbm(second)),
+            sems(4),
+            after=after,
+            any_in=True,
+        )
+
+    kv_send, kv = part(k, v, (halved[0],))
     kv_got = lax.ppermute(kv_send, "c", swap)
-    qg_send = call(send_half, [pair_shape], (held_in_hbm(q), held_in_hbm(g)), two_sems, any_in=True)[0]
+    qg_send, qg = part(q, g)
     qg_got = lax.ppermute(qg_send, "c", swap)
 
     def exchange(pay):
@@ -337,90 +400,49 @@
     pay, started = call(
         functools.partial(state_body, n, rows),
         [sd((n, pay_one, HD), F32), token],
-        (k, v, kv_got),
+        (kv, kv_got),
         scratch,
         flops=2 * macs,
         pinned=True,
     )
     got = exchange(pay)
-    *parts, weight, halved = call(
-        halve_body,
-        [half_shape] * (2 * CHUNKS) + [sd((3, 3, CHUNKS * width), F32), token],
-        (held_in_hbm(conv_grad), held_in_hbm(conv_weight)),
-        held * (2 * CHUNKS) + held_weight + sems(5),
-        after=(started,),
-        any_in=True,
-        hbm_out=5,
-    )
-    row_send, row_mine = parts[::2], parts[1::2]
-
-    def move_in(i):
-        near = lax.ppermute(row_send[i], "x", swap)
-        return near, lax.ppermute(row_mine[i], ("z", "x"), even_down + odd_up)
-
-    def move_on(i, near, far):
-        onward = lax.ppermute(near, ("z", "x"), even_up + odd_down)
-        out_send, sent = call(
-            functools.partial(send_body, i * width),
-            [half_shape, token],
-            (row_mine[i], near, far, weight),
-            held * 3 + held_weight + held + sems(4),
-            flops=20 * cols * width,
-            any_in=True,
-            hbm_out=1,
-        )
-        return onward, lax.ppermute(out_send, "x", swap), sent
-
-    def finish(i, near, onward, back, before=()):
-        return call(
-            functools.partial(keep_body, i * width),
-            [sd(conv_grad.shape, BF16), token],
-            (row_mine[i], near, onward, back, weight, *before),
-            held * 4 + held_weight + held + sems(5),
-            flops=20 * cols * width,
-            any_in=True,
-            hbm_out=1,
-            alias={5: 0} if before else None,
-        )
-
-    near_a, far_a = move_in(0)
+    ties = {"near": near, "far": far, "sent": sent, "kept": kept, "halved": halved}
+
+    def tied(stage):
+        return tuple(ties[name][i] for name, i in ORDER[stage])
+
     pay, norm, inv = call(
         functools.partial(grad_body, n, rows, scale),
         [sd((n, pay_two, HD), F32), sd((HALF, HD), F32), sd((HALF, 2 * tok), F32)],
-        (got, q, g, qg_got),
+        (got, qg, qg_got),
         scratch,
         flops=4 * macs,
         pinned=True,
-        after=(near_a, far_a),
-    )
-    near_b, far_b = move_in(1)
-    onward_a, back_a, sent_a = move_on(0, near_a, far_a)
+        after=tied(0),
+    )
     got = exchange(pay)
     pay, query_mine, query_send = call(
         functools.partial(query_body, n, rows, scale),
         [sd((n, pay_one, HD), F32)] + [sd((half, tok), BF16)] * 2,
-        (got, q, g, qg_got, norm, inv),
+        (got, qg, qg_got, norm, inv),
         scratch,
         flops=4 * macs,
         pinned=True,
-        after=(near_b, far_b, sent_a),
+        after=tied(1),
     )
     query_got = lax.ppermute(query_send, "c", swap)
-    onward_b, back_b, sent_b = move_on(1, near_b, far_b)
-    input_grad, kept = finish(0, near_a, onward_a, back_a)
     whole_shape = sd((2 * half, tok), BF16)
     query_out, merged = call(merge_query, [whole_shape, token], (query_mine, query_got))
     got = exchange(pay)
     key_mine, key_send = call(
         functools.partial(key_body, n, rows),
         [pair_shape] * 2,
-        (got, k, v, kv_got),
+        (got, kv, kv_got),
         scratch,
         flops=8 * macs,
-        after=(kept, merged, sent_b),
+        after=(merged, *tied(2)),
     )
     key_got = lax.ppermute(key_send, "c", swap)
-    input_grad, _ = finish(1, near_b, onward_b, back_b, (input_grad,))
     outs = query_out, *call(merge_pair, [whole_shape] * 2, (key_mine, key_got))
     outs = [jnp.swapaxes(o.reshape(*queries.shape[:2], 2 * half, -1), 2, 3) for o in outs]
     return (*outs, input_grad)

time: 95.6 us -> 82.7 us (0.87)
  starting transfers between devices: 36.8 us -> 25.2 us
  waiting for transfers between devices: 32.1 us -> 36.4 us
  Pallas kernels: 22 us -> 19.1 us
  local copies, waits for them, and re-layouts: 2.94 us -> 0.65 us
    all_to_all x3, waiting for transfers between devices: 0.01 us -> 22.1 us  [exchange(): return lax.all_to_all(pay, CHIPS, split_axis=0, concat_axis=0, tiled=True)]
    ppermute x2 -> x1, waiting for transfers between devices: 15.5 us -> 6.64 us  [move_in(): near = lax.ppermute(row_send[i], 'x', swap)]
    ppermute x6 -> x3, waiting for transfers between devices: 13.9 us -> 6.08 us  [the longest x1 3.67 us: shards(): onward[i] = lax.ppermute(near[i], ('z', 'x'), even_up + odd_down)]
    ppermute x6 -> x3, starting transfers between devices: 11.3 us -> 6.01 us  [the longest x1 4.72 us: shards(): onward[i] = lax.ppermute(near[i], ('z', 'x'), even_up + odd_down)]
    all_to_all x3, starting transfers between devices: 20.8 us -> 15.9 us  [exchange(): return lax.all_to_all(pay, CHIPS, split_axis=0, concat_axis=0, tiled=True)]
    pallas_call x13 -> x11, Pallas kernels: 22 us -> 19.1 us  [call(): pl.pallas_call(ordered, out_shape=shapes, in_specs=[free if any_in else f...]
    unnamed x28 -> x2, local copies, waits for them, and re-layouts: 2.94 us -> 0.65 us
    ppermute x1, waiting for transfers between devices: 1.56 us -> 0.01 us  [shards(): qg_got = lax.ppermute(qg_send, 'c', swap)]
  transfers between devices with their start and end apart: 15 -> 11, of which waited for: 10 -> 7; matrix products, arithmetic and copies ran while one was open for 0% -> 0% of each run, Pallas kernels for 16% -> 16%
where the time goes in v6:
time: 82.7 us; the launch traced here: 82.1 us
  waiting for transfers between devices  36.4 us (44%)
  starting transfers between devices  25.2 us (30%)
  Pallas kernels  19.1 us (23%)
    all_to_all x3, waiting for transfers between devices, exchange(): return lax.all_to_all(pay, CHIPS, split_axis=0, concat_axis=0, tiled=True)  22.1 us
    pallas_call x11, Pallas kernels, call(): pl.pallas_call(ordered, out_shape=shapes, in_specs=[free if any_in else f...  19.1 us
    all_to_all x3, starting transfers between devices, exchange(): return lax.all_to_all(pay, CHIPS, split_axis=0, concat_axis=0, tiled=True)  15.9 us
    ppermute x1, waiting for transfers between devices, move_in(): near = lax.ppermute(row_send[i], 'x', swap)  6.64 us
    ppermute x1, starting transfers between devices, shards(): onward[i] = lax.ppermute(near[i], ('z', 'x'), even_up + odd_down)  4.72 us
    ppermute x1, waiting for transfers between devices, shards(): onward[i] = lax.ppermute(near[i], ('z', 'x'), even_up + odd_down)  3.67 us
    ppermute x1, starting transfers between devices, move_in(): near = lax.ppermute(row_send[i], 'x', swap)  2.56 us
    ppermute x1, waiting for transfers between devices, move_in(): lax.ppermute(row_mine[i], ('z', 'x'), even_down + odd_up)  2.4 us
  transfers between devices with their start and end apart: 11, of which 7 were waited for; matrix products, arithmetic and copies ran while one was open for 0% of the time, Pallas kernels for 16%

profile of v6, /device:TPU:0, one launch (start us, length us, event | category | flops | bytes accessed | tf_op | source)
XLA Modules:
  0.0 82.1 jit_solution(10121038375402795334)
XLA Ops:
  0.6 1.4 %shard_map.93 = (bf16[128,2816]{1,0:T(8,128)(2,1)S(1)}, bf16[128,2816]{1,0:T(8,128)(2,1)S(1)}, f32[3,3,2816]{2,1,0:T(4,128)S(1)}, f32[8,128]{1,0:T(8,128)S(1)}) custom-call(bf16[1,1,128,5632]{3,2,1,0:T(8,128)(2,1)} %refs_0_.1, f32[3,3,5632]{2,1,0:T(4,128)} %refs_1_.1), custom_call_target="tpu_custom_call" | custom-call | bytes 3191808 | tf_op jit(solution)/shard_map/pallas_call | solution.py:58
  2.0 1.2 %shard_map.94 = (bf16[2,560,128]{2,1,0:T(8,128)(2,1)S(1)}, bf16[2,560,128]{2,1,0:T(8,128)(2,1)S(1)}) custom-call(bf16[1120,128]{1,0:T(8,128)(2,1)} %bitcast.21, bf16[1120,128]{1,0:T(8,128)(2,1)} %bitcast.22, f32[8,128]{1,0:T(8,128)S(1)} %get-tuple-element.29.refs_2_), custom_call_target="tpu_custom_call" | custom-call | bytes 1146880 | tf_op jit(solution)/shard_map/pallas_call | solution.py:58
  3.2 0.5 collective-permute-start
  3.7 2.6 %collective-permute-start.2 = (bf16[128,2816]{1,0:T(8,128)(2,1)S(1)}, bf16[128,2816]{1,0:T(8,128)(2,1)}, u32[]{:S(2)}, u32[]{:S(2)}) collective-permute-start(bf16[128,2816]{1,0:T(8,128)(2,1)S(1)} %get-tuple-element.35), channel_id=1, source_target_pairs={{0,1},{1,0},{2,3},{3,2},{4,5},{5,4},{6,7},{7,6},{8,9},{9,8},{10,11... | collective-permute-start | bytes 2162696 | tf_op jit(solution)/shard_map/ppermute | solution.py:346
  6.3 1.3 %collective-permute-start.3 = (bf16[128,2816]{1,0:T(8,128)(2,1)S(1)}, bf16[128,2816]{1,0:T(8,128)(2,1)}, u32[]{:S(2)}, u32[]{:S(2)}) collective-permute-start(bf16[128,2816]{1,0:T(8,128)(2,1)S(1)} %get-tuple-element.36.refs_0_), channel_id=1, source_target_pairs={{2,0},{4,2},{6,4},{1,3},{3,5},{5,7},{10,8},{12,10},{14,12},{9,11},... | collective-permute-start | bytes 2162696 | tf_op jit(solution)/shard_map/ppermute | solution.py:347
  7.6 0.0 collective-permute-done.refs_1_.refs_2_
  7.6 1.7 %shard_map.95 = (f32[16,40,112]{2,1,0:T(8,128)}, f32[8,128]{1,0:T(8,128)}) custom-call(bf16[2,560,128]{2,1,0:T(8,128)(2,1)S(1)} %get-tuple-element.30.refs_0_.refs_1_, bf16[2,560,128]{2,1,0:T(8,128)(2,1)S(1)} %collective-permute-done.refs_1_.refs_2_), custom_call_target="tpu_custom_call" | custom-call | flops 32112640 | bytes 864256 | tf_op jit(solution)/shard_map/pallas_call | solution.py:58
  9.3 7.9 %all-to-all-start = ((f32[16,40,112]{2,1,0:T(8,128)}), f32[16,40,112]{2,1,0:T(8,128)S(1)}, u32[]{:S(2)}, u32[]{:S(2)}) async-start(f32[16,40,112]{2,1,0:T(8,128)} %get-tuple-element.32), calls=%async_computation | async-start | bytes 655360 | tf_op jit(solution)/shard_map/all_to_all | solution.py:397
  17.2 1.2 %shard_map.96 = (bf16[2,560,128]{2,1,0:T(8,128)(2,1)S(1)}, bf16[2,560,128]{2,1,0:T(8,128)(2,1)S(1)}) custom-call(bf16[1120,128]{1,0:T(8,128)(2,1)} %bitcast.23, bf16[1120,128]{1,0:T(8,128)(2,1)} %bitcast.24), custom_call_target="tpu_custom_call" | custom-call | bytes 1146880 | tf_op jit(solution)/shard_map/pallas_call | solution.py:58
  18.3 0.1 collective-permute-start.1
  18.4 6.6 %collective-permute-done.2.refs_1_.refs_3_ = bf16[128,2816]{1,0:T(8,128)(2,1)} collective-permute-done((bf16[128,2816]{1,0:T(8,128)(2,1)S(1)}, bf16[128,2816]{1,0:T(8,128)(2,1)}, u32[]{:S(2)}, u32[]{:S(2)}) %collective-permute-start.2) | collective-permute-done | bytes 720928 | tf_op jit(solution)/shard_map/ppermute | solution.py:346
  25.1 2.4 %collective-permute-done.3.refs_2_.refs_4_ = bf16[128,2816]{1,0:T(8,128)(2,1)} collective-permute-done((bf16[128,2816]{1,0:T(8,128)(2,1)S(1)}, bf16[128,2816]{1,0:T(8,128)(2,1)}, u32[]{:S(2)}, u32[]{:S(2)}) %collective-permute-start.3) | collective-permute-done | bytes 720928 | tf_op jit(solution)/shard_map/ppermute | solution.py:347
  27.5 3.8 %shard_map.97 = (bf16[128,2816]{1,0:T(8,128)(2,1)}, f32[8,128]{1,0:T(8,128)S(1)}) custom-call(bf16[128,2816]{1,0:T(8,128)(2,1)S(1)} %get-tuple-element.36.refs_0_, bf16[128,2816]{1,0:T(8,128)(2,1)} %collective-permute-done.2.refs_1_.refs_3_, bf16[128,2816]{1,0:T(8,128)(2,1)} %collective-permute-done.3.refs_2_.refs_4_, ...), custom_call_target="tpu_custom_call" | custom-call | flops 7208960 | bytes 2989056 | tf_op jit(solution)/shard_map/pallas_call | solution.py:58
  31.3 0.0 collective-permute-done.1.refs_2_
  31.3 3.3 %all-to-all-done.refs_0_ = f32[16,40,112]{2,1,0:T(8,128)S(1)} async-done(((f32[16,40,112]{2,1,0:T(8,128)}), f32[16,40,112]{2,1,0:T(8,128)S(1)}, u32[]{:S(2)}, u32[]{:S(2)}) %all-to-all-start) | async-done | bytes 286752 | tf_op jit(solution)/shard_map/all_to_all | solution.py:397
  34.6 1.8 %shard_map.98 = (f32[16,72,112]{2,1,0:T(8,128)}, f32[5,112]{1,0:T(8,128)S(1)}, f32[5,256]{1,0:T(8,128)S(1)}) custom-call(f32[16,40,112]{2,1,0:T(8,128)S(1)} %all-to-all-done.refs_0_, bf16[2,560,128]{2,1,0:T(8,128)(2,1)S(1)} %get-tuple-element.33.refs_1_, bf16[2,560,128]{2,1,0:T(8,128)(2,1)S(1)} %collective-permute-done.1.refs_2_, ...), custom_call_target="tpu_custom_call" | custom-call | flops 64225280 | bytes 1383616 | tf_op jit(solution)/shard_map/pallas_call | solution.py:58
  36.4 4.4 %all-to-all-start.1 = ((f32[16,72,112]{2,1,0:T(8,128)}), f32[16,72,112]{2,1,0:T(8,128)S(1)}, u32[]{:S(2)}, u32[]{:S(2)}) async-start(f32[16,72,112]{2,1,0:T(8,128)} %get-tuple-element.39), calls=%async_computation.1 | async-start | bytes 1179648 | tf_op jit(solution)/shard_map/all_to_all | solution.py:397
  40.8 4.7 %collective-permute-start.5 = (bf16[128,2816]{1,0:T(8,128)(2,1)}, bf16[128,2816]{1,0:T(8,128)(2,1)}, u32[]{:S(2)}, u32[]{:S(2)}) collective-permute-start(bf16[128,2816]{1,0:T(8,128)(2,1)} %collective-permute-done.2.refs_1_.refs_3_), channel_id=1, source_target_pairs={{0,2},{2,4},{4,6},{3,1},{5,3},{7,5},{8,10},{10,12},{12,14},{11,9},... | collective-permute-start | bytes 2162696 | tf_op jit(solution)/shard_map/ppermute | solution.py:377
  45.5 0.0 collective-permute-start.6
  45.5 11.6 %all-to-all-done.1.refs_0_ = f32[16,72,112]{2,1,0:T(8,128)S(1)} async-done(((f32[16,72,112]{2,1,0:T(8,128)}), f32[16,72,112]{2,1,0:T(8,128)S(1)}, u32[]{:S(2)}, u32[]{:S(2)}) %all-to-all-start.1) | async-done | bytes 516128 | tf_op jit(solution)/shard_map/all_to_all | solution.py:397
  57.1 2.0 %shard_map.99 = (f32[16,40,112]{2,1,0:T(8,128)}, bf16[560,128]{1,0:T(8,128)(2,1)S(1)}, bf16[560,128]{1,0:T(8,128)(2,1)S(1)}) custom-call(f32[16,72,112]{2,1,0:T(8,128)S(1)} %all-to-all-done.1.refs_0_, bf16[2,560,128]{2,1,0:T(8,128)(2,1)S(1)} %get-tuple-element.33.refs_1_, bf16[2,560,128]{2,1,0:T(8,128)(2,1)S(1)} %collective-permute-done.1.refs_2_, ...), custom_call_target="tpu_custom_call" | custom-call | flops 64225280 | bytes 1670336 | tf_op jit(solution)/shard_map/pallas_call | solution.py:58
  59.0 0.0 copy-start
  59.0 0.7 copy-done
  59.7 3.6 %all-to-all-start.2 = ((f32[16,40,112]{2,1,0:T(8,128)}), f32[16,40,112]{2,1,0:T(8,128)S(1)}, u32[]{:S(2)}, u32[]{:S(2)}) async-start(f32[16,40,112]{2,1,0:T(8,128)} %get-tuple-element.45), calls=%async_computation.2 | async-start | bytes 655360 | tf_op jit(solution)/shard_map/all_to_all | solution.py:397
  63.3 0.1 collective-permute-start.4
  63.4 3.7 %collective-permute-done.5.refs_2_ = bf16[128,2816]{1,0:T(8,128)(2,1)} collective-permute-done((bf16[128,2816]{1,0:T(8,128)(2,1)}, bf16[128,2816]{1,0:T(8,128)(2,1)}, u32[]{:S(2)}, u32[]{:S(2)}) %collective-permute-start.5) | collective-permute-done | bytes 720928 | tf_op jit(solution)/shard_map/ppermute | solution.py:377
  67.1 0.0 collective-permute-done.6.refs_3_
  67.1 4.1 %shard_map.101 = (bf16[1,1,128,5632]{3,2,1,0:T(8,128)(2,1)}, f32[8,128]{1,0:T(8,128)S(1)}) custom-call(bf16[128,2816]{1,0:T(8,128)(2,1)S(1)} %get-tuple-element.36.refs_0_, bf16[128,2816]{1,0:T(8,128)(2,1)} %collective-permute-done.2.refs_1_.refs_3_, bf16[128,2816]{1,0:T(8,128)(2,1)} %collective-permute-done.5.refs_2_, ...), custom_call_target="tpu_custom_call" | custom-call | flops 7208960 | bytes 4430848 | tf_op jit(solution)/shard_map/pallas_call | solution.py:58
  71.2 0.0 collective-permute-done.4.refs_1_
  71.2 0.7 shard_map.100
  71.9 7.2 %all-to-all-done.2.refs_0_ = f32[16,40,112]{2,1,0:T(8,128)S(1)} async-done(((f32[16,40,112]{2,1,0:T(8,128)}), f32[16,40,112]{2,1,0:T(8,128)S(1)}, u32[]{:S(2)}, u32[]{:S(2)}) %all-to-all-start.2) | async-done | bytes 286752 | tf_op jit(solution)/shard_map/all_to_all | solution.py:397
  79.2 0.5 shard_map.102
  79.6 0.1 collective-permute-start.7
  79.7 1.6 %collective-permute-done.7.refs_1_ = bf16[2,560,128]{2,1,0:T(8,128)(2,1)S(1)} collective-permute-done((bf16[2,560,128]{2,1,0:T(8,128)(2,1)S(1)}, bf16[2,560,128]{2,1,0:T(8,128)(2,1)S(1)}, u32[]{:S(2)}, u32[]{:S(2)}) %collective-permute-start.7) | collective-permute-done | bytes 286752 | tf_op jit(solution)/shard_map/ppermute | solution.py:445
  81.3 0.9 %shard_map.103 = (bf16[1120,128]{1,0:T(8,128)(2,1)}, bf16[1120,128]{1,0:T(8,128)(2,1)}) custom-call(bf16[2,560,128]{2,1,0:T(8,128)(2,1)S(1)} %get-tuple-element.49.refs_0_, bf16[2,560,128]{2,1,0:T(8,128)(2,1)S(1)} %collective-permute-done.7.refs_1_), custom_call_target="tpu_custom_call" | custom-call | bytes 1146880 | tf_op jit(solution)/shard_map/pallas_call | solution.py:58
Async XLA Ops:
  3.2 4.4 %collective-permute-start = (bf16[2,560,128]{2,1,0:T(8,128)(2,1)S(1)}, bf16[2,560,128]{2,1,0:T(8,128)(2,1)S(1)}, u32[]{:S(2)}, u32[]{:S(2)}) collective-permute-start(bf16[2,560,128]{2,1,0:T(8,128)(2,1)S(1)} %get-tuple-element.31), channel_id=1, source_target_pairs={{0,8},{8,0},{1,9},{9,1},{2,10},{10,2},{3,11},{11,3},{4,12},{12,4},... | collective-permute-start | bytes 860168 | tf_op jit(solution)/shard_map/ppermute | solution.py:392
  3.7 21.4 %collective-permute-start.2 = (bf16[128,2816]{1,0:T(8,128)(2,1)S(1)}, bf16[128,2816]{1,0:T(8,128)(2,1)}, u32[]{:S(2)}, u32[]{:S(2)}) collective-permute-start(bf16[128,2816]{1,0:T(8,128)(2,1)S(1)} %get-tuple-element.35), channel_id=1, source_target_pairs={{0,1},{1,0},{2,3},{3,2},{4,5},{5,4},{6,7},{7,6},{8,9},{9,8},{10,11... | collective-permute-start | bytes 2162696 | tf_op jit(solution)/shard_map/ppermute | solution.py:346
  6.3 21.2 %collective-permute-start.3 = (bf16[128,2816]{1,0:T(8,128)(2,1)S(1)}, bf16[128,2816]{1,0:T(8,128)(2,1)}, u32[]{:S(2)}, u32[]{:S(2)}) collective-permute-start(bf16[128,2816]{1,0:T(8,128)(2,1)S(1)} %get-tuple-element.36.refs_0_), channel_id=1, source_target_pairs={{2,0},{4,2},{6,4},{1,3},{3,5},{5,7},{10,8},{12,10},{14,12},{9,11},... | collective-permute-start | bytes 2162696 | tf_op jit(solution)/shard_map/ppermute | solution.py:347
  9.3 25.4 %all-to-all-start = ((f32[16,40,112]{2,1,0:T(8,128)}), f32[16,40,112]{2,1,0:T(8,128)S(1)}, u32[]{:S(2)}, u32[]{:S(2)}) async-start(f32[16,40,112]{2,1,0:T(8,128)} %get-tuple-element.32), calls=%async_computation | async-start | bytes 655360 | tf_op jit(solution)/shard_map/all_to_all | solution.py:397
  18.3 13.0 %collective-permute-start.1 = (bf16[2,560,128]{2,1,0:T(8,128)(2,1)S(1)}, bf16[2,560,128]{2,1,0:T(8,128)(2,1)S(1)}, u32[]{:S(2)}, u32[]{:S(2)}) collective-permute-start(bf16[2,560,128]{2,1,0:T(8,128)(2,1)S(1)} %get-tuple-element.34), channel_id=1, source_target_pairs={{0,8},{8,0},{1,9},{9,1},{2,10},{10,2},{3,11},{11,3},{4,12},{12,4},... | collective-permute-start | bytes 860168 | tf_op jit(solution)/shard_map/ppermute | solution.py:394
  36.4 20.7 %all-to-all-start.1 = ((f32[16,72,112]{2,1,0:T(8,128)}), f32[16,72,112]{2,1,0:T(8,128)S(1)}, u32[]{:S(2)}, u32[]{:S(2)}) async-start(f32[16,72,112]{2,1,0:T(8,128)} %get-tuple-element.39), calls=%async_computation.1 | async-start | bytes 1179648 | tf_op jit(solution)/shard_map/all_to_all | solution.py:397
  40.8 26.3 %collective-permute-start.5 = (bf16[128,2816]{1,0:T(8,128)(2,1)}, bf16[128,2816]{1,0:T(8,128)(2,1)}, u32[]{:S(2)}, u32[]{:S(2)}) collective-permute-start(bf16[128,2816]{1,0:T(8,128)(2,1)} %collective-permute-done.2.refs_1_.refs_3_), channel_id=1, source_target_pairs={{0,2},{2,4},{4,6},{3,1},{5,3},{7,5},{8,10},{10,12},{12,14},{11,9},... | collective-permute-start | bytes 2162696 | tf_op jit(solution)/shard_map/ppermute | solution.py:377
  45.5 21.6 %collective-permute-start.6 = (bf16[128,2816]{1,0:T(8,128)(2,1)}, bf16[128,2816]{1,0:T(8,128)(2,1)S(1)}, u32[]{:S(2)}, u32[]{:S(2)}) collective-permute-start(bf16[128,2816]{1,0:T(8,128)(2,1)} %get-tuple-element.47), channel_id=1, source_target_pairs={{0,1},{1,0},{2,3},{3,2},{4,5},{5,4},{6,7},{7,6},{8,9},{9,8},{10,11... | collective-permute-start | bytes 2162696 | tf_op jit(solution)/shard_map/ppermute | solution.py:379
  59.0 0.7 copy-start
  59.7 19.5 %all-to-all-start.2 = ((f32[16,40,112]{2,1,0:T(8,128)}), f32[16,40,112]{2,1,0:T(8,128)S(1)}, u32[]{:S(2)}, u32[]{:S(2)}) async-start(f32[16,40,112]{2,1,0:T(8,128)} %get-tuple-element.45), calls=%async_computation.2 | async-start | bytes 655360 | tf_op jit(solution)/shard_map/all_to_all | solution.py:397
  63.3 7.8 %collective-permute-start.4 = (bf16[560,128]{1,0:T(8,128)(2,1)}, bf16[560,128]{1,0:T(8,128)(2,1)S(1)}, u32[]{:S(2)}, u32[]{:S(2)}) collective-permute-start(bf16[560,128]{1,0:T(8,128)(2,1)} %copy-done), channel_id=1, source_target_pairs={{0,8},{8,0},{1,9},{9,1},{2,10},{10,2},{3,11},{11,3},{4,12},{12,4},... | collective-permute-start | bytes 430088 | tf_op jit(solution)/shard_map/ppermute | solution.py:433
  79.6 1.6 %collective-permute-start.7 = (bf16[2,560,128]{2,1,0:T(8,128)(2,1)S(1)}, bf16[2,560,128]{2,1,0:T(8,128)(2,1)S(1)}, u32[]{:S(2)}, u32[]{:S(2)}) collective-permute-start(bf16[2,560,128]{2,1,0:T(8,128)(2,1)S(1)} %get-tuple-element.50), channel_id=1, source_target_pairs={{0,8},{8,0},{1,9},{9,1},{2,10},{10,2},{3,11},{11,3},{4,12},{12,4},... | collective-permute-start | bytes 860168 | tf_op jit(solution)/shard_map/ppermute | solution.py:445

commit v7 on v6

--- a/solution.py
+++ b/solution.py
@@ -16,7 +16,9 @@
 CUTS = (0,)
 CHUNKS = 1
 EARLY = 1
-ORDER = [[('near', 0), ('far', 0), ('sent', 0)], [], [('kept', 0)]]
+ORDER = [[], [('sent', 0)], [('kept', 0)]]
+SEND_COST = 500000000
+KEEP_COST = 10000000000
 CHIPS = ("y", "z", "x")
 F32 = jnp.float32
 BF16 = jnp.bfloat16
@@ -103,6 +105,23 @@
         (b_ref.at[theirs], send_ref.at[1]),
         (a_ref.at[mine], own_ref.at[0]),
         (b_ref.at[mine], own_ref.at[1]),
+    ]
+    copy_all(pairs, sems)
+
+
+def first_body(row, weight, a_ref, b_ref, send, mine, weight_mine, token, kv_send, kv, sems):
+    token[...] = jnp.zeros(token.shape, F32)
+    side = lax.axis_index("x")
+    own, theirs = halves(kv_send.shape[1])
+    half = row.shape[3] // 2
+    pairs = [
+        (a_ref.at[theirs], kv_send.at[0]),
+        (b_ref.at[theirs], kv_send.at[1]),
+        (a_ref.at[own], kv.at[0]),
+        (b_ref.at[own], kv.at[1]),
+        (row.at[0, 0, :, columns_at(side * half, half)], mine),
+        (row.at[0, 0, :, columns_at((1 - side) * half, half)], send),
+        (weight.at[:, :, columns_at(side * half, half)], weight_mine),
     ]
     copy_all(pairs, sems)
 
@@ -352,7 +371,7 @@
             [sd((cols, widths[i]), BF16), token],
             (row_mine[i], near[i], far[i], weight[i]),
             hold(i, 3) + hold_weight(i) + hold(i, 1) + sems(4),
-            flops=20 * cols * widths[i],
+            flops=SEND_COST,
             any_in=True,
             hbm_out=1,
         )
@@ -363,7 +382,7 @@
             [sd(conv_grad.shape, BF16), token],
             (row_mine[i], near[i], onward[i], back[i], weight[i], *before),
             hold(i, 4) + hold_weight(i) + hold(i, 1) + sems(5),
-            flops=20 * cols * widths[i],
+            flops=KEEP_COST,
             any_in=True,
             hbm_out=1,
             alias={5: 0} if before else None,
@@ -372,7 +391,14 @@
     row_mine, row_send, weight, halved, near, far = {}, {}, {}, {}, {}, {}
     sent, onward, back, kept = {}, {}, {}, {}
     for i in range(CHUNKS):
-        row_send[i], row_mine[i], weight[i], halved[i] = halve(i, ())
+        row_send[i], row_mine[i], weight[i], halved[i], kv_send, kv = call(
+            first_body,
+            [sd((cols, widths[i]), BF16)] * 2
+            + [sd((3, 3, widths[i]), F32), token, pair_shape, pair_shape],
+            tuple(map(held_in_hbm, (conv_grad, conv_weight, k, v))),
+            sems(7),
+            any_in=True,
+        )
         near[i], far[i] = move_in(i)
         onward[i] = lax.ppermute(near[i], ("z", "x"), even_up + odd_down)
         out_send, sent[i] = send_out(i)
@@ -388,7 +414,6 @@
             any_in=True,
         )
 
-    kv_send, kv = part(k, v, (halved[0],))
     kv_got = lax.ppermute(kv_send, "c", swap)
     qg_send, qg = part(q, g)
     qg_got = lax.ppermute(qg_send, "c", swap)

time: 82.7 us -> 75.5 us (0.913); the launches traced: 82.1 us -> 74 us
  waiting for transfers between devices: 36.4 us -> 27.4 us
  starting transfers between devices: 25.2 us -> 26.3 us
    all_to_all x3, waiting for transfers between devices: 22.1 us -> 13.9 us  [exchange(): return lax.all_to_all(pay, CHIPS, split_axis=0, concat_axis=0, tiled=True)]
    ppermute x1, waiting for transfers between devices: 3.67 us -> 0.01 us  [shards(): onward[i] = lax.ppermute(near[i], ('z', 'x'), even_up + odd_down)]
    ppermute x1, waiting for transfers between devices: 0.01 us -> 3.05 us  [shards(): back[i] = lax.ppermute(out_send, 'x', swap)]
    all_to_all x3, starting transfers between devices: 15.9 us -> 18.9 us  [exchange(): return lax.all_to_all(pay, CHIPS, split_axis=0, concat_axis=0, tiled=True)]
    ppermute x1, waiting for transfers between devices: 2.4 us -> 0.01 us  [move_in(): lax.ppermute(row_mine[i], ('z', 'x'), even_down + odd_up)]
    ppermute x1, waiting for transfers between devices: 0.01 us -> 1.56 us  [shards(): qg_got = lax.ppermute(qg_send, 'c', swap)]
    ppermute x1, starting transfers between devices: 4.72 us -> 3.43 us  [shards(): onward[i] = lax.ppermute(near[i], ('z', 'x'), even_up + odd_down)]
    ppermute x1, waiting for transfers between devices: 0.01 us -> 1.2 us  [shards(): kv_got = lax.ppermute(kv_send, 'c', swap)]
  transfers between devices with their start and end apart: 11 -> 11, of which waited for: 7 -> 8; matrix products, arithmetic and copies ran while one was open for 0% -> 0% of each run, Pallas kernels for 16% -> 18%
where the time goes in v7:
time: 75.5 us; the launch traced here: 74 us
  waiting for transfers between devices  27.4 us (36%)
  starting transfers between devices  26.3 us (35%)
  Pallas kernels  18.9 us (25%)
  between operations  0.79 us (1%)
    pallas_call x10, Pallas kernels, call(): pl.pallas_call(ordered, out_shape=shapes, in_specs=[free if any_in else f...  18.9 us
    all_to_all x3, starting transfers between devices, exchange(): return lax.all_to_all(pay, CHIPS, split_axis=0, concat_axis=0, tiled=True)  18.9 us
    all_to_all x3, waiting for transfers between devices, exchange(): return lax.all_to_all(pay, CHIPS, split_axis=0, concat_axis=0, tiled=True)  13.9 us
    ppermute x1, waiting for transfers between devices, move_in(): near = lax.ppermute(row_send[i], 'x', swap)  6.13 us
    ppermute x1, starting transfers between devices, shards(): onward[i] = lax.ppermute(near[i], ('z', 'x'), even_up + odd_down)  3.43 us
    ppermute x1, waiting for transfers between devices, shards(): back[i] = lax.ppermute(out_send, 'x', swap)  3.05 us
    ppermute x1, starting transfers between devices, move_in(): near = lax.ppermute(row_send[i], 'x', swap)  1.93 us
    ppermute x1, waiting for transfers between devices, shards(): qg_got = lax.ppermute(qg_send, 'c', swap)  1.56 us
  transfers between devices with their start and end apart: 11, of which 8 were waited for; matrix products, arithmetic and copies ran while one was open for 0% of the time, Pallas kernels for 18%

profile of v7, /device:TPU:0, one launch (start us, length us, event | category | flops | bytes accessed | tf_op | source)
XLA Modules:
  0.0 74.0 jit_solution(5886073056498385098)
XLA Ops:
  0.6 2.3 %shard_map.93 = (bf16[128,2816]{1,0:T(8,128)(2,1)S(1)}, bf16[128,2816]{1,0:T(8,128)(2,1)S(1)}, f32[3,3,2816]{2,1,0:T(4,128)S(1)}, f32[8,128]{1,0:T(8,128)}, bf16...) custom-call(bf16[1,1,128,5632]{3,2,1,0:T(8,128)(2,1)} %refs_0_.1, f32[3,3,5632]{2,1,0:T(4,128)} %refs_1_.1, ...), custom_call_target="tpu_custom_call" | custom-call | bytes 4338688 | tf_op jit(solution)/shard_map/pallas_call | solution.py:60
  2.9 0.5 collective-permute-start
  3.4 1.2 %collective-permute-done.refs_1_.refs_2_ = bf16[2,560,128]{2,1,0:T(8,128)(2,1)S(1)} collective-permute-done((bf16[2,560,128]{2,1,0:T(8,128)(2,1)S(1)}, bf16[2,560,128]{2,1,0:T(8,128)(2,1)S(1)}, u32[]{:S(2)}, u32[]{:S(2)}) %collective-permute-start) | collective-permute-done | bytes 286752 | tf_op jit(solution)/shard_map/ppermute | solution.py:417
  4.6 1.7 %shard_map.94 = (f32[16,40,112]{2,1,0:T(8,128)}, f32[8,128]{1,0:T(8,128)}) custom-call(bf16[2,560,128]{2,1,0:T(8,128)(2,1)S(1)} %get-tuple-element.28.refs_0_.refs_1_, bf16[2,560,128]{2,1,0:T(8,128)(2,1)S(1)} %collective-permute-done.refs_1_.refs_2_), custom_call_target="tpu_custom_call" | custom-call | flops 32112640 | bytes 864256 | tf_op jit(solution)/shard_map/pallas_call | solution.py:60
  6.3 8.2 %all-to-all-start = ((f32[16,40,112]{2,1,0:T(8,128)}), f32[16,40,112]{2,1,0:T(8,128)S(1)}, u32[]{:S(2)}, u32[]{:S(2)}) async-start(f32[16,40,112]{2,1,0:T(8,128)} %get-tuple-element.30), calls=%async_computation | async-start | bytes 655360 | tf_op jit(solution)/shard_map/all_to_all | solution.py:422
  14.6 1.9 %collective-permute-start.2 = (bf16[128,2816]{1,0:T(8,128)(2,1)S(1)}, bf16[128,2816]{1,0:T(8,128)(2,1)}, u32[]{:S(2)}, u32[]{:S(2)}) collective-permute-start(bf16[128,2816]{1,0:T(8,128)(2,1)S(1)} %get-tuple-element.37), channel_id=1, source_target_pairs={{0,1},{1,0},{2,3},{3,2},{4,5},{5,4},{6,7},{7,6},{8,9},{9,8},{10,11... | collective-permute-start | bytes 2162696 | tf_op jit(solution)/shard_map/ppermute | solution.py:365
  16.5 1.3 %collective-permute-start.3 = (bf16[128,2816]{1,0:T(8,128)(2,1)S(1)}, bf16[128,2816]{1,0:T(8,128)(2,1)}, u32[]{:S(2)}, u32[]{:S(2)}) collective-permute-start(bf16[128,2816]{1,0:T(8,128)(2,1)S(1)} %get-tuple-element.36.refs_0_), channel_id=1, source_target_pairs={{2,0},{4,2},{6,4},{1,3},{3,5},{5,7},{10,8},{12,10},{14,12},{9,11},... | collective-permute-start | bytes 2162696 | tf_op jit(solution)/shard_map/ppermute | solution.py:366
  17.8 1.2 %shard_map.95 = (bf16[2,560,128]{2,1,0:T(8,128)(2,1)S(1)}, bf16[2,560,128]{2,1,0:T(8,128)(2,1)S(1)}) custom-call(bf16[1120,128]{1,0:T(8,128)(2,1)} %bitcast.23, bf16[1120,128]{1,0:T(8,128)(2,1)} %bitcast.24), custom_call_target="tpu_custom_call" | custom-call | bytes 1146880 | tf_op jit(solution)/shard_map/pallas_call | solution.py:60
  19.0 0.1 collective-permute-start.1
  19.1 1.6 %collective-permute-done.1.refs_2_ = bf16[2,560,128]{2,1,0:T(8,128)(2,1)S(1)} collective-permute-done((bf16[2,560,128]{2,1,0:T(8,128)(2,1)S(1)}, bf16[2,560,128]{2,1,0:T(8,128)(2,1)S(1)}, u32[]{:S(2)}, u32[]{:S(2)}) %collective-permute-start.1) | collective-permute-done | bytes 286752 | tf_op jit(solution)/shard_map/ppermute | solution.py:419
  20.6 5.7 %all-to-all-done.refs_0_ = f32[16,40,112]{2,1,0:T(8,128)S(1)} async-done(((f32[16,40,112]{2,1,0:T(8,128)}), f32[16,40,112]{2,1,0:T(8,128)S(1)}, u32[]{:S(2)}, u32[]{:S(2)}) %all-to-all-start) | async-done | bytes 286752 | tf_op jit(solution)/shard_map/all_to_all | solution.py:422
  26.3 1.8 %shard_map.96 = (f32[16,72,112]{2,1,0:T(8,128)}, f32[5,112]{1,0:T(8,128)S(1)}, f32[5,256]{1,0:T(8,128)S(1)}) custom-call(f32[16,40,112]{2,1,0:T(8,128)S(1)} %all-to-all-done.refs_0_, bf16[2,560,128]{2,1,0:T(8,128)(2,1)S(1)} %get-tuple-element.31.refs_1_, bf16[2,560,128]{2,1,0:T(8,128)(2,1)S(1)} %collective-permute-done.1.refs_2_), custom_call_target="tpu_custom_call" | custom-call | flops 64225280 | bytes 1383616 | tf_op jit(solution)/shard_map/pallas_call | solution.py:60
  28.1 3.6 %all-to-all-start.1 = ((f32[16,72,112]{2,1,0:T(8,128)}), f32[16,72,112]{2,1,0:T(8,128)S(1)}, u32[]{:S(2)}, u32[]{:S(2)}) async-start(f32[16,72,112]{2,1,0:T(8,128)} %get-tuple-element.33), calls=%async_computation.1 | async-start | bytes 1179648 | tf_op jit(solution)/shard_map/all_to_all | solution.py:422
  31.7 6.1 %collective-permute-done.2.refs_1_ = bf16[128,2816]{1,0:T(8,128)(2,1)} collective-permute-done((bf16[128,2816]{1,0:T(8,128)(2,1)S(1)}, bf16[128,2816]{1,0:T(8,128)(2,1)}, u32[]{:S(2)}, u32[]{:S(2)}) %collective-permute-start.2) | collective-permute-done | bytes 720928 | tf_op jit(solution)/shard_map/ppermute | solution.py:365
  37.8 3.4 %collective-permute-start.5 = (bf16[128,2816]{1,0:T(8,128)(2,1)}, bf16[128,2816]{1,0:T(8,128)(2,1)}, u32[]{:S(2)}, u32[]{:S(2)}) collective-permute-start(bf16[128,2816]{1,0:T(8,128)(2,1)} %collective-permute-done.2.refs_1_), channel_id=1, source_target_pairs={{0,2},{2,4},{4,6},{3,1},{5,3},{7,5},{8,10},{10,12},{12,14},{11,9},... | collective-permute-start | bytes 2162696 | tf_op jit(solution)/shard_map/ppermute | solution.py:403
  41.3 0.0 collective-permute-done.3.refs_2_
  41.3 3.8 %shard_map.97 = (bf16[128,2816]{1,0:T(8,128)(2,1)}, f32[8,128]{1,0:T(8,128)S(1)}) custom-call(bf16[128,2816]{1,0:T(8,128)(2,1)S(1)} %get-tuple-element.36.refs_0_, bf16[128,2816]{1,0:T(8,128)(2,1)} %collective-permute-done.2.refs_1_, bf16[128,2816]{1,0:T(8,128)(2,1)} %collective-permute-done.3.refs_2_, f32[3,3,2816]{2,1,0:T(4,128)S(1)} %get-tuple-element.38.refs_3_.refs_4_), custom_call_target="tpu_custom_call" | custom-call | flops 500000000 | bytes 2989056 | tf_op jit(solution)/shard_map/pallas_call | solution.py:60
  45.1 0.1 collective-permute-start.6
  45.2 5.0 %all-to-all-done.1.refs_0_ = f32[16,72,112]{2,1,0:T(8,128)S(1)} async-done(((f32[16,72,112]{2,1,0:T(8,128)}), f32[16,72,112]{2,1,0:T(8,128)S(1)}, u32[]{:S(2)}, u32[]{:S(2)}) %all-to-all-start.1) | async-done | bytes 516128 | tf_op jit(solution)/shard_map/all_to_all | solution.py:422
  50.2 2.0 %shard_map.98 = (f32[16,40,112]{2,1,0:T(8,128)}, bf16[560,128]{1,0:T(8,128)(2,1)S(1)}, bf16[560,128]{1,0:T(8,128)(2,1)S(1)}) custom-call(f32[16,72,112]{2,1,0:T(8,128)S(1)} %all-to-all-done.1.refs_0_, bf16[2,560,128]{2,1,0:T(8,128)(2,1)S(1)} %get-tuple-element.31.refs_1_, bf16[2,560,128]{2,1,0:T(8,128)(2,1)S(1)} %collective-permute-done.1.refs_2_, ...), custom_call_target="tpu_custom_call" | custom-call | flops 64225280 | bytes 1670336 | tf_op jit(solution)/shard_map/pallas_call | solution.py:60
  52.2 0.0 copy-start
  52.2 0.7 copy-done
  52.9 7.0 %all-to-all-start.2 = ((f32[16,40,112]{2,1,0:T(8,128)}), f32[16,40,112]{2,1,0:T(8,128)S(1)}, u32[]{:S(2)}, u32[]{:S(2)}) async-start(f32[16,40,112]{2,1,0:T(8,128)} %get-tuple-element.43), calls=%async_computation.2 | async-start | bytes 655360 | tf_op jit(solution)/shard_map/all_to_all | solution.py:422
  59.9 0.1 collective-permute-start.4
  60.0 0.0 collective-permute-done.5.refs_2_
  60.0 3.0 %collective-permute-done.6.refs_3_ = bf16[128,2816]{1,0:T(8,128)(2,1)S(1)} collective-permute-done((bf16[128,2816]{1,0:T(8,128)(2,1)}, bf16[128,2816]{1,0:T(8,128)(2,1)S(1)}, u32[]{:S(2)}, u32[]{:S(2)}) %collective-permute-start.6) | collective-permute-done | bytes 720928 | tf_op jit(solution)/shard_map/ppermute | solution.py:405
  63.0 4.1 %shard_map.100 = (bf16[1,1,128,5632]{3,2,1,0:T(8,128)(2,1)}, f32[8,128]{1,0:T(8,128)S(1)}) custom-call(bf16[128,2816]{1,0:T(8,128)(2,1)S(1)} %get-tuple-element.36.refs_0_, bf16[128,2816]{1,0:T(8,128)(2,1)} %collective-permute-done.2.refs_1_, bf16[128,2816]{1,0:T(8,128)(2,1)} %collective-permute-done.5.refs_2_, ...), custom_call_target="tpu_custom_call" | custom-call | flops 10000000000 | bytes 4430848 | tf_op jit(solution)/shard_map/pallas_call | solution.py:60
  67.1 0.0 collective-permute-done.4.refs_1_
  67.1 0.7 %shard_map.99 = (bf16[1120,128]{1,0:T(8,128)(2,1)}, f32[8,128]{1,0:T(8,128)S(1)}) custom-call(bf16[560,128]{1,0:T(8,128)(2,1)S(1)} %get-tuple-element.40.refs_0_, bf16[560,128]{1,0:T(8,128)(2,1)S(1)} %collective-permute-done.4.refs_1_), custom_call_target="tpu_custom_call" | custom-call | bytes 577536 | tf_op jit(solution)/shard_map/pallas_call | solution.py:60
  67.9 3.1 %all-to-all-done.2.refs_0_ = f32[16,40,112]{2,1,0:T(8,128)S(1)} async-done(((f32[16,40,112]{2,1,0:T(8,128)}), f32[16,40,112]{2,1,0:T(8,128)S(1)}, u32[]{:S(2)}, u32[]{:S(2)}) %all-to-all-start.2) | async-done | bytes 286752 | tf_op jit(solution)/shard_map/all_to_all | solution.py:422
  71.0 0.5 shard_map.101
  71.5 0.1 collective-permute-start.7
  71.6 1.6 %collective-permute-done.7.refs_1_ = bf16[2,560,128]{2,1,0:T(8,128)(2,1)S(1)} collective-permute-done((bf16[2,560,128]{2,1,0:T(8,128)(2,1)S(1)}, bf16[2,560,128]{2,1,0:T(8,128)(2,1)S(1)}, u32[]{:S(2)}, u32[]{:S(2)}) %collective-permute-start.7) | collective-permute-done | bytes 286752 | tf_op jit(solution)/shard_map/ppermute | solution.py:470
  73.2 0.9 %shard_map.102 = (bf16[1120,128]{1,0:T(8,128)(2,1)}, bf16[1120,128]{1,0:T(8,128)(2,1)}) custom-call(bf16[2,560,128]{2,1,0:T(8,128)(2,1)S(1)} %get-tuple-element.47.refs_0_, bf16[2,560,128]{2,1,0:T(8,128)(2,1)S(1)} %collective-permute-done.7.refs_1_), custom_call_target="tpu_custom_call" | custom-call | bytes 1146880 | tf_op jit(solution)/shard_map/pallas_call | solution.py:60
Async XLA Ops:
  2.9 1.7 %collective-permute-start = (bf16[2,560,128]{2,1,0:T(8,128)(2,1)S(1)}, bf16[2,560,128]{2,1,0:T(8,128)(2,1)S(1)}, u32[]{:S(2)}, u32[]{:S(2)}) collective-permute-start(bf16[2,560,128]{2,1,0:T(8,128)(2,1)S(1)} %get-tuple-element.29), channel_id=1, source_target_pairs={{0,8},{8,0},{1,9},{9,1},{2,10},{10,2},{3,11},{11,3},{4,12},{12,4},... | collective-permute-start | bytes 860168 | tf_op jit(solution)/shard_map/ppermute | solution.py:417
  6.3 20.0 %all-to-all-start = ((f32[16,40,112]{2,1,0:T(8,128)}), f32[16,40,112]{2,1,0:T(8,128)S(1)}, u32[]{:S(2)}, u32[]{:S(2)}) async-start(f32[16,40,112]{2,1,0:T(8,128)} %get-tuple-element.30), calls=%async_computation | async-start | bytes 655360 | tf_op jit(solution)/shard_map/all_to_all | solution.py:422
  14.6 23.2 %collective-permute-start.2 = (bf16[128,2816]{1,0:T(8,128)(2,1)S(1)}, bf16[128,2816]{1,0:T(8,128)(2,1)}, u32[]{:S(2)}, u32[]{:S(2)}) collective-permute-start(bf16[128,2816]{1,0:T(8,128)(2,1)S(1)} %get-tuple-element.37), channel_id=1, source_target_pairs={{0,1},{1,0},{2,3},{3,2},{4,5},{5,4},{6,7},{7,6},{8,9},{9,8},{10,11... | collective-permute-start | bytes 2162696 | tf_op jit(solution)/shard_map/ppermute | solution.py:365
  16.5 24.8 %collective-permute-start.3 = (bf16[128,2816]{1,0:T(8,128)(2,1)S(1)}, bf16[128,2816]{1,0:T(8,128)(2,1)}, u32[]{:S(2)}, u32[]{:S(2)}) collective-permute-start(bf16[128,2816]{1,0:T(8,128)(2,1)S(1)} %get-tuple-element.36.refs_0_), channel_id=1, source_target_pairs={{2,0},{4,2},{6,4},{1,3},{3,5},{5,7},{10,8},{12,10},{14,12},{9,11},... | collective-permute-start | bytes 2162696 | tf_op jit(solution)/shard_map/ppermute | solution.py:366
  19.0 1.6 %collective-permute-start.1 = (bf16[2,560,128]{2,1,0:T(8,128)(2,1)S(1)}, bf16[2,560,128]{2,1,0:T(8,128)(2,1)S(1)}, u32[]{:S(2)}, u32[]{:S(2)}) collective-permute-start(bf16[2,560,128]{2,1,0:T(8,128)(2,1)S(1)} %get-tuple-element.32), channel_id=1, source_target_pairs={{0,8},{8,0},{1,9},{9,1},{2,10},{10,2},{3,11},{11,3},{4,12},{12,4},... | collective-permute-start | bytes 860168 | tf_op jit(solution)/shard_map/ppermute | solution.py:419
  28.1 22.1 %all-to-all-start.1 = ((f32[16,72,112]{2,1,0:T(8,128)}), f32[16,72,112]{2,1,0:T(8,128)S(1)}, u32[]{:S(2)}, u32[]{:S(2)}) async-start(f32[16,72,112]{2,1,0:T(8,128)} %get-tuple-element.33), calls=%async_computation.1 | async-start | bytes 1179648 | tf_op jit(solution)/shard_map/all_to_all | solution.py:422
  37.8 22.1 %collective-permute-start.5 = (bf16[128,2816]{1,0:T(8,128)(2,1)}, bf16[128,2816]{1,0:T(8,128)(2,1)}, u32[]{:S(2)}, u32[]{:S(2)}) collective-permute-start(bf16[128,2816]{1,0:T(8,128)(2,1)} %collective-permute-done.2.refs_1_), channel_id=1, source_target_pairs={{0,2},{2,4},{4,6},{3,1},{5,3},{7,5},{8,10},{10,12},{12,14},{11,9},... | collective-permute-start | bytes 2162696 | tf_op jit(solution)/shard_map/ppermute | solution.py:403
  45.1 17.9 %collective-permute-start.6 = (bf16[128,2816]{1,0:T(8,128)(2,1)}, bf16[128,2816]{1,0:T(8,128)(2,1)S(1)}, u32[]{:S(2)}, u32[]{:S(2)}) collective-permute-start(bf16[128,2816]{1,0:T(8,128)(2,1)} %get-tuple-element.45), channel_id=1, source_target_pairs={{0,1},{1,0},{2,3},{3,2},{4,5},{5,4},{6,7},{7,6},{8,9},{9,8},{10,11... | collective-permute-start | bytes 2162696 | tf_op jit(solution)/shard_map/ppermute | solution.py:405
  52.2 0.7 copy-start
  52.9 18.2 %all-to-all-start.2 = ((f32[16,40,112]{2,1,0:T(8,128)}), f32[16,40,112]{2,1,0:T(8,128)S(1)}, u32[]{:S(2)}, u32[]{:S(2)}) async-start(f32[16,40,112]{2,1,0:T(8,128)} %get-tuple-element.43), calls=%async_computation.2 | async-start | bytes 655360 | tf_op jit(solution)/shard_map/all_to_all | solution.py:422
  59.9 7.2 %collective-permute-start.4 = (bf16[560,128]{1,0:T(8,128)(2,1)}, bf16[560,128]{1,0:T(8,128)(2,1)S(1)}, u32[]{:S(2)}, u32[]{:S(2)}) collective-permute-start(bf16[560,128]{1,0:T(8,128)(2,1)} %copy-done), channel_id=1, source_target_pairs={{0,8},{8,0},{1,9},{9,1},{2,10},{10,2},{3,11},{11,3},{4,12},{12,4},... | collective-permute-start | bytes 430088 | tf_op jit(solution)/shard_map/ppermute | solution.py:458
  71.5 1.6 %collective-permute-start.7 = (bf16[2,560,128]{2,1,0:T(8,128)(2,1)S(1)}, bf16[2,560,128]{2,1,0:T(8,128)(2,1)S(1)}, u32[]{:S(2)}, u32[]{:S(2)}) collective-permute-start(bf16[2,560,128]{2,1,0:T(8,128)(2,1)S(1)} %get-tuple-element.48), channel_id=1, source_target_pairs={{0,8},{8,0},{1,9},{9,1},{2,10},{10,2},{3,11},{11,3},{4,12},{12,4},... | collective-permute-start | bytes 860168 | tf_op jit(solution)/shard_map/ppermute | solution.py:470

commit v8 on v7

--- a/solution.py
+++ b/solution.py
@@ -13,6 +13,7 @@
 EPSILON = 1e-06
 HALF = HEADS // 2
 LANES = 128
+PIECES = 4
 CUTS = (0,)
 CHUNKS = 1
 EARLY = 1
@@ -32,14 +33,15 @@
     return pltpu.with_memory_space_constraint(x, pltpu.HBM)
 
 
-def call(body, outs, args, scratch=(), flops=0, after=(), any_in=False, hbm_out=0, pinned=False, alias=None):
+def call(body, outs, args, scratch=(), flops=0, after=(), any_in=False, hbm_out=0, pinned=0, alias=None):
     size = sum(math.prod(a.shape) * a.dtype.itemsize for a in list(args) + list(outs))
     fast = pl.BlockSpec(memory_space=pltpu.VMEM)
     slow = pl.BlockSpec(memory_space=pltpu.HBM)
     free = pl.BlockSpec(memory_space=pl.ANY)
     scratch = list(scratch)
     if pinned:
-        scratch += [pltpu.VMEM(outs[0].shape, outs[0].dtype), pltpu.SemaphoreType.DMA((1,))]
+        scratch += [pltpu.VMEM(o.shape, o.dtype) for o in outs[:pinned]]
+        scratch += [pltpu.SemaphoreType.DMA((pinned,))]
 
     def ordered(*refs):
         ins = refs[: len(args)]
@@ -48,9 +50,10 @@
         if not pinned:
             body(*ins, *made, *held)
             return
-        first, sem = held[-2:]
-        body(*ins, first, *made[1:], *held[:-2])
-        copy_all([(first, made[0])], sem)
+        *held, sem = held
+        kept, held = held[-pinned:], held[:-pinned]
+        body(*ins, *kept, *made[pinned:], *held)
+        copy_all(list(zip(kept, made)), sem)
 
     out_specs = [slow if i < max(hbm_out, pinned) else fast for i in range(len(outs))]
     shapes = [
@@ -109,19 +112,16 @@
     copy_all(pairs, sems)
 
 
-def first_body(row, weight, a_ref, b_ref, send, mine, weight_mine, token, kv_send, kv, sems):
+def first_body(row, weight, send, mine, weight_mine, token, sems):
     token[...] = jnp.zeros(token.shape, F32)
     side = lax.axis_index("x")
-    own, theirs = halves(kv_send.shape[1])
-    half = row.shape[3] // 2
+    half = mine.shape[1]
+    own = columns_at(side * half, half)
+    other = columns_at((1 - side) * half, half)
     pairs = [
-        (a_ref.at[theirs], kv_send.at[0]),
-        (b_ref.at[theirs], kv_send.at[1]),
-        (a_ref.at[own], kv.at[0]),
-        (b_ref.at[own], kv.at[1]),
-        (row.at[0, 0, :, columns_at(side * half, half)], mine),
-        (row.at[0, 0, :, columns_at((1 - side) * half, half)], send),
-        (weight.at[:, :, columns_at(side * half, half)], weight_mine),
+        (row.at[0, 0, :, own], mine),
+        (row.at[0, 0, :, other], send),
+        (weight.at[:, :, own], weight_mine),
     ]
     copy_all(pairs, sems)
 
@@ -140,11 +140,14 @@
     out[theirs] = far[...]
 
 
-def merge_pair(own, far, first, second):
-    mine, theirs = halves(own.shape[1])
-    for i, out in enumerate((first, second)):
-        out[mine] = own[i]
-        out[theirs] = far[i]
+def place_own(own, first, second, sems):
+    mine, _ = halves(own.shape[1])
+    copy_all([(own.at[0], first.at[mine]), (own.at[1], second.at[mine])], sems)
+
+
+def place_far(far, first_in, second_in, first, second, sems):
+    _, theirs = halves(far.shape[1])
+    copy_all([(far.at[0], first.at[theirs]), (far.at[1], second.at[theirs])], sems)
 
 
 def head_of(own, got, i, h):
@@ -275,40 +278,70 @@
     copy_all(list(zip(pairs, (send, mine, weight_mine))), sems)
 
 
+def pieces_of(width):
+    step = -(-(width // LANES) // PIECES) * LANES
+    return [(at, min(step, width - at)) for at in range(0, width, step)]
+
+
+def staged(sources, held, sems, made, picks, out_of):
+    width = made.shape[1]
+    loads, stores = [], []
+    for n, (at, size) in enumerate(pieces_of(width)):
+        part = pl.ds(at, size)
+        group = []
+        for m, (a, b) in enumerate(zip(sources, held)):
+            index = (slice(None),) * (len(a.shape) - 1) + (part,)
+            group.append(pltpu.make_async_copy(a.at[index], b.at[index], sems.at[n, m]))
+        for c in group:
+            c.start()
+        loads.append(group)
+    *planes, weight = held[:4]
+    for n, (at, size) in enumerate(pieces_of(width)):
+        for c in loads[n]:
+            c.wait()
+
+        @pl.loop(at // LANES, (at + size) // LANES)
+        def _(t):
+            lanes = columns_at(t * LANES, LANES)
+            made[:, lanes] = taps(planes, weight, picks, lanes)
+
+        for m, (a, b) in enumerate(out_of(at, size)):
+            c = pltpu.make_async_copy(a, b, sems.at[n, len(sources) + m])
+            c.start()
+            stores.append(c)
+    for c in stores:
+        c.wait()
+
+
 def send_body(mine, got, far, weight, out, token, *held):
     *held, made, sems = held
     token[...] = jnp.zeros(token.shape, F32)
-    copy_all(list(zip((mine, got, far, weight), held)), sems)
-    mine, got, far, weight = held
     side = lax.axis_index("x")
-    width = mine.shape[1]
-
-    @pl.loop(0, width // LANES)
-    def _(t):
-        lanes = columns_at(t * LANES, LANES)
-        made[:, lanes] = taps((got, mine, far), weight, (1, 2 - 2 * side, 2 * side), lanes)
-
-    copy_all([(made, out)], sems)
-
-
-def keep_body(at, mine, got, far, back, weight, *refs):
-    out, token, *held = refs[-9:]
+
+    def out_of(at, size):
+        return [(made.at[:, pl.ds(at, size)], out.at[:, pl.ds(at, size)])]
+
+    staged((got, mine, far, weight), held, sems, made, (1, 2 - 2 * side, 2 * side), out_of)
+
+
+def keep_body(mine, got, far, back, weight, out, token, *held):
     *held, made, sems = held
     token[...] = jnp.zeros(token.shape, F32)
-    copy_all(list(zip((mine, got, far, back, weight), held)), sems)
-    mine, got, far, back, weight = held
     side = lax.axis_index("x")
-    width = mine.shape[1]
-
-    @pl.loop(0, width // LANES)
-    def _(t):
-        lanes = columns_at(t * LANES, LANES)
-        made[:, lanes] = taps((mine, got, far), weight, (1, 2 * side, 2 - 2 * side), lanes)
-
     half = out.shape[3] // 2
-    here = columns_at(side * half + at, width)
-    there = columns_at((1 - side) * half + at, width)
-    copy_all([(made, out.at[0, 0, :, here]), (back, out.at[0, 0, :, there])], sems)
+
+    def out_of(at, size):
+        here = columns_at(side * half + at, size)
+        there = columns_at((1 - side) * half + at, size)
+        part = pl.ds(at, size)
+        back_held = held[4]
+        return [
+            (made.at[:, part], out.at[0, 0, :, here]),
+            (back_held.at[:, part], out.at[0, 0, :, there]),
+        ]
+
+    sources = (mine, got, far, weight, back)
+    staged(sources, held, sems, made, (1, 2 * side, 2 - 2 * side), out_of)
 
 
 def shards(queries, key_proj, value_proj, attn_grad, conv_grad, conv_weight):
@@ -370,7 +403,7 @@
             send_body,
             [sd((cols, widths[i]), BF16), token],
             (row_mine[i], near[i], far[i], weight[i]),
-            hold(i, 3) + hold_weight(i) + hold(i, 1) + sems(4),
+            hold(i, 3) + hold_weight(i) + hold(i, 1) + [pltpu.SemaphoreType.DMA((PIECES, 5))],
             flops=SEND_COST,
             any_in=True,
             hbm_out=1,
@@ -378,10 +411,10 @@
 
     def finish(i, before=()):
         return call(
-            functools.partial(keep_body, starts[i]),
+            keep_body,
             [sd(conv_grad.shape, BF16), token],
             (row_mine[i], near[i], onward[i], back[i], weight[i], *before),
-            hold(i, 4) + hold_weight(i) + hold(i, 1) + sems(5),
+            hold(i, 3) + hold_weight(i) + hold(i, 2) + [pltpu.SemaphoreType.DMA((PIECES, 7))],
             flops=KEEP_COST,
             any_in=True,
             hbm_out=1,
@@ -391,12 +424,11 @@
     row_mine, row_send, weight, halved, near, far = {}, {}, {}, {}, {}, {}
     sent, onward, back, kept = {}, {}, {}, {}
     for i in range(CHUNKS):
-        row_send[i], row_mine[i], weight[i], halved[i], kv_send, kv = call(
+        row_send[i], row_mine[i], weight[i], halved[i] = call(
             first_body,
-            [sd((cols, widths[i]), BF16)] * 2
-            + [sd((3, 3, widths[i]), F32), token, pair_shape, pair_shape],
-            tuple(map(held_in_hbm, (conv_grad, conv_weight, k, v))),
-            sems(7),
+            [sd((cols, widths[i]), BF16)] * 2 + [sd((3, 3, widths[i]), F32), token],
+            tuple(map(held_in_hbm, (conv_grad, conv_weight))),
+            sems(3),
             any_in=True,
         )
         near[i], far[i] = move_in(i)
@@ -414,6 +446,7 @@
             any_in=True,
         )
 
+    kv_send, kv = part(k, v)
     kv_got = lax.ppermute(kv_send, "c", swap)
     qg_send, qg = part(q, g)
     qg_got = lax.ppermute(qg_send, "c", swap)
@@ -428,10 +461,11 @@
         (kv, kv_got),
         scratch,
         flops=2 * macs,
-        pinned=True,
+        after=(halved[0],),
+        pinned=1,
     )
     got = exchange(pay)
-    ties = {"near": near, "far": far, "sent": sent, "kept": kept, "halved": halved}
+    ties = {"near": near, "far": far, "sent": sent, "kept": kept}
 
     def tied(stage):
         return tuple(ties[name][i] for name, i in ORDER[stage])
@@ -442,7 +476,7 @@
         (got, qg, qg_got),
         scratch,
         flops=4 * macs,
-        pinned=True,
+        pinned=1,
         after=tied(0),
     )
     got = exchange(pay)
@@ -452,7 +486,7 @@
         (got, qg, qg_got, norm, inv),
         scratch,
         flops=4 * macs,
-        pinned=True,
+        pinned=1,
         after=tied(1),
     )
     query_got = lax.ppermute(query_send, "c", swap)
@@ -468,7 +502,16 @@
         after=(merged, *tied(2)),
     )
     key_got = lax.ppermute(key_send, "c", swap)
-    outs = query_out, *call(merge_pair, [whole_shape] * 2, (key_mine, key_got))
+    own = call(place_own, [whole_shape] * 2, (key_mine,), sems(2), any_in=True, hbm_out=2)
+    outs = query_out, *call(
+        place_far,
+        [whole_shape] * 2,
+        (key_got, *own),
+        sems(2),
+        any_in=True,
+        hbm_out=2,
+        alias={1: 0, 2: 1},
+    )
     outs = [jnp.swapaxes(o.reshape(*queries.shape[:2], 2 * half, -1), 2, 3) for o in outs]
     return (*outs, input_grad)
 

time: 75.5 us -> 73.5 us (0.974); the launches traced: 74 us -> 73 us
    all_to_all x3, waiting for transfers between devices: 13.9 us -> 15.8 us  [exchange(): return lax.all_to_all(pay, CHIPS, split_axis=0, concat_axis=0, tiled=True)]
    ppermute x1, waiting for transfers between devices: 1.2 us -> 0.01 us  [shards(): kv_got = lax.ppermute(kv_send, 'c', swap)]
    pallas_call x10 -> x12, Pallas kernels: 18.9 us -> 18.3 us  [call(): pl.pallas_call(ordered, out_shape=shapes, in_specs=[free if any_in else f...]
  transfers between devices with their start and end apart: 11 -> 11, of which waited for: 8 -> 7; matrix products, arithmetic and copies ran while one was open for 0% -> 0% of each run, Pallas kernels for 18% -> 20%
where the time goes in v8:
time: 73.5 us; the launch traced here: 73 us
  waiting for transfers between devices  27 us (37%)
  starting transfers between devices  26.2 us (36%)
  Pallas kernels  18.3 us (25%)
  between operations  0.81 us (1%)
    all_to_all x3, starting transfers between devices, exchange(): return lax.all_to_all(pay, CHIPS, split_axis=0, concat_axis=0, tiled=True)  18.8 us
    pallas_call x12, Pallas kernels, call(): pl.pallas_call(ordered, out_shape=shapes, in_specs=[free if any_in else f...  18.3 us
    all_to_all x3, waiting for transfers between devices, exchange(): return lax.all_to_all(pay, CHIPS, split_axis=0, concat_axis=0, tiled=True)  15.8 us
    ppermute x1, waiting for transfers between devices, move_in(): near = lax.ppermute(row_send[i], 'x', swap)  6.29 us
    ppermute x1, starting transfers between devices, shards(): onward[i] = lax.ppermute(near[i], ('z', 'x'), even_up + odd_down)  3.38 us
    ppermute x1, waiting for transfers between devices, shards(): back[i] = lax.ppermute(out_send, 'x', swap)  2.54 us
    ppermute x1, starting transfers between devices, move_in(): near = lax.ppermute(row_send[i], 'x', swap)  1.93 us
    ppermute x1, waiting for transfers between devices, shards(): qg_got = lax.ppermute(qg_send, 'c', swap)  1.56 us
  transfers between devices with their start and end apart: 11, of which 7 were waited for; matrix products, arithmetic and copies ran while one was open for 0% of the time, Pallas kernels for 20%

profile of v8, /device:TPU:0, one launch (start us, length us, event | category | flops | bytes accessed | tf_op | source)
XLA Modules:
  0.0 73.0 jit_solution(5950654040633212354)
XLA Ops:
  0.6 1.2 %shard_map.93 = (bf16[2,560,128]{2,1,0:T(8,128)(2,1)S(1)}, bf16[2,560,128]{2,1,0:T(8,128)(2,1)S(1)}) custom-call(bf16[1120,128]{1,0:T(8,128)(2,1)} %bitcast.21, bf16[1120,128]{1,0:T(8,128)(2,1)} %bitcast.22), custom_call_target="tpu_custom_call" | custom-call | bytes 1146880 | tf_op jit(solution)/shard_map/pallas_call | solution.py:63
  1.8 0.5 collective-permute-start
  2.3 1.4 %shard_map.94 = (bf16[128,2816]{1,0:T(8,128)(2,1)S(1)}, bf16[128,2816]{1,0:T(8,128)(2,1)S(1)}, f32[3,3,2816]{2,1,0:T(4,128)S(1)}, f32[8,128]{1,0:T(8,128)S(1)}) custom-call(bf16[1,1,128,5632]{3,2,1,0:T(8,128)(2,1)} %refs_0_.1, f32[3,3,5632]{2,1,0:T(4,128)} %refs_1_.1), custom_call_target="tpu_custom_call" | custom-call | bytes 3191808 | tf_op jit(solution)/shard_map/pallas_call | solution.py:63
  3.7 0.0 collective-permute-done.refs_1_.refs_2_
  3.7 1.7 %shard_map.95 = (f32[16,40,112]{2,1,0:T(8,128)}, f32[8,128]{1,0:T(8,128)}) custom-call(bf16[2,560,128]{2,1,0:T(8,128)(2,1)S(1)} %get-tuple-element.31.refs_0_.refs_1_, bf16[2,560,128]{2,1,0:T(8,128)(2,1)S(1)} %collective-permute-done.refs_1_.refs_2_, f32[8,128]{1,0:T(8,128)S(1)} %get-tuple-element.33.refs_2_), custom_call_target="tpu_custom_call" | custom-call | flops 32112640 | bytes 864256 | tf_op jit(solution)/shard_map/pallas_call | solution.py:63
  5.4 8.1 %all-to-all-start = ((f32[16,40,112]{2,1,0:T(8,128)}), f32[16,40,112]{2,1,0:T(8,128)S(1)}, u32[]{:S(2)}, u32[]{:S(2)}) async-start(f32[16,40,112]{2,1,0:T(8,128)} %get-tuple-element.34), calls=%async_computation | async-start | bytes 655360 | tf_op jit(solution)/shard_map/all_to_all | solution.py:455
  13.5 1.9 %collective-permute-start.2 = (bf16[128,2816]{1,0:T(8,128)(2,1)S(1)}, bf16[128,2816]{1,0:T(8,128)(2,1)}, u32[]{:S(2)}, u32[]{:S(2)}) collective-permute-start(bf16[128,2816]{1,0:T(8,128)(2,1)S(1)} %get-tuple-element.41), channel_id=1, source_target_pairs={{0,1},{1,0},{2,3},{3,2},{4,5},{5,4},{6,7},{7,6},{8,9},{9,8},{10,11... | collective-permute-start | bytes 2162696 | tf_op jit(solution)/shard_map/ppermute | solution.py:398
  15.4 1.3 %collective-permute-start.3 = (bf16[128,2816]{1,0:T(8,128)(2,1)S(1)}, bf16[128,2816]{1,0:T(8,128)(2,1)}, u32[]{:S(2)}, u32[]{:S(2)}) collective-permute-start(bf16[128,2816]{1,0:T(8,128)(2,1)S(1)} %get-tuple-element.40.refs_0_), channel_id=1, source_target_pairs={{2,0},{4,2},{6,4},{1,3},{3,5},{5,7},{10,8},{12,10},{14,12},{9,11},... | collective-permute-start | bytes 2162696 | tf_op jit(solution)/shard_map/ppermute | solution.py:399
  16.7 1.2 %shard_map.96 = (bf16[2,560,128]{2,1,0:T(8,128)(2,1)S(1)}, bf16[2,560,128]{2,1,0:T(8,128)(2,1)S(1)}) custom-call(bf16[1120,128]{1,0:T(8,128)(2,1)} %bitcast.23, bf16[1120,128]{1,0:T(8,128)(2,1)} %bitcast.24), custom_call_target="tpu_custom_call" | custom-call | bytes 1146880 | tf_op jit(solution)/shard_map/pallas_call | solution.py:63
  17.9 0.1 collective-permute-start.1
  17.9 1.6 %collective-permute-done.1.refs_2_ = bf16[2,560,128]{2,1,0:T(8,128)(2,1)S(1)} collective-permute-done((bf16[2,560,128]{2,1,0:T(8,128)(2,1)S(1)}, bf16[2,560,128]{2,1,0:T(8,128)(2,1)S(1)}, u32[]{:S(2)}, u32[]{:S(2)}) %collective-permute-start.1) | collective-permute-done | bytes 286752 | tf_op jit(solution)/shard_map/ppermute | solution.py:452
  19.5 5.8 %all-to-all-done.refs_0_ = f32[16,40,112]{2,1,0:T(8,128)S(1)} async-done(((f32[16,40,112]{2,1,0:T(8,128)}), f32[16,40,112]{2,1,0:T(8,128)S(1)}, u32[]{:S(2)}, u32[]{:S(2)}) %all-to-all-start) | async-done | bytes 286752 | tf_op jit(solution)/shard_map/all_to_all | solution.py:455
  25.3 1.8 %shard_map.97 = (f32[16,72,112]{2,1,0:T(8,128)}, f32[5,112]{1,0:T(8,128)S(1)}, f32[5,256]{1,0:T(8,128)S(1)}) custom-call(f32[16,40,112]{2,1,0:T(8,128)S(1)} %all-to-all-done.refs_0_, bf16[2,560,128]{2,1,0:T(8,128)(2,1)S(1)} %get-tuple-element.35.refs_1_, bf16[2,560,128]{2,1,0:T(8,128)(2,1)S(1)} %collective-permute-done.1.refs_2_), custom_call_target="tpu_custom_call" | custom-call | flops 64225280 | bytes 1383616 | tf_op jit(solution)/shard_map/pallas_call | solution.py:63
  27.1 3.6 %all-to-all-start.1 = ((f32[16,72,112]{2,1,0:T(8,128)}), f32[16,72,112]{2,1,0:T(8,128)S(1)}, u32[]{:S(2)}, u32[]{:S(2)}) async-start(f32[16,72,112]{2,1,0:T(8,128)} %get-tuple-element.37), calls=%async_computation.1 | async-start | bytes 1179648 | tf_op jit(solution)/shard_map/all_to_all | solution.py:455
  30.7 6.3 %collective-permute-done.2.refs_1_ = bf16[128,2816]{1,0:T(8,128)(2,1)} collective-permute-done((bf16[128,2816]{1,0:T(8,128)(2,1)S(1)}, bf16[128,2816]{1,0:T(8,128)(2,1)}, u32[]{:S(2)}, u32[]{:S(2)}) %collective-permute-start.2) | collective-permute-done | bytes 720928 | tf_op jit(solution)/shard_map/ppermute | solution.py:398
  36.9 3.4 %collective-permute-start.5 = (bf16[128,2816]{1,0:T(8,128)(2,1)}, bf16[128,2816]{1,0:T(8,128)(2,1)}, u32[]{:S(2)}, u32[]{:S(2)}) collective-permute-start(bf16[128,2816]{1,0:T(8,128)(2,1)} %collective-permute-done.2.refs_1_), channel_id=1, source_target_pairs={{0,2},{2,4},{4,6},{3,1},{5,3},{7,5},{8,10},{10,12},{12,14},{11,9},... | collective-permute-start | bytes 2162696 | tf_op jit(solution)/shard_map/ppermute | solution.py:435
  40.3 0.0 collective-permute-done.3.refs_2_
  40.3 3.2 %shard_map.98 = (bf16[128,2816]{1,0:T(8,128)(2,1)}, f32[8,128]{1,0:T(8,128)S(1)}) custom-call(bf16[128,2816]{1,0:T(8,128)(2,1)S(1)} %get-tuple-element.40.refs_0_, bf16[128,2816]{1,0:T(8,128)(2,1)} %collective-permute-done.2.refs_1_, bf16[128,2816]{1,0:T(8,128)(2,1)} %collective-permute-done.3.refs_2_, f32[3,3,2816]{2,1,0:T(4,128)S(1)} %get-tuple-element.42.refs_3_.refs_4_), custom_call_target="tpu_custom_call" | custom-call | flops 500000000 | bytes 2989056 | tf_op jit(solution)/shard_map/pallas_call | solution.py:63
  43.5 0.1 collective-permute-start.6
  43.6 5.6 %all-to-all-done.1.refs_0_ = f32[16,72,112]{2,1,0:T(8,128)S(1)} async-done(((f32[16,72,112]{2,1,0:T(8,128)}), f32[16,72,112]{2,1,0:T(8,128)S(1)}, u32[]{:S(2)}, u32[]{:S(2)}) %all-to-all-start.1) | async-done | bytes 516128 | tf_op jit(solution)/shard_map/all_to_all | solution.py:455
  49.2 2.0 %shard_map.99 = (f32[16,40,112]{2,1,0:T(8,128)}, bf16[560,128]{1,0:T(8,128)(2,1)S(1)}, bf16[560,128]{1,0:T(8,128)(2,1)S(1)}) custom-call(f32[16,72,112]{2,1,0:T(8,128)S(1)} %all-to-all-done.1.refs_0_, bf16[2,560,128]{2,1,0:T(8,128)(2,1)S(1)} %get-tuple-element.35.refs_1_, bf16[2,560,128]{2,1,0:T(8,128)(2,1)S(1)} %collective-permute-done.1.refs_2_, ...), custom_call_target="tpu_custom_call" | custom-call | flops 64225280 | bytes 1670336 | tf_op jit(solution)/shard_map/pallas_call | solution.py:63
  51.2 0.0 copy-start
  51.2 0.7 copy-done
  51.8 7.1 %all-to-all-start.2 = ((f32[16,40,112]{2,1,0:T(8,128)}), f32[16,40,112]{2,1,0:T(8,128)S(1)}, u32[]{:S(2)}, u32[]{:S(2)}) async-start(f32[16,40,112]{2,1,0:T(8,128)} %get-tuple-element.47), calls=%async_computation.2 | async-start | bytes 655360 | tf_op jit(solution)/shard_map/all_to_all | solution.py:455
  58.9 0.1 collective-permute-start.4
  59.0 0.0 collective-permute-done.5.refs_2_
  59.0 2.5 %collective-permute-done.6.refs_3_ = bf16[128,2816]{1,0:T(8,128)(2,1)S(1)} collective-permute-done((bf16[128,2816]{1,0:T(8,128)(2,1)}, bf16[128,2816]{1,0:T(8,128)(2,1)S(1)}, u32[]{:S(2)}, u32[]{:S(2)}) %collective-permute-start.6) | collective-permute-done | bytes 720928 | tf_op jit(solution)/shard_map/ppermute | solution.py:437
  61.6 3.3 %shard_map.101 = (bf16[1,1,128,5632]{3,2,1,0:T(8,128)(2,1)}, f32[8,128]{1,0:T(8,128)S(1)}) custom-call(bf16[128,2816]{1,0:T(8,128)(2,1)S(1)} %get-tuple-element.40.refs_0_, bf16[128,2816]{1,0:T(8,128)(2,1)} %collective-permute-done.2.refs_1_, bf16[128,2816]{1,0:T(8,128)(2,1)} %collective-permute-done.5.refs_2_, ...), custom_call_target="tpu_custom_call" | custom-call | flops 10000000000 | bytes 4430848 | tf_op jit(solution)/shard_map/pallas_call | solution.py:63
  64.9 0.0 collective-permute-done.4.refs_1_
  64.9 0.7 %shard_map.100 = (bf16[1120,128]{1,0:T(8,128)(2,1)}, f32[8,128]{1,0:T(8,128)S(1)}) custom-call(bf16[560,128]{1,0:T(8,128)(2,1)S(1)} %get-tuple-element.44.refs_0_, bf16[560,128]{1,0:T(8,128)(2,1)S(1)} %collective-permute-done.4.refs_1_), custom_call_target="tpu_custom_call" | custom-call | bytes 577536 | tf_op jit(solution)/shard_map/pallas_call | solution.py:63
  65.7 4.4 %all-to-all-done.2.refs_0_ = f32[16,40,112]{2,1,0:T(8,128)S(1)} async-done(((f32[16,40,112]{2,1,0:T(8,128)}), f32[16,40,112]{2,1,0:T(8,128)S(1)}, u32[]{:S(2)}, u32[]{:S(2)}) %all-to-all-start.2) | async-done | bytes 286752 | tf_op jit(solution)/shard_map/all_to_all | solution.py:455
  70.1 0.5 shard_map.102
  70.6 0.1 collective-permute-start.7
  70.7 0.7 %shard_map.103 = (bf16[1120,128]{1,0:T(8,128)(2,1)}, bf16[1120,128]{1,0:T(8,128)(2,1)}) custom-call(bf16[2,560,128]{2,1,0:T(8,128)(2,1)S(1)} %get-tuple-element.52.refs_0_), custom_call_target="tpu_custom_call" | custom-call | bytes 860160 | tf_op jit(solution)/shard_map/pallas_call | solution.py:63
  71.4 0.8 %collective-permute-done.7.refs_0_ = bf16[2,560,128]{2,1,0:T(8,128)(2,1)S(1)} collective-permute-done((bf16[2,560,128]{2,1,0:T(8,128)(2,1)S(1)}, bf16[2,560,128]{2,1,0:T(8,128)(2,1)S(1)}, u32[]{:S(2)}, u32[]{:S(2)}) %collective-permute-start.7) | collective-permute-done | bytes 286752 | tf_op jit(solution)/shard_map/ppermute | solution.py:504
  72.2 0.7 shard_map.104
Async XLA Ops:
  1.8 1.9 %collective-permute-start = (bf16[2,560,128]{2,1,0:T(8,128)(2,1)S(1)}, bf16[2,560,128]{2,1,0:T(8,128)(2,1)S(1)}, u32[]{:S(2)}, u32[]{:S(2)}) collective-permute-start(bf16[2,560,128]{2,1,0:T(8,128)(2,1)S(1)} %get-tuple-element.32), channel_id=1, source_target_pairs={{0,8},{8,0},{1,9},{9,1},{2,10},{10,2},{3,11},{11,3},{4,12},{12,4},... | collective-permute-start | bytes 860168 | tf_op jit(solution)/shard_map/ppermute | solution.py:450
  5.4 19.9 %all-to-all-start = ((f32[16,40,112]{2,1,0:T(8,128)}), f32[16,40,112]{2,1,0:T(8,128)S(1)}, u32[]{:S(2)}, u32[]{:S(2)}) async-start(f32[16,40,112]{2,1,0:T(8,128)} %get-tuple-element.34), calls=%async_computation | async-start | bytes 655360 | tf_op jit(solution)/shard_map/all_to_all | solution.py:455
  13.5 23.5 %collective-permute-start.2 = (bf16[128,2816]{1,0:T(8,128)(2,1)S(1)}, bf16[128,2816]{1,0:T(8,128)(2,1)}, u32[]{:S(2)}, u32[]{:S(2)}) collective-permute-start(bf16[128,2816]{1,0:T(8,128)(2,1)S(1)} %get-tuple-element.41), channel_id=1, source_target_pairs={{0,1},{1,0},{2,3},{3,2},{4,5},{5,4},{6,7},{7,6},{8,9},{9,8},{10,11... | collective-permute-start | bytes 2162696 | tf_op jit(solution)/shard_map/ppermute | solution.py:398
  15.4 24.9 %collective-permute-start.3 = (bf16[128,2816]{1,0:T(8,128)(2,1)S(1)}, bf16[128,2816]{1,0:T(8,128)(2,1)}, u32[]{:S(2)}, u32[]{:S(2)}) collective-permute-start(bf16[128,2816]{1,0:T(8,128)(2,1)S(1)} %get-tuple-element.40.refs_0_), channel_id=1, source_target_pairs={{2,0},{4,2},{6,4},{1,3},{3,5},{5,7},{10,8},{12,10},{14,12},{9,11},... | collective-permute-start | bytes 2162696 | tf_op jit(solution)/shard_map/ppermute | solution.py:399
  17.9 1.6 %collective-permute-start.1 = (bf16[2,560,128]{2,1,0:T(8,128)(2,1)S(1)}, bf16[2,560,128]{2,1,0:T(8,128)(2,1)S(1)}, u32[]{:S(2)}, u32[]{:S(2)}) collective-permute-start(bf16[2,560,128]{2,1,0:T(8,128)(2,1)S(1)} %get-tuple-element.36), channel_id=1, source_target_pairs={{0,8},{8,0},{1,9},{9,1},{2,10},{10,2},{3,11},{11,3},{4,12},{12,4},... | collective-permute-start | bytes 860168 | tf_op jit(solution)/shard_map/ppermute | solution.py:452
  27.1 22.1 %all-to-all-start.1 = ((f32[16,72,112]{2,1,0:T(8,128)}), f32[16,72,112]{2,1,0:T(8,128)S(1)}, u32[]{:S(2)}, u32[]{:S(2)}) async-start(f32[16,72,112]{2,1,0:T(8,128)} %get-tuple-element.37), calls=%async_computation.1 | async-start | bytes 1179648 | tf_op jit(solution)/shard_map/all_to_all | solution.py:455
  36.9 22.1 %collective-permute-start.5 = (bf16[128,2816]{1,0:T(8,128)(2,1)}, bf16[128,2816]{1,0:T(8,128)(2,1)}, u32[]{:S(2)}, u32[]{:S(2)}) collective-permute-start(bf16[128,2816]{1,0:T(8,128)(2,1)} %collective-permute-done.2.refs_1_), channel_id=1, source_target_pairs={{0,2},{2,4},{4,6},{3,1},{5,3},{7,5},{8,10},{10,12},{12,14},{11,9},... | collective-permute-start | bytes 2162696 | tf_op jit(solution)/shard_map/ppermute | solution.py:435
  43.5 18.0 %collective-permute-start.6 = (bf16[128,2816]{1,0:T(8,128)(2,1)}, bf16[128,2816]{1,0:T(8,128)(2,1)S(1)}, u32[]{:S(2)}, u32[]{:S(2)}) collective-permute-start(bf16[128,2816]{1,0:T(8,128)(2,1)} %get-tuple-element.49), channel_id=1, source_target_pairs={{0,1},{1,0},{2,3},{3,2},{4,5},{5,4},{6,7},{7,6},{8,9},{9,8},{10,11... | collective-permute-start | bytes 2162696 | tf_op jit(solution)/shard_map/ppermute | solution.py:437
  51.2 0.7 copy-start
  51.8 18.3 %all-to-all-start.2 = ((f32[16,40,112]{2,1,0:T(8,128)}), f32[16,40,112]{2,1,0:T(8,128)S(1)}, u32[]{:S(2)}, u32[]{:S(2)}) async-start(f32[16,40,112]{2,1,0:T(8,128)} %get-tuple-element.47), calls=%async_computation.2 | async-start | bytes 655360 | tf_op jit(solution)/shard_map/all_to_all | solution.py:455
  58.9 6.0 %collective-permute-start.4 = (bf16[560,128]{1,0:T(8,128)(2,1)}, bf16[560,128]{1,0:T(8,128)(2,1)S(1)}, u32[]{:S(2)}, u32[]{:S(2)}) collective-permute-start(bf16[560,128]{1,0:T(8,128)(2,1)} %copy-done), channel_id=1, source_target_pairs={{0,8},{8,0},{1,9},{9,1},{2,10},{10,2},{3,11},{11,3},{4,12},{12,4},... | collective-permute-start | bytes 430088 | tf_op jit(solution)/shard_map/ppermute | solution.py:492
  70.6 1.6 %collective-permute-start.7 = (bf16[2,560,128]{2,1,0:T(8,128)(2,1)S(1)}, bf16[2,560,128]{2,1,0:T(8,128)(2,1)S(1)}, u32[]{:S(2)}, u32[]{:S(2)}) collective-permute-start(bf16[2,560,128]{2,1,0:T(8,128)(2,1)S(1)} %get-tuple-element.51), channel_id=1, source_target_pairs={{0,8},{8,0},{1,9},{9,1},{2,10},{10,2},{3,11},{11,3},{4,12},{12,4},... | collective-permute-start | bytes 860168 | tf_op jit(solution)/shard_map/ppermute | solution.py:504

commit v9 on v8

--- a/solution.py
+++ b/solution.py
@@ -20,7 +20,7 @@
 ORDER = [[], [('sent', 0)], [('kept', 0)]]
 SEND_COST = 500000000
 KEEP_COST = 10000000000
-CHIPS = ("y", "z", "x")
+CHIPS = ("z", "x", "y")
 F32 = jnp.float32
 BF16 = jnp.bfloat16
 
@@ -200,26 +200,34 @@
         pay[j, rows : 2 * rows] = whole[j * rows : (j + 1) * rows]
 
 
-def query_body(
-    n, rows, scale, got, qg, qg_got, norm_ref, inv_ref, pay, out_mine, out_theirs, whole
-):
+def scaled_state(whole, qg, qg_got, inv_ref, scale, h):
+    feat = jnp.maximum(head_of(qg, qg_got, 0, h), 0)
+    grad = head_of(qg, qg_got, 1, h)
+    hi, lo = pieces(whole[h * HD : (h + 1) * HD])
+    prod = dot(hi, grad, NN) + dot(lo, grad, NN)
+    query = feat.astype(F32)
+    inv = inv_ref[h : h + 1]
+    weight = inv * scale
+    proj = jnp.sum(query * prod, axis=0, keepdims=True) * weight * inv
+    return feat, query, prod, weight, proj
+
+
+def norm_body(n, rows, scale, got, qg, qg_got, inv_ref, pay, whole):
     total = sum_of(got, n, rows, 2 * rows)
     for j in range(n):
         whole[j * rows : (j + 1) * rows] = got[j, :rows]
         pay[j, :rows] = total
+    for h in range(HALF):
+        feat, _, _, _, proj = scaled_state(whole, qg, qg_got, inv_ref, scale, h)
+        pay[:, rows + h : rows + h + 1] = spread(-exact_rows(proj, feat, NT), n)
+
+
+def query_body(scale, whole, qg, qg_got, norm_ref, inv_ref, out_mine, out_theirs):
     norms = columns(norm_ref[...])
     tok = out_mine.shape[1]
     for h in range(HALF):
         part = slice(h * HD, (h + 1) * HD)
-        feat = jnp.maximum(head_of(qg, qg_got, 0, h), 0)
-        query = feat.astype(F32)
-        grad = head_of(qg, qg_got, 1, h)
-        hi, lo = pieces(whole[part])
-        prod = dot(hi, grad, NN) + dot(lo, grad, NN)
-        inv = inv_ref[h : h + 1]
-        weight = inv * scale
-        proj = jnp.sum(query * prod, axis=0, keepdims=True) * weight * inv
-        pay[:, rows + h : rows + h + 1] = spread(-exact_rows(proj, feat, NT), n)
+        _, query, prod, weight, proj = scaled_state(whole, qg, qg_got, inv_ref, scale, h)
         out = prod * weight - norms[:HD, h : h + 1] * proj
         out = jnp.where(query > 0, out, 0.0).astype(BF16)
         out_mine[part] = out[:, :tok]
@@ -480,14 +488,19 @@
         after=tied(0),
     )
     got = exchange(pay)
-    pay, query_mine, query_send = call(
-        functools.partial(query_body, n, rows, scale),
-        [sd((n, pay_one, HD), F32)] + [sd((half, tok), BF16)] * 2,
-        (got, qg, qg_got, norm, inv),
-        scratch,
+    pay, state = call(
+        functools.partial(norm_body, n, rows, scale),
+        [sd((n, pay_one, HD), F32), sd((n * rows, HD), F32)],
+        (got, qg, qg_got, inv),
         flops=4 * macs,
         pinned=1,
         after=tied(1),
+    )
+    query_mine, query_send = call(
+        functools.partial(query_body, scale),
+        [sd((half, tok), BF16)] * 2,
+        (state, qg, qg_got, norm, inv),
+        flops=4 * macs,
     )
     query_got = lax.ppermute(query_send, "c", swap)
     whole_shape = sd((2 * half, tok), BF16)

time: 73.5 us -> 72.9 us (level)
  starting transfers between devices: 26.2 us -> 22.8 us
  waiting for transfers between devices: 27 us -> 30 us
    all_to_all x3, starting transfers between devices: 18.8 us -> 16.4 us  [exchange(): return lax.all_to_all(pay, CHIPS, split_axis=0, concat_axis=0, tiled=True)]
    ppermute x1, waiting for transfers between devices: 6.29 us -> 7.93 us  [move_in(): near = lax.ppermute(row_send[i], 'x', swap)]
    all_to_all x3, waiting for transfers between devices: 15.8 us -> 17.1 us  [exchange(): return lax.all_to_all(pay, CHIPS, split_axis=0, concat_axis=0, tiled=True)]
    ppermute x1, starting transfers between devices: 3.38 us -> 2.44 us  [shards(): onward[i] = lax.ppermute(near[i], ('z', 'x'), even_up + odd_down)]
    pallas_call x12 -> x13, Pallas kernels: 18.3 us -> 18.7 us  [call(): pl.pallas_call(ordered, out_shape=shapes, in_specs=[free if any_in else f...]
where the time goes in v9:
time: 72.9 us; the launch traced here: 72.3 us
  waiting for transfers between devices  30 us (41%)
  starting transfers between devices  22.8 us (31%)
  Pallas kernels  18.7 us (26%)
  between operations  0.81 us (1%)
    pallas_call x13, Pallas kernels, call(): pl.pallas_call(ordered, out_shape=shapes, in_specs=[free if any_in else f...  18.7 us
    all_to_all x3, waiting for transfers between devices, exchange(): return lax.all_to_all(pay, CHIPS, split_axis=0, concat_axis=0, tiled=True)  17.1 us
    all_to_all x3, starting transfers between devices, exchange(): return lax.all_to_all(pay, CHIPS, split_axis=0, concat_axis=0, tiled=True)  16.4 us
    ppermute x1, waiting for transfers between devices, move_in(): near = lax.ppermute(row_send[i], 'x', swap)  7.93 us
    ppermute x1, waiting for transfers between devices, shards(): back[i] = lax.ppermute(out_send, 'x', swap)  2.53 us
    ppermute x1, starting transfers between devices, shards(): onward[i] = lax.ppermute(near[i], ('z', 'x'), even_up + odd_down)  2.44 us
    ppermute x1, starting transfers between devices, move_in(): near = lax.ppermute(row_send[i], 'x', swap)  1.93 us
    ppermute x1, waiting for transfers between devices, shards(): qg_got = lax.ppermute(qg_send, 'c', swap)  1.56 us
  transfers between devices with their start and end apart: 11, of which 7 were waited for; matrix products, arithmetic and copies ran while one was open for 0% of the time, Pallas kernels for 20%

profile of v9, /device:TPU:0, one launch (start us, length us, event | category | flops | bytes accessed | tf_op | source)
XLA Modules:
  0.0 72.3 jit_solution(16994842187945957564)
XLA Ops:
  0.6 1.2 %shard_map.93 = (bf16[2,560,128]{2,1,0:T(8,128)(2,1)S(1)}, bf16[2,560,128]{2,1,0:T(8,128)(2,1)S(1)}) custom-call(bf16[1120,128]{1,0:T(8,128)(2,1)} %bitcast.21, bf16[1120,128]{1,0:T(8,128)(2,1)} %bitcast.22), custom_call_target="tpu_custom_call" | custom-call | bytes 1146880 | tf_op jit(solution)/shard_map/pallas_call | solution.py:63
  1.8 0.5 collective-permute-start
  2.3 1.4 %shard_map.94 = (bf16[128,2816]{1,0:T(8,128)(2,1)S(1)}, bf16[128,2816]{1,0:T(8,128)(2,1)S(1)}, f32[3,3,2816]{2,1,0:T(4,128)S(1)}, f32[8,128]{1,0:T(8,128)S(1)}) custom-call(bf16[1,1,128,5632]{3,2,1,0:T(8,128)(2,1)} %refs_0_.1, f32[3,3,5632]{2,1,0:T(4,128)} %refs_1_.1), custom_call_target="tpu_custom_call" | custom-call | bytes 3191808 | tf_op jit(solution)/shard_map/pallas_call | solution.py:63
  3.7 0.0 collective-permute-done.refs_1_.refs_2_
  3.7 1.7 %shard_map.95 = (f32[16,40,112]{2,1,0:T(8,128)}, f32[8,128]{1,0:T(8,128)}) custom-call(bf16[2,560,128]{2,1,0:T(8,128)(2,1)S(1)} %get-tuple-element.32.refs_0_.refs_1_, bf16[2,560,128]{2,1,0:T(8,128)(2,1)S(1)} %collective-permute-done.refs_1_.refs_2_, f32[8,128]{1,0:T(8,128)S(1)} %get-tuple-element.34.refs_2_), custom_call_target="tpu_custom_call" | custom-call | flops 32112640 | bytes 864256 | tf_op jit(solution)/shard_map/pallas_call | solution.py:63
  5.4 8.1 %all-to-all-start = ((f32[16,40,112]{2,1,0:T(8,128)}), f32[16,40,112]{2,1,0:T(8,128)S(1)}, u32[]{:S(2)}, u32[]{:S(2)}) async-start(f32[16,40,112]{2,1,0:T(8,128)} %get-tuple-element.35), calls=%async_computation | async-start | bytes 655360 | tf_op jit(solution)/shard_map/all_to_all | solution.py:463
  13.5 1.9 %collective-permute-start.2 = (bf16[128,2816]{1,0:T(8,128)(2,1)S(1)}, bf16[128,2816]{1,0:T(8,128)(2,1)}, u32[]{:S(2)}, u32[]{:S(2)}) collective-permute-start(bf16[128,2816]{1,0:T(8,128)(2,1)S(1)} %get-tuple-element.41), channel_id=1, source_target_pairs={{0,1},{1,0},{2,3},{3,2},{4,5},{5,4},{6,7},{7,6},{8,9},{9,8},{10,11... | collective-permute-start | bytes 2162696 | tf_op jit(solution)/shard_map/ppermute | solution.py:406
  15.4 1.3 %collective-permute-start.3 = (bf16[128,2816]{1,0:T(8,128)(2,1)S(1)}, bf16[128,2816]{1,0:T(8,128)(2,1)}, u32[]{:S(2)}, u32[]{:S(2)}) collective-permute-start(bf16[128,2816]{1,0:T(8,128)(2,1)S(1)} %get-tuple-element.40.refs_0_), channel_id=1, source_target_pairs={{2,0},{4,2},{6,4},{1,3},{3,5},{5,7},{10,8},{12,10},{14,12},{9,11},... | collective-permute-start | bytes 2162696 | tf_op jit(solution)/shard_map/ppermute | solution.py:407
  16.7 1.2 %shard_map.96 = (bf16[2,560,128]{2,1,0:T(8,128)(2,1)S(1)}, bf16[2,560,128]{2,1,0:T(8,128)(2,1)S(1)}) custom-call(bf16[1120,128]{1,0:T(8,128)(2,1)} %bitcast.23, bf16[1120,128]{1,0:T(8,128)(2,1)} %bitcast.24), custom_call_target="tpu_custom_call" | custom-call | bytes 1146880 | tf_op jit(solution)/shard_map/pallas_call | solution.py:63
  17.9 0.1 collective-permute-start.1
  17.9 1.6 %collective-permute-done.1.refs_2_ = bf16[2,560,128]{2,1,0:T(8,128)(2,1)S(1)} collective-permute-done((bf16[2,560,128]{2,1,0:T(8,128)(2,1)S(1)}, bf16[2,560,128]{2,1,0:T(8,128)(2,1)S(1)}, u32[]{:S(2)}, u32[]{:S(2)}) %collective-permute-start.1) | collective-permute-done | bytes 286752 | tf_op jit(solution)/shard_map/ppermute | solution.py:460
  19.5 5.9 %all-to-all-done.refs_0_ = f32[16,40,112]{2,1,0:T(8,128)S(1)} async-done(((f32[16,40,112]{2,1,0:T(8,128)}), f32[16,40,112]{2,1,0:T(8,128)S(1)}, u32[]{:S(2)}, u32[]{:S(2)}) %all-to-all-start) | async-done | bytes 286752 | tf_op jit(solution)/shard_map/all_to_all | solution.py:463
  25.4 1.8 %shard_map.97 = (f32[16,72,112]{2,1,0:T(8,128)}, f32[5,112]{1,0:T(8,128)S(1)}, f32[5,256]{1,0:T(8,128)S(1)}) custom-call(f32[16,40,112]{2,1,0:T(8,128)S(1)} %all-to-all-done.refs_0_, bf16[2,560,128]{2,1,0:T(8,128)(2,1)S(1)} %get-tuple-element.36.refs_1_, bf16[2,560,128]{2,1,0:T(8,128)(2,1)S(1)} %collective-permute-done.1.refs_2_), custom_call_target="tpu_custom_call" | custom-call | flops 64225280 | bytes 1383616 | tf_op jit(solution)/shard_map/pallas_call | solution.py:63
  27.1 3.6 %all-to-all-start.1 = ((f32[16,72,112]{2,1,0:T(8,128)}), f32[16,72,112]{2,1,0:T(8,128)S(1)}, u32[]{:S(2)}, u32[]{:S(2)}) async-start(f32[16,72,112]{2,1,0:T(8,128)} %get-tuple-element.38), calls=%async_computation.1 | async-start | bytes 1179648 | tf_op jit(solution)/shard_map/all_to_all | solution.py:463
  30.7 7.9 %collective-permute-done.2.refs_1_ = bf16[128,2816]{1,0:T(8,128)(2,1)} collective-permute-done((bf16[128,2816]{1,0:T(8,128)(2,1)S(1)}, bf16[128,2816]{1,0:T(8,128)(2,1)}, u32[]{:S(2)}, u32[]{:S(2)}) %collective-permute-start.2) | collective-permute-done | bytes 720928 | tf_op jit(solution)/shard_map/ppermute | solution.py:406
  38.7 2.4 %collective-permute-start.5 = (bf16[128,2816]{1,0:T(8,128)(2,1)}, bf16[128,2816]{1,0:T(8,128)(2,1)}, u32[]{:S(2)}, u32[]{:S(2)}) collective-permute-start(bf16[128,2816]{1,0:T(8,128)(2,1)} %collective-permute-done.2.refs_1_), channel_id=1, source_target_pairs={{0,2},{2,4},{4,6},{3,1},{5,3},{7,5},{8,10},{10,12},{12,14},{11,9},... | collective-permute-start | bytes 2162696 | tf_op jit(solution)/shard_map/ppermute | solution.py:443
  41.1 0.0 collective-permute-done.3.refs_2_
  41.1 3.2 %shard_map.98 = (bf16[128,2816]{1,0:T(8,128)(2,1)}, f32[8,128]{1,0:T(8,128)S(1)}) custom-call(bf16[128,2816]{1,0:T(8,128)(2,1)S(1)} %get-tuple-element.40.refs_0_, bf16[128,2816]{1,0:T(8,128)(2,1)} %collective-permute-done.2.refs_1_, bf16[128,2816]{1,0:T(8,128)(2,1)} %collective-permute-done.3.refs_2_, f32[3,3,2816]{2,1,0:T(4,128)S(1)} %get-tuple-element.42.refs_3_.refs_4_), custom_call_target="tpu_custom_call" | custom-call | flops 500000000 | bytes 2989056 | tf_op jit(solution)/shard_map/pallas_call | solution.py:63
  44.3 0.1 collective-permute-start.6
  44.4 7.2 %all-to-all-done.1.refs_0_ = f32[16,72,112]{2,1,0:T(8,128)S(1)} async-done(((f32[16,72,112]{2,1,0:T(8,128)}), f32[16,72,112]{2,1,0:T(8,128)S(1)}, u32[]{:S(2)}, u32[]{:S(2)}) %all-to-all-start.1) | async-done | bytes 516128 | tf_op jit(solution)/shard_map/all_to_all | solution.py:463
  51.6 1.9 %shard_map.99 = (f32[16,40,112]{2,1,0:T(8,128)}, f32[560,112]{1,0:T(8,128)S(1)}) custom-call(f32[16,72,112]{2,1,0:T(8,128)S(1)} %all-to-all-done.1.refs_0_, bf16[2,560,128]{2,1,0:T(8,128)(2,1)S(1)} %get-tuple-element.36.refs_1_, bf16[2,560,128]{2,1,0:T(8,128)(2,1)S(1)} %collective-permute-done.1.refs_2_, f32[5,256]{1,0:T(8,128)S(1)} %get-tuple-element.39.refs_3_.refs_4_, ...), custom_call_target="tpu_custom_call" | custom-call | flops 64225280 | bytes 1632256 | tf_op jit(solution)/shard_map/pallas_call | solution.py:63
  53.5 4.7 %all-to-all-start.2 = ((f32[16,40,112]{2,1,0:T(8,128)}), f32[16,40,112]{2,1,0:T(8,128)S(1)}, u32[]{:S(2)}, u32[]{:S(2)}) async-start(f32[16,40,112]{2,1,0:T(8,128)} %get-tuple-element.49), calls=%async_computation.2 | async-start | bytes 655360 | tf_op jit(solution)/shard_map/all_to_all | solution.py:463
  58.3 0.4 shard_map.100
  58.7 0.1 collective-permute-start.4
  58.8 0.0 collective-permute-done.5.refs_2_
  58.8 2.5 %collective-permute-done.6.refs_3_ = bf16[128,2816]{1,0:T(8,128)(2,1)} collective-permute-done((bf16[128,2816]{1,0:T(8,128)(2,1)}, bf16[128,2816]{1,0:T(8,128)(2,1)}, u32[]{:S(2)}, u32[]{:S(2)}) %collective-permute-start.6) | collective-permute-done | bytes 720928 | tf_op jit(solution)/shard_map/ppermute | solution.py:445
  61.3 3.4 %shard_map.102 = (bf16[1,1,128,5632]{3,2,1,0:T(8,128)(2,1)}, f32[8,128]{1,0:T(8,128)S(1)}) custom-call(bf16[128,2816]{1,0:T(8,128)(2,1)S(1)} %get-tuple-element.40.refs_0_, bf16[128,2816]{1,0:T(8,128)(2,1)} %collective-permute-done.2.refs_1_, bf16[128,2816]{1,0:T(8,128)(2,1)} %collective-permute-done.5.refs_2_, ...), custom_call_target="tpu_custom_call" | custom-call | flops 10000000000 | bytes 4430848 | tf_op jit(solution)/shard_map/pallas_call | solution.py:63
  64.7 0.0 collective-permute-done.4.refs_1_
  64.7 0.7 %shard_map.101 = (bf16[1120,128]{1,0:T(8,128)(2,1)}, f32[8,128]{1,0:T(8,128)S(1)}) custom-call(bf16[560,128]{1,0:T(8,128)(2,1)S(1)} %get-tuple-element.46.refs_0_, bf16[560,128]{1,0:T(8,128)(2,1)S(1)} %collective-permute-done.4.refs_1_), custom_call_target="tpu_custom_call" | custom-call | bytes 577536 | tf_op jit(solution)/shard_map/pallas_call | solution.py:63
  65.5 4.0 %all-to-all-done.2.refs_0_ = f32[16,40,112]{2,1,0:T(8,128)S(1)} async-done(((f32[16,40,112]{2,1,0:T(8,128)}), f32[16,40,112]{2,1,0:T(8,128)S(1)}, u32[]{:S(2)}, u32[]{:S(2)}) %all-to-all-start.2) | async-done | bytes 286752 | tf_op jit(solution)/shard_map/all_to_all | solution.py:463
  69.5 0.5 shard_map.103
  70.0 0.1 collective-permute-start.7
  70.1 0.7 %shard_map.104 = (bf16[1120,128]{1,0:T(8,128)(2,1)}, bf16[1120,128]{1,0:T(8,128)(2,1)}) custom-call(bf16[2,560,128]{2,1,0:T(8,128)(2,1)S(1)} %get-tuple-element.54.refs_0_), custom_call_target="tpu_custom_call" | custom-call | bytes 860160 | tf_op jit(solution)/shard_map/pallas_call | solution.py:63
  70.8 0.8 %collective-permute-done.7.refs_0_ = bf16[2,560,128]{2,1,0:T(8,128)(2,1)S(1)} collective-permute-done((bf16[2,560,128]{2,1,0:T(8,128)(2,1)S(1)}, bf16[2,560,128]{2,1,0:T(8,128)(2,1)S(1)}, u32[]{:S(2)}, u32[]{:S(2)}) %collective-permute-start.7) | collective-permute-done | bytes 286752 | tf_op jit(solution)/shard_map/ppermute | solution.py:517
  71.6 0.7 shard_map.105
Async XLA Ops:
  1.8 1.9 %collective-permute-start = (bf16[2,560,128]{2,1,0:T(8,128)(2,1)S(1)}, bf16[2,560,128]{2,1,0:T(8,128)(2,1)S(1)}, u32[]{:S(2)}, u32[]{:S(2)}) collective-permute-start(bf16[2,560,128]{2,1,0:T(8,128)(2,1)S(1)} %get-tuple-element.33), channel_id=1, source_target_pairs={{0,8},{8,0},{1,9},{9,1},{2,10},{10,2},{3,11},{11,3},{4,12},{12,4},... | collective-permute-start | bytes 860168 | tf_op jit(solution)/shard_map/ppermute | solution.py:458
  5.4 20.0 %all-to-all-start = ((f32[16,40,112]{2,1,0:T(8,128)}), f32[16,40,112]{2,1,0:T(8,128)S(1)}, u32[]{:S(2)}, u32[]{:S(2)}) async-start(f32[16,40,112]{2,1,0:T(8,128)} %get-tuple-element.35), calls=%async_computation | async-start | bytes 655360 | tf_op jit(solution)/shard_map/all_to_all | solution.py:463
  13.5 25.2 %collective-permute-start.2 = (bf16[128,2816]{1,0:T(8,128)(2,1)S(1)}, bf16[128,2816]{1,0:T(8,128)(2,1)}, u32[]{:S(2)}, u32[]{:S(2)}) collective-permute-start(bf16[128,2816]{1,0:T(8,128)(2,1)S(1)} %get-tuple-element.41), channel_id=1, source_target_pairs={{0,1},{1,0},{2,3},{3,2},{4,5},{5,4},{6,7},{7,6},{8,9},{9,8},{10,11... | collective-permute-start | bytes 2162696 | tf_op jit(solution)/shard_map/ppermute | solution.py:406
  15.4 25.7 %collective-permute-start.3 = (bf16[128,2816]{1,0:T(8,128)(2,1)S(1)}, bf16[128,2816]{1,0:T(8,128)(2,1)}, u32[]{:S(2)}, u32[]{:S(2)}) collective-permute-start(bf16[128,2816]{1,0:T(8,128)(2,1)S(1)} %get-tuple-element.40.refs_0_), channel_id=1, source_target_pairs={{2,0},{4,2},{6,4},{1,3},{3,5},{5,7},{10,8},{12,10},{14,12},{9,11},... | collective-permute-start | bytes 2162696 | tf_op jit(solution)/shard_map/ppermute | solution.py:407
  17.9 1.6 %collective-permute-start.1 = (bf16[2,560,128]{2,1,0:T(8,128)(2,1)S(1)}, bf16[2,560,128]{2,1,0:T(8,128)(2,1)S(1)}, u32[]{:S(2)}, u32[]{:S(2)}) collective-permute-start(bf16[2,560,128]{2,1,0:T(8,128)(2,1)S(1)} %get-tuple-element.37), channel_id=1, source_target_pairs={{0,8},{8,0},{1,9},{9,1},{2,10},{10,2},{3,11},{11,3},{4,12},{12,4},... | collective-permute-start | bytes 860168 | tf_op jit(solution)/shard_map/ppermute | solution.py:460
  27.1 24.5 %all-to-all-start.1 = ((f32[16,72,112]{2,1,0:T(8,128)}), f32[16,72,112]{2,1,0:T(8,128)S(1)}, u32[]{:S(2)}, u32[]{:S(2)}) async-start(f32[16,72,112]{2,1,0:T(8,128)} %get-tuple-element.38), calls=%async_computation.1 | async-start | bytes 1179648 | tf_op jit(solution)/shard_map/all_to_all | solution.py:463
  38.7 20.1 %collective-permute-start.5 = (bf16[128,2816]{1,0:T(8,128)(2,1)}, bf16[128,2816]{1,0:T(8,128)(2,1)}, u32[]{:S(2)}, u32[]{:S(2)}) collective-permute-start(bf16[128,2816]{1,0:T(8,128)(2,1)} %collective-permute-done.2.refs_1_), channel_id=1, source_target_pairs={{0,2},{2,4},{4,6},{3,1},{5,3},{7,5},{8,10},{10,12},{12,14},{11,9},... | collective-permute-start | bytes 2162696 | tf_op jit(solution)/shard_map/ppermute | solution.py:443
  44.3 17.0 %collective-permute-start.6 = (bf16[128,2816]{1,0:T(8,128)(2,1)}, bf16[128,2816]{1,0:T(8,128)(2,1)}, u32[]{:S(2)}, u32[]{:S(2)}) collective-permute-start(bf16[128,2816]{1,0:T(8,128)(2,1)} %get-tuple-element.51), channel_id=1, source_target_pairs={{0,1},{1,0},{2,3},{3,2},{4,5},{5,4},{6,7},{7,6},{8,9},{9,8},{10,11... | collective-permute-start | bytes 2162696 | tf_op jit(solution)/shard_map/ppermute | solution.py:445
  53.5 16.0 %all-to-all-start.2 = ((f32[16,40,112]{2,1,0:T(8,128)}), f32[16,40,112]{2,1,0:T(8,128)S(1)}, u32[]{:S(2)}, u32[]{:S(2)}) async-start(f32[16,40,112]{2,1,0:T(8,128)} %get-tuple-element.49), calls=%async_computation.2 | async-start | bytes 655360 | tf_op jit(solution)/shard_map/all_to_all | solution.py:463
  58.7 6.1 %collective-permute-start.4 = (bf16[560,128]{1,0:T(8,128)(2,1)S(1)}, bf16[560,128]{1,0:T(8,128)(2,1)S(1)}, u32[]{:S(2)}, u32[]{:S(2)}) collective-permute-start(bf16[560,128]{1,0:T(8,128)(2,1)S(1)} %get-tuple-element.47), channel_id=1, source_target_pairs={{0,8},{8,0},{1,9},{9,1},{2,10},{10,2},{3,11},{11,3},{4,12},{12,4},... | collective-permute-start | bytes 430088 | tf_op jit(solution)/shard_map/ppermute | solution.py:505
  70.0 1.6 %collective-permute-start.7 = (bf16[2,560,128]{2,1,0:T(8,128)(2,1)S(1)}, bf16[2,560,128]{2,1,0:T(8,128)(2,1)S(1)}, u32[]{:S(2)}, u32[]{:S(2)}) collective-permute-start(bf16[2,560,128]{2,1,0:T(8,128)(2,1)S(1)} %get-tuple-element.53), channel_id=1, source_target_pairs={{0,8},{8,0},{1,9},{9,1},{2,10},{10,2},{3,11},{11,3},{4,12},{12,4},... | collective-permute-start | bytes 860168 | tf_op jit(solution)/shard_map/ppermute | solution.py:517

commit v10 on v9

--- a/solution.py
+++ b/solution.py
@@ -172,21 +172,40 @@
     return total
 
 
-def state_body(n, rows, kv, kv_got, pay, token, whole):
+def deliver(pay, out, whole, sems, n, rows, first, done, todo):
+    while todo and (todo[0] + 1) * rows <= done or todo and done >= HALF * HD:
+        j = todo.pop(0)
+        pay[j, first : first + rows] = whole[j * rows : (j + 1) * rows]
+        pltpu.make_async_copy(pay.at[j], out.at[j], sems.at[j]).start()
+
+
+def arrive(pay, out, sems, n):
+    for j in range(n):
+        pltpu.make_async_copy(pay.at[j], out.at[j], sems.at[j]).wait()
+
+
+def state_body(n, rows, kv, kv_got, out, token, whole, pay, sems):
     token[...] = jnp.zeros(token.shape, F32)
+    for h in range(HALF):
+        key = jnp.maximum(head_of(kv, kv_got, 0, h), 0)
+        norm = dot(jnp.ones((8, key.shape[1]), BF16), key, NT)[:1]
+        pay[:, rows + h : rows + h + 1] = spread(norm, n)
+    todo = list(range(n))
     for h in range(HALF):
         key = jnp.maximum(head_of(kv, kv_got, 0, h), 0)
         val = head_of(kv, kv_got, 1, h)
         whole[h * HD : (h + 1) * HD] = dot(key, val, NT)
-        norm = dot(jnp.ones((8, key.shape[1]), BF16), key, NT)[:1]
-        pay[:, rows + h : rows + h + 1] = spread(norm, n)
-    for j in range(n):
-        pay[j, :rows] = whole[j * rows : (j + 1) * rows]
-
-
-def grad_body(n, rows, scale, got, qg, qg_got, pay, norm_ref, inv_ref, whole):
+        deliver(pay, out, whole, sems, n, rows, 0, (h + 1) * HD, todo)
+    arrive(pay, out, sems, n)
+
+
+def grad_body(n, rows, scale, got, qg, qg_got, out, norm_ref, inv_ref, whole, pay, sems):
     total = sum_of(got, n, 0, rows + HALF)
     norm_ref[...] = total[rows:]
+    shard = total[:rows]
+    for j in range(n):
+        pay[j, :rows] = shard
+    todo = list(range(n))
     for h in range(HALF):
         query = jnp.maximum(head_of(qg, qg_got, 0, h), 0)
         grad = head_of(qg, qg_got, 1, h)
@@ -194,10 +213,8 @@
         inv_ref[h : h + 1] = inv
         hi, lo = pieces(grad.astype(F32) * (inv * scale))
         whole[h * HD : (h + 1) * HD] = dot(query, hi, NT) + dot(query, lo, NT)
-    shard = total[:rows]
-    for j in range(n):
-        pay[j, :rows] = shard
-        pay[j, rows : 2 * rows] = whole[j * rows : (j + 1) * rows]
+        deliver(pay, out, whole, sems, n, rows, rows, (h + 1) * HD, todo)
+    arrive(pay, out, sems, n)
 
 
 def scaled_state(whole, qg, qg_got, inv_ref, scale, h):
@@ -467,10 +484,10 @@
         functools.partial(state_body, n, rows),
         [sd((n, pay_one, HD), F32), token],
         (kv, kv_got),
-        scratch,
+        scratch + [pltpu.VMEM((n, pay_one, HD), F32), pltpu.SemaphoreType.DMA((n,))],
         flops=2 * macs,
         after=(halved[0],),
-        pinned=1,
+        hbm_out=1,
     )
     got = exchange(pay)
     ties = {"near": near, "far": far, "sent": sent, "kept": kept}
@@ -482,9 +499,9 @@
         functools.partial(grad_body, n, rows, scale),
         [sd((n, pay_two, HD), F32), sd((HALF, HD), F32), sd((HALF, 2 * tok), F32)],
         (got, qg, qg_got),
-        scratch,
+        scratch + [pltpu.VMEM((n, pay_two, HD), F32), pltpu.SemaphoreType.DMA((n,))],
         flops=4 * macs,
-        pinned=1,
+        hbm_out=1,
         after=tied(0),
     )
     got = exchange(pay)

time: 72.9 us -> 72.8 us (level)
  no operation moved by 1% of the time
where the time goes in v10:
time: 72.8 us; the launch traced here: 72.3 us
  waiting for transfers between devices  30.1 us (41%)
  starting transfers between devices  22.7 us (31%)
  Pallas kernels  18.7 us (26%)
  between operations  0.81 us (1%)
    pallas_call x13, Pallas kernels, call(): pl.pallas_call(ordered, out_shape=shapes, in_specs=[free if any_in else f...  18.7 us
    all_to_all x3, waiting for transfers between devices, exchange(): return lax.all_to_all(pay, CHIPS, split_axis=0, concat_axis=0, tiled=True)  17.1 us
    all_to_all x3, starting transfers between devices, exchange(): return lax.all_to_all(pay, CHIPS, split_axis=0, concat_axis=0, tiled=True)  16.4 us
    ppermute x1, waiting for transfers between devices, move_in(): near = lax.ppermute(row_send[i], 'x', swap)  8.13 us
    ppermute x1, waiting for transfers between devices, shards(): back[i] = lax.ppermute(out_send, 'x', swap)  2.51 us
    ppermute x1, starting transfers between devices, shards(): onward[i] = lax.ppermute(near[i], ('z', 'x'), even_up + odd_down)  2.29 us
    ppermute x1, starting transfers between devices, move_in(): near = lax.ppermute(row_send[i], 'x', swap)  1.93 us
    ppermute x1, waiting for transfers between devices, shards(): qg_got = lax.ppermute(qg_send, 'c', swap)  1.56 us
  transfers between devices with their start and end apart: 11, of which 7 were waited for; matrix products, arithmetic and copies ran while one was open for 0% of the time, Pallas kernels for 20%

profile of v10, /device:TPU:0, one launch (start us, length us, event | category | flops | bytes accessed | tf_op | source)
XLA Modules:
  0.0 72.3 jit_solution(9073879081548594049)
XLA Ops:
  0.6 1.2 %shard_map.93 = (bf16[2,560,128]{2,1,0:T(8,128)(2,1)S(1)}, bf16[2,560,128]{2,1,0:T(8,128)(2,1)S(1)}) custom-call(bf16[1120,128]{1,0:T(8,128)(2,1)} %bitcast.21, bf16[1120,128]{1,0:T(8,128)(2,1)} %bitcast.22), custom_call_target="tpu_custom_call" | custom-call | bytes 1146880 | tf_op jit(solution)/shard_map/pallas_call | solution.py:63
  1.8 0.5 collective-permute-start
  2.3 1.4 %shard_map.94 = (bf16[128,2816]{1,0:T(8,128)(2,1)S(1)}, bf16[128,2816]{1,0:T(8,128)(2,1)S(1)}, f32[3,3,2816]{2,1,0:T(4,128)S(1)}, f32[8,128]{1,0:T(8,128)S(1)}) custom-call(bf16[1,1,128,5632]{3,2,1,0:T(8,128)(2,1)} %refs_0_.1, f32[3,3,5632]{2,1,0:T(4,128)} %refs_1_.1), custom_call_target="tpu_custom_call" | custom-call | bytes 3191808 | tf_op jit(solution)/shard_map/pallas_call | solution.py:63
  3.7 0.0 collective-permute-done.refs_1_.refs_2_
  3.7 1.7 %shard_map.95 = (f32[16,40,112]{2,1,0:T(8,128)}, f32[8,128]{1,0:T(8,128)}) custom-call(bf16[2,560,128]{2,1,0:T(8,128)(2,1)S(1)} %get-tuple-element.32.refs_0_.refs_1_, bf16[2,560,128]{2,1,0:T(8,128)(2,1)S(1)} %collective-permute-done.refs_1_.refs_2_, f32[8,128]{1,0:T(8,128)S(1)} %get-tuple-element.34.refs_2_), custom_call_target="tpu_custom_call" | custom-call | flops 32112640 | bytes 864256 | tf_op jit(solution)/shard_map/pallas_call | solution.py:63
  5.4 8.1 %all-to-all-start = ((f32[16,40,112]{2,1,0:T(8,128)}), f32[16,40,112]{2,1,0:T(8,128)S(1)}, u32[]{:S(2)}, u32[]{:S(2)}) async-start(f32[16,40,112]{2,1,0:T(8,128)} %get-tuple-element.35), calls=%async_computation | async-start | bytes 655360 | tf_op jit(solution)/shard_map/all_to_all | solution.py:480
  13.5 1.9 %collective-permute-start.2 = (bf16[128,2816]{1,0:T(8,128)(2,1)S(1)}, bf16[128,2816]{1,0:T(8,128)(2,1)}, u32[]{:S(2)}, u32[]{:S(2)}) collective-permute-start(bf16[128,2816]{1,0:T(8,128)(2,1)S(1)} %get-tuple-element.41), channel_id=1, source_target_pairs={{0,1},{1,0},{2,3},{3,2},{4,5},{5,4},{6,7},{7,6},{8,9},{9,8},{10,11... | collective-permute-start | bytes 2162696 | tf_op jit(solution)/shard_map/ppermute | solution.py:423
  15.4 1.3 %collective-permute-start.3 = (bf16[128,2816]{1,0:T(8,128)(2,1)S(1)}, bf16[128,2816]{1,0:T(8,128)(2,1)}, u32[]{:S(2)}, u32[]{:S(2)}) collective-permute-start(bf16[128,2816]{1,0:T(8,128)(2,1)S(1)} %get-tuple-element.40.refs_0_), channel_id=1, source_target_pairs={{2,0},{4,2},{6,4},{1,3},{3,5},{5,7},{10,8},{12,10},{14,12},{9,11},... | collective-permute-start | bytes 2162696 | tf_op jit(solution)/shard_map/ppermute | solution.py:424
  16.7 1.2 %shard_map.96 = (bf16[2,560,128]{2,1,0:T(8,128)(2,1)S(1)}, bf16[2,560,128]{2,1,0:T(8,128)(2,1)S(1)}) custom-call(bf16[1120,128]{1,0:T(8,128)(2,1)} %bitcast.23, bf16[1120,128]{1,0:T(8,128)(2,1)} %bitcast.24), custom_call_target="tpu_custom_call" | custom-call | bytes 1146880 | tf_op jit(solution)/shard_map/pallas_call | solution.py:63
  17.9 0.1 collective-permute-start.1
  17.9 1.6 %collective-permute-done.1.refs_2_ = bf16[2,560,128]{2,1,0:T(8,128)(2,1)S(1)} collective-permute-done((bf16[2,560,128]{2,1,0:T(8,128)(2,1)S(1)}, bf16[2,560,128]{2,1,0:T(8,128)(2,1)S(1)}, u32[]{:S(2)}, u32[]{:S(2)}) %collective-permute-start.1) | collective-permute-done | bytes 286752 | tf_op jit(solution)/shard_map/ppermute | solution.py:477
  19.5 5.9 %all-to-all-done.refs_0_ = f32[16,40,112]{2,1,0:T(8,128)S(1)} async-done(((f32[16,40,112]{2,1,0:T(8,128)}), f32[16,40,112]{2,1,0:T(8,128)S(1)}, u32[]{:S(2)}, u32[]{:S(2)}) %all-to-all-start) | async-done | bytes 286752 | tf_op jit(solution)/shard_map/all_to_all | solution.py:480
  25.4 1.7 %shard_map.97 = (f32[16,72,112]{2,1,0:T(8,128)}, f32[5,112]{1,0:T(8,128)S(1)}, f32[5,256]{1,0:T(8,128)S(1)}) custom-call(f32[16,40,112]{2,1,0:T(8,128)S(1)} %all-to-all-done.refs_0_, bf16[2,560,128]{2,1,0:T(8,128)(2,1)S(1)} %get-tuple-element.36.refs_1_, bf16[2,560,128]{2,1,0:T(8,128)(2,1)S(1)} %collective-permute-done.1.refs_2_), custom_call_target="tpu_custom_call" | custom-call | flops 64225280 | bytes 1383616 | tf_op jit(solution)/shard_map/pallas_call | solution.py:63
  27.1 3.6 %all-to-all-start.1 = ((f32[16,72,112]{2,1,0:T(8,128)}), f32[16,72,112]{2,1,0:T(8,128)S(1)}, u32[]{:S(2)}, u32[]{:S(2)}) async-start(f32[16,72,112]{2,1,0:T(8,128)} %get-tuple-element.38), calls=%async_computation.1 | async-start | bytes 1179648 | tf_op jit(solution)/shard_map/all_to_all | solution.py:480
  30.7 8.1 %collective-permute-done.2.refs_1_ = bf16[128,2816]{1,0:T(8,128)(2,1)} collective-permute-done((bf16[128,2816]{1,0:T(8,128)(2,1)S(1)}, bf16[128,2816]{1,0:T(8,128)(2,1)}, u32[]{:S(2)}, u32[]{:S(2)}) %collective-permute-start.2) | collective-permute-done | bytes 720928 | tf_op jit(solution)/shard_map/ppermute | solution.py:423
  38.8 2.3 %collective-permute-start.5 = (bf16[128,2816]{1,0:T(8,128)(2,1)}, bf16[128,2816]{1,0:T(8,128)(2,1)}, u32[]{:S(2)}, u32[]{:S(2)}) collective-permute-start(bf16[128,2816]{1,0:T(8,128)(2,1)} %collective-permute-done.2.refs_1_), channel_id=1, source_target_pairs={{0,2},{2,4},{4,6},{3,1},{5,3},{7,5},{8,10},{10,12},{12,14},{11,9},... | collective-permute-start | bytes 2162696 | tf_op jit(solution)/shard_map/ppermute | solution.py:460
  41.1 0.0 collective-permute-done.3.refs_2_
  41.1 3.2 %shard_map.98 = (bf16[128,2816]{1,0:T(8,128)(2,1)}, f32[8,128]{1,0:T(8,128)S(1)}) custom-call(bf16[128,2816]{1,0:T(8,128)(2,1)S(1)} %get-tuple-element.40.refs_0_, bf16[128,2816]{1,0:T(8,128)(2,1)} %collective-permute-done.2.refs_1_, bf16[128,2816]{1,0:T(8,128)(2,1)} %collective-permute-done.3.refs_2_, f32[3,3,2816]{2,1,0:T(4,128)S(1)} %get-tuple-element.42.refs_3_.refs_4_), custom_call_target="tpu_custom_call" | custom-call | flops 500000000 | bytes 2989056 | tf_op jit(solution)/shard_map/pallas_call | solution.py:63
  44.3 0.1 collective-permute-start.6
  44.4 7.2 %all-to-all-done.1.refs_0_ = f32[16,72,112]{2,1,0:T(8,128)S(1)} async-done(((f32[16,72,112]{2,1,0:T(8,128)}), f32[16,72,112]{2,1,0:T(8,128)S(1)}, u32[]{:S(2)}, u32[]{:S(2)}) %all-to-all-start.1) | async-done | bytes 516128 | tf_op jit(solution)/shard_map/all_to_all | solution.py:480
  51.7 1.9 %shard_map.99 = (f32[16,40,112]{2,1,0:T(8,128)}, f32[560,112]{1,0:T(8,128)S(1)}) custom-call(f32[16,72,112]{2,1,0:T(8,128)S(1)} %all-to-all-done.1.refs_0_, bf16[2,560,128]{2,1,0:T(8,128)(2,1)S(1)} %get-tuple-element.36.refs_1_, bf16[2,560,128]{2,1,0:T(8,128)(2,1)S(1)} %collective-permute-done.1.refs_2_, f32[5,256]{1,0:T(8,128)S(1)} %get-tuple-element.39.refs_3_.refs_4_, ...), custom_call_target="tpu_custom_call" | custom-call | flops 64225280 | bytes 1632256 | tf_op jit(solution)/shard_map/pallas_call | solution.py:63
  53.5 4.7 %all-to-all-start.2 = ((f32[16,40,112]{2,1,0:T(8,128)}), f32[16,40,112]{2,1,0:T(8,128)S(1)}, u32[]{:S(2)}, u32[]{:S(2)}) async-start(f32[16,40,112]{2,1,0:T(8,128)} %get-tuple-element.49), calls=%async_computation.2 | async-start | bytes 655360 | tf_op jit(solution)/shard_map/all_to_all | solution.py:480
  58.3 0.4 shard_map.100
  58.7 0.1 collective-permute-start.4
  58.8 0.0 collective-permute-done.5.refs_2_
  58.8 2.5 %collective-permute-done.6.refs_3_ = bf16[128,2816]{1,0:T(8,128)(2,1)} collective-permute-done((bf16[128,2816]{1,0:T(8,128)(2,1)}, bf16[128,2816]{1,0:T(8,128)(2,1)}, u32[]{:S(2)}, u32[]{:S(2)}) %collective-permute-start.6) | collective-permute-done | bytes 720928 | tf_op jit(solution)/shard_map/ppermute | solution.py:462
  61.3 3.4 %shard_map.102 = (bf16[1,1,128,5632]{3,2,1,0:T(8,128)(2,1)}, f32[8,128]{1,0:T(8,128)S(1)}) custom-call(bf16[128,2816]{1,0:T(8,128)(2,1)S(1)} %get-tuple-element.40.refs_0_, bf16[128,2816]{1,0:T(8,128)(2,1)} %collective-permute-done.2.refs_1_, bf16[128,2816]{1,0:T(8,128)(2,1)} %collective-permute-done.5.refs_2_, ...), custom_call_target="tpu_custom_call" | custom-call | flops 10000000000 | bytes 4430848 | tf_op jit(solution)/shard_map/pallas_call | solution.py:63
  64.7 0.0 collective-permute-done.4.refs_1_
  64.7 0.7 %shard_map.101 = (bf16[1120,128]{1,0:T(8,128)(2,1)}, f32[8,128]{1,0:T(8,128)S(1)}) custom-call(bf16[560,128]{1,0:T(8,128)(2,1)S(1)} %get-tuple-element.46.refs_0_, bf16[560,128]{1,0:T(8,128)(2,1)S(1)} %collective-permute-done.4.refs_1_), custom_call_target="tpu_custom_call" | custom-call | bytes 577536 | tf_op jit(solution)/shard_map/pallas_call | solution.py:63
  65.5 4.0 %all-to-all-done.2.refs_0_ = f32[16,40,112]{2,1,0:T(8,128)S(1)} async-done(((f32[16,40,112]{2,1,0:T(8,128)}), f32[16,40,112]{2,1,0:T(8,128)S(1)}, u32[]{:S(2)}, u32[]{:S(2)}) %all-to-all-start.2) | async-done | bytes 286752 | tf_op jit(solution)/shard_map/all_to_all | solution.py:480
  69.4 0.5 shard_map.103
  69.9 0.1 collective-permute-start.7
  70.0 0.7 %shard_map.104 = (bf16[1120,128]{1,0:T(8,128)(2,1)}, bf16[1120,128]{1,0:T(8,128)(2,1)}) custom-call(bf16[2,560,128]{2,1,0:T(8,128)(2,1)S(1)} %get-tuple-element.54.refs_0_), custom_call_target="tpu_custom_call" | custom-call | bytes 860160 | tf_op jit(solution)/shard_map/pallas_call | solution.py:63
  70.8 0.8 %collective-permute-done.7.refs_0_ = bf16[2,560,128]{2,1,0:T(8,128)(2,1)S(1)} collective-permute-done((bf16[2,560,128]{2,1,0:T(8,128)(2,1)S(1)}, bf16[2,560,128]{2,1,0:T(8,128)(2,1)S(1)}, u32[]{:S(2)}, u32[]{:S(2)}) %collective-permute-start.7) | collective-permute-done | bytes 286752 | tf_op jit(solution)/shard_map/ppermute | solution.py:534
  71.6 0.7 shard_map.105
Async XLA Ops:
  1.8 1.9 %collective-permute-start = (bf16[2,560,128]{2,1,0:T(8,128)(2,1)S(1)}, bf16[2,560,128]{2,1,0:T(8,128)(2,1)S(1)}, u32[]{:S(2)}, u32[]{:S(2)}) collective-permute-start(bf16[2,560,128]{2,1,0:T(8,128)(2,1)S(1)} %get-tuple-element.33), channel_id=1, source_target_pairs={{0,8},{8,0},{1,9},{9,1},{2,10},{10,2},{3,11},{11,3},{4,12},{12,4},... | collective-permute-start | bytes 860168 | tf_op jit(solution)/shard_map/ppermute | solution.py:475
  5.4 20.0 %all-to-all-start = ((f32[16,40,112]{2,1,0:T(8,128)}), f32[16,40,112]{2,1,0:T(8,128)S(1)}, u32[]{:S(2)}, u32[]{:S(2)}) async-start(f32[16,40,112]{2,1,0:T(8,128)} %get-tuple-element.35), calls=%async_computation | async-start | bytes 655360 | tf_op jit(solution)/shard_map/all_to_all | solution.py:480
  13.5 25.4 %collective-permute-start.2 = (bf16[128,2816]{1,0:T(8,128)(2,1)S(1)}, bf16[128,2816]{1,0:T(8,128)(2,1)}, u32[]{:S(2)}, u32[]{:S(2)}) collective-permute-start(bf16[128,2816]{1,0:T(8,128)(2,1)S(1)} %get-tuple-element.41), channel_id=1, source_target_pairs={{0,1},{1,0},{2,3},{3,2},{4,5},{5,4},{6,7},{7,6},{8,9},{9,8},{10,11... | collective-permute-start | bytes 2162696 | tf_op jit(solution)/shard_map/ppermute | solution.py:423
  15.4 25.7 %collective-permute-start.3 = (bf16[128,2816]{1,0:T(8,128)(2,1)S(1)}, bf16[128,2816]{1,0:T(8,128)(2,1)}, u32[]{:S(2)}, u32[]{:S(2)}) collective-permute-start(bf16[128,2816]{1,0:T(8,128)(2,1)S(1)} %get-tuple-element.40.refs_0_), channel_id=1, source_target_pairs={{2,0},{4,2},{6,4},{1,3},{3,5},{5,7},{10,8},{12,10},{14,12},{9,11},... | collective-permute-start | bytes 2162696 | tf_op jit(solution)/shard_map/ppermute | solution.py:424
  17.9 1.6 %collective-permute-start.1 = (bf16[2,560,128]{2,1,0:T(8,128)(2,1)S(1)}, bf16[2,560,128]{2,1,0:T(8,128)(2,1)S(1)}, u32[]{:S(2)}, u32[]{:S(2)}) collective-permute-start(bf16[2,560,128]{2,1,0:T(8,128)(2,1)S(1)} %get-tuple-element.37), channel_id=1, source_target_pairs={{0,8},{8,0},{1,9},{9,1},{2,10},{10,2},{3,11},{11,3},{4,12},{12,4},... | collective-permute-start | bytes 860168 | tf_op jit(solution)/shard_map/ppermute | solution.py:477
  27.1 24.6 %all-to-all-start.1 = ((f32[16,72,112]{2,1,0:T(8,128)}), f32[16,72,112]{2,1,0:T(8,128)S(1)}, u32[]{:S(2)}, u32[]{:S(2)}) async-start(f32[16,72,112]{2,1,0:T(8,128)} %get-tuple-element.38), calls=%async_computation.1 | async-start | bytes 1179648 | tf_op jit(solution)/shard_map/all_to_all | solution.py:480
  38.8 19.9 %collective-permute-start.5 = (bf16[128,2816]{1,0:T(8,128)(2,1)}, bf16[128,2816]{1,0:T(8,128)(2,1)}, u32[]{:S(2)}, u32[]{:S(2)}) collective-permute-start(bf16[128,2816]{1,0:T(8,128)(2,1)} %collective-permute-done.2.refs_1_), channel_id=1, source_target_pairs={{0,2},{2,4},{4,6},{3,1},{5,3},{7,5},{8,10},{10,12},{12,14},{11,9},... | collective-permute-start | bytes 2162696 | tf_op jit(solution)/shard_map/ppermute | solution.py:460
  44.3 17.0 %collective-permute-start.6 = (bf16[128,2816]{1,0:T(8,128)(2,1)}, bf16[128,2816]{1,0:T(8,128)(2,1)}, u32[]{:S(2)}, u32[]{:S(2)}) collective-permute-start(bf16[128,2816]{1,0:T(8,128)(2,1)} %get-tuple-element.51), channel_id=1, source_target_pairs={{0,1},{1,0},{2,3},{3,2},{4,5},{5,4},{6,7},{7,6},{8,9},{9,8},{10,11... | collective-permute-start | bytes 2162696 | tf_op jit(solution)/shard_map/ppermute | solution.py:462
  53.5 15.9 %all-to-all-start.2 = ((f32[16,40,112]{2,1,0:T(8,128)}), f32[16,40,112]{2,1,0:T(8,128)S(1)}, u32[]{:S(2)}, u32[]{:S(2)}) async-start(f32[16,40,112]{2,1,0:T(8,128)} %get-tuple-element.49), calls=%async_computation.2 | async-start | bytes 655360 | tf_op jit(solution)/shard_map/all_to_all | solution.py:480
  58.7 6.0 %collective-permute-start.4 = (bf16[560,128]{1,0:T(8,128)(2,1)S(1)}, bf16[560,128]{1,0:T(8,128)(2,1)S(1)}, u32[]{:S(2)}, u32[]{:S(2)}) collective-permute-start(bf16[560,128]{1,0:T(8,128)(2,1)S(1)} %get-tuple-element.47), channel_id=1, source_target_pairs={{0,8},{8,0},{1,9},{9,1},{2,10},{10,2},{3,11},{11,3},{4,12},{12,4},... | collective-permute-start | bytes 430088 | tf_op jit(solution)/shard_map/ppermute | solution.py:522
  69.9 1.6 %collective-permute-start.7 = (bf16[2,560,128]{2,1,0:T(8,128)(2,1)S(1)}, bf16[2,560,128]{2,1,0:T(8,128)(2,1)S(1)}, u32[]{:S(2)}, u32[]{:S(2)}) collective-permute-start(bf16[2,560,128]{2,1,0:T(8,128)(2,1)S(1)} %get-tuple-element.53), channel_id=1, source_target_pairs={{0,8},{8,0},{1,9},{9,1},{2,10},{10,2},{3,11},{11,3},{4,12},{12,4},... | collective-permute-start | bytes 860168 | tf_op jit(solution)/shard_map/ppermute | solution.py:534
